TPU v7x, 32 devices: a whole 2x2x4 slice. The times are simulated.
32 devices in a mesh: gx: 4 (over y, x), gy: 8 (over z, core).
Axes of the slice: x: 2, y: 2, z: 4, core: 2. Of those that a mesh axis runs over, the one named last changes fastest.
Arguments:
- patches: bfloat16 [512, 6144], P('gy', 'gx'), may hold values from -2000 to 2000
- norm_gain: float32 [6144], P('gx'), may hold values from 0.5 to 1.5
- w_up: bfloat16 [6144, 24576], P('gx', 'gy'), may hold values from -0.078125 to 0.078125
- bias_up: float32 [24576], P('gy'), may hold values from -4 to 4
- w_down: bfloat16 [24576, 6144], P('gy', 'gx'), may hold values from -0.0390625 to 0.0390625
- bias_down: float32 [6144], P('gx'), may hold values from -4 to 4
- cotangent: bfloat16 [512, 6144], P('gy', 'gx'), may hold values from -4 to 4
Outputs:
- mlp_out: bfloat16 [512, 6144], P('gy', 'gx')
- grad_patches: bfloat16 [512, 6144], P('gy', 'gx')
- grad_gain: float32 [6144], P('gx')
- grad_w_up: float32 [6144, 24576], P('gx', 'gy')
- grad_bias_up: float32 [24576], P('gy')
- grad_w_down: float32 [24576, 6144], P('gy', 'gx')
- grad_bias_down: float32 [6144], P('gx')
All inputs are finite; a program needn't handle non-finite values.
Results may differ from a plain program's by a relative error of at most 0.007.
Values may be sent and summed in bfloat16 or wider, within the bound.
No kernel may reach another device: no remote copies, remote signals or barrier semaphores. Data moves between devices by JAX's collectives and lax.ppermute only.
A program may use at most 128 MiB of HBM per device.

v0:
```python
import jax
import jax.numpy as jnp
from jax import lax
from jax.sharding import PartitionSpec as P

D = 6144


epsilon = 1e-06
inv_root_two = 0.7071067811865476
inv_root_two_pi = 0.3989422804014327


def gelu_value(hidden):
    return 0.5 * hidden * (1.0 + lax.erf(hidden * inv_root_two))


def gelu_slope(hidden):
    return (
        0.5 * (1.0 + lax.erf(hidden * inv_root_two))
        + hidden * jnp.exp(-0.5 * hidden * hidden) * inv_root_two_pi
    )


def over_rows(left, right):
    return lax.dot_general(
        left, right, (((0,), (0,)), ((), ())), preferred_element_type=jnp.float32
    )


def over_cols(left, right):
    return lax.dot_general(
        left, right, (((1,), (1,)), ((), ())), preferred_element_type=jnp.float32
    )


def shards(patches, norm_gain, w_up, bias_up, w_down, bias_down, cotangent):
    values = patches.astype(jnp.float32)
    row_total, row_squares = lax.psum(
        (jnp.sum(values, axis=1), jnp.sum(values * values, axis=1)), "gx"
    )
    row_mean = (row_total / D)[:, None]
    variance = (row_squares / D)[:, None] - row_mean * row_mean
    inv_std = lax.rsqrt(variance + epsilon)
    standard = (values - row_mean) * inv_std
    normed = (standard * norm_gain).astype(jnp.bfloat16)
    partial_value = jnp.dot(
        lax.all_gather(normed, "gy", axis=0, tiled=True), w_up, preferred_element_type=jnp.float32
    )
    hidden = lax.psum(partial_value, "gx") + bias_up
    act_whole = gelu_value(hidden).astype(jnp.bfloat16)
    block = act_whole
    mlp_out = (
        lax.psum_scatter(
            jnp.dot(block, w_down, preferred_element_type=jnp.float32),
            "gy",
            scatter_dimension=0,
            tiled=True,
        )
        + bias_down
    ).astype(jnp.bfloat16)
    piece = lax.all_gather(cotangent, "gy", axis=0, tiled=True)
    weight_total = over_rows(act_whole, piece)
    act_grads = over_cols(piece, w_down)
    grad_act = lax.psum(act_grads, "gx")
    grad_whole = (grad_act * gelu_slope(hidden)).astype(jnp.bfloat16)
    grad_bias_up = jnp.sum(grad_whole, axis=0, dtype=jnp.float32)
    grad_w_up = over_rows(lax.all_gather(normed, "gy", axis=0, tiled=True), grad_whole)
    block = grad_whole
    grad_normed = lax.psum_scatter(over_cols(block, w_up), "gy", scatter_dimension=0, tiled=True)
    grad_gain, grad_bias_down = lax.psum(
        (jnp.sum(grad_normed * standard, axis=0), jnp.sum(cotangent, axis=0, dtype=jnp.float32)),
        "gy",
    )
    scaled = grad_normed * norm_gain
    first_total, second_total = lax.psum(
        (jnp.sum(scaled, axis=1), jnp.sum(scaled * standard, axis=1)), "gx"
    )
    first_mean = (first_total / D)[:, None]
    second_mean = (second_total / D)[:, None]
    grad_patches = (inv_std * (scaled - first_mean - standard * second_mean)).astype(jnp.bfloat16)
    return (mlp_out, grad_patches, grad_gain, grad_w_up, grad_bias_up, weight_total, grad_bias_down)


def solution(mesh):
    in_specs = (
        P("gy", "gx"),
        P("gx"),
        P("gx", "gy"),
        P("gy"),
        P("gy", "gx"),
        P("gx"),
        P("gy", "gx"),
    )
    out_specs = (
        P("gy", "gx"),
        P("gy", "gx"),
        P("gx"),
        P("gx", "gy"),
        P("gy"),
        P("gy", "gx"),
        P("gx"),
    )
    return jax.shard_map(shards, mesh=mesh, in_specs=in_specs, out_specs=out_specs, check_vma=False)
```

profile of v0, /device:TPU:0, one launch (start us, length us, event | category | flops | bytes accessed | tf_op | source)
XLA Modules:
  0.0 431.4 jit_solution(6825433028517386059)
XLA Ops:
  7.2 0.0 all-gather.3.cloned.1.call-start
  7.2 1.1 convert_reduce_fusion.1
  8.3 11.4 %all-reduce.2 = (f32[64]{0:T(128)S(1)}, f32[64]{0:T(128)S(1)}) all-reduce(f32[64]{0:T(128)S(1)} %get-tuple-element.11, f32[64]{0:T(128)S(1)} %get-tuple-element.10), channel_id=1, replica_groups=mesh['gx'=4,'gy'=8] {'gx'}, use_global_device_ids=true, to_apply=%region_3.0 | all-reduce | flops 128 | bytes 1024 | tf_op jit(solution)/shard_map/psum | solution.py:39
  19.7 1.7 fusion.11
  21.4 0.0 all-gather.3.cloned.1.call-update
  21.4 0.0 all-gather.5.cloned.1.call-start
  21.5 0.7 all-gather.5.cloned.1.call-update
  22.2 0.0 all-reduce.6.cloned.1.call-start
  22.2 23.8 %all-gather.3.cloned.1.call-done = bf16[512,1536]{1,0:T(8,128)(2,1)} async-done(((bf16[64,1536]{1,0:T(8,128)(2,1)}), bf16[512,1536]{1,0:T(8,128)(2,1)}) %all-gather.3.cloned.1.call-update) | async-done | bytes 1572880 | tf_op jit(solution)/shard_map/all_gather | solution.py:48
  46.0 9.7 %fusion.19 = f32[512,3072]{1,0:T(8,128)} fusion(bf16[512,1536]{1,0:T(8,128)(2,1)} %all-gather.3.cloned.1.call-done, bf16[1536,3072]{1,0:T(8,128)(2,1)} %param.9), kind=kOutput, calls=%fused_computation.32 | convolution fusion | flops 4831838208 | bytes 17301504 | tf_op jit(solution)/shard_map/dot_general | solution.py:47
  55.7 16.6 %all-gather.5.cloned.1.call-done = bf16[512,1536]{1,0:T(8,128)(2,1)} async-done(((bf16[64,1536]{1,0:T(8,128)(2,1)}), bf16[512,1536]{1,0:T(8,128)(2,1)}) %all-gather.5.cloned.1.call-update) | async-done | bytes 1572880 | tf_op jit(solution)/shard_map/all_gather | solution.py:62
  72.3 9.8 %fusion.21 = f32[512,3072]{1,0:T(8,128)} fusion(bf16[512,1536]{1,0:T(8,128)(2,1)} %all-gather.5.cloned.1.call-done, bf16[3072,1536]{1,0:T(8,128)(2,1)} %param.11), kind=kOutput, calls=%fused_computation.34 | convolution fusion | flops 4831838208 | bytes 17301504 | tf_op jit(solution)/shard_map/dot_general | solution.py:32
  82.1 0.0 copy-start.4
  82.1 0.0 all-reduce.6.cloned.1.call-update
  82.1 0.0 reduce-scatter.5.cloned.1.call-start
  82.1 239.9 %all-reduce.6.cloned.1.call-done = (f32[512,3072]{1,0:T(8,128)}, f32[512,3072]{1,0:T(8,128)}) async-done(((f32[512,3072]{1,0:T(8,128)}, f32[512,3072]{1,0:T(8,128)}), (f32[512,3072]{1,0:T(8,128)}, f32[512,3072]{1,0:T(8,128)})) %all-reduce.6.cloned.1.call-update) | async-done | bytes 12582928 | tf_op jit(solution)/shard_map/psum | solution.py:50
  322.0 0.0 copy-done.4
  322.0 7.5 %convert_reduce_fusion = (f32[3072]{0:T(1024)}, bf16[512,3072]{1,0:T(8,128)(2,1)S(1)}, bf16[512,3072]{1,0:T(8,128)(2,1)S(1)}) fusion(f32[512,3072]{1,0:T(8,128)} %get-tuple-element.19, f32[512,3072]{1,0:T(8,128)} %get-tuple-element.18, f32[3072]{0:T(1024)S(1)} %copy-done.4), kind=kLoop, calls=%fused_computation.7 | loop fusion | flops 25162752 | bytes 18898944 | tf_op jit(solution)/shard_map/reduce_sum | solution.py:67
  329.5 0.0 copy-start
  329.5 1.7 copy-done
  331.2 9.3 %fusion.22 = f32[512,1536]{1,0:T(8,128)} fusion(bf16[512,3072]{1,0:T(8,128)(2,1)S(1)} %get-tuple-element.21, bf16[1536,3072]{1,0:T(8,128)(2,1)} %param.9), kind=kOutput, calls=%fused_computation.35 | convolution fusion | flops 4831838208 | bytes 15728640 | tf_op jit(solution)/shard_map/dot_general | solution.py:32
  340.5 0.0 reduce-scatter.5.cloned.1.call-update
  340.5 0.2 reduce-scatter.3.cloned.1.call-start
  340.7 0.0 copy-start.2
  340.8 9.3 %fusion.20 = f32[512,1536]{1,0:T(8,128)} fusion(bf16[512,3072]{1,0:T(8,128)(2,1)S(1)} %get-tuple-element.22, bf16[3072,1536]{1,0:T(8,128)(2,1)} %param.11), kind=kOutput, calls=%fused_computation.33 | convolution fusion | flops 4831838208 | bytes 15728640 | tf_op jit(solution)/shard_map/dot_general | solution.py:55
  350.0 0.0 reduce-scatter.3.cloned.1.call-update
  350.0 0.0 copy-done.2
  350.1 0.0 copy-start.6
  350.1 11.5 %fusion.23 = f32[1536,3072]{1,0:T(8,128)} fusion(bf16[512,1536]{1,0:T(8,128)(2,1)} %all-gather.3.cloned.1.call-done, bf16[512,3072]{1,0:T(8,128)(2,1)} %copy-done), kind=kOutput, calls=%fused_computation.36 | convolution fusion | flops 4831838208 | bytes 23592960 | tf_op jit(solution)/shard_map/dot_general | solution.py:26
  361.6 0.0 copy-done.6
  361.6 0.0 copy-start.1
  361.6 0.0 copy-start.3
  361.6 0.0 copy-start.5
  361.6 9.5 %fusion.24 = f32[3072,1536]{1,0:T(8,128)} fusion(bf16[512,3072]{1,0:T(8,128)(2,1)S(1)} %get-tuple-element.22, bf16[512,1536]{1,0:T(8,128)(2,1)S(1)} %copy-done.6), kind=kOutput, calls=%fused_computation.37 | convolution fusion | flops 4831838208 | bytes 23592960 | tf_op jit(solution)/shard_map/dot_general | solution.py:26
  371.2 9.8 %reduce-scatter.5.cloned.1.call-done = f32[64,1536]{1,0:T(8,128)} async-done(((f32[512,1536]{1,0:T(8,128)}), f32[64,1536]{1,0:T(8,128)}) %reduce-scatter.5.cloned.1.call-update) | async-done | bytes 393232 | tf_op jit(solution)/shard_map/reduce_scatter | solution.py:70
  381.0 0.0 copy-done.1
  381.0 0.0 copy-done.3
  381.0 1.3 fusion.16
  382.3 9.9 %all-reduce.1 = (f32[64]{0:T(128)S(1)}, f32[64]{0:T(128)S(1)}) all-reduce(f32[64]{0:T(128)S(1)} %get-tuple-element.8, f32[64]{0:T(128)S(1)} %get-tuple-element.9), channel_id=1, replica_groups=mesh['gx'=4,'gy'=8] {'gx'}, use_global_device_ids=true, to_apply=%region_11.0 | all-reduce | flops 128 | bytes 1024 | tf_op jit(solution)/shard_map/psum | solution.py:76
  392.1 27.6 %all-reduce = (f32[1536]{0:T(1024)}, f32[1536]{0:T(1024)}) all-reduce(f32[1536]{0:T(1024)S(1)} %get-tuple-element.7, f32[1536]{0:T(1024)S(1)} %convert_reduce_fusion.2), channel_id=1, replica_groups=mesh['gx'=4,'gy'=8] {'gy'}, use_global_device_ids=true, to_apply=%region_13.0 | all-reduce | flops 3072 | bytes 24576 | tf_op jit(solution)/shard_map/psum | solution.py:71
  419.7 1.9 fusion.15
  421.6 1.6 reduce-scatter.3.cloned.1.call-done
  423.2 0.0 copy-done.5
  423.2 1.7 add_convert_fusion
  (3 shorter events, 0.1 us)
Async XLA Ops:
  7.2 38.9 %all-gather.3.cloned.1.call-start = ((), (), s32[]{:S(2)}) async-start(), calls=%async_computation.2 | async-start | bytes 1769472 | tf_op jit(solution)/shard_map/all_gather | solution.py:48
  21.4 50.9 %all-gather.5.cloned.1.call-start = ((), (), s32[]{:S(2)}) async-start(), calls=%async_computation.4 | async-start | bytes 1769472 | tf_op jit(solution)/shard_map/all_gather | solution.py:62
  22.2 299.8 %all-reduce.6.cloned.1.call-start = ((), (), s32[]{:S(2)}) async-start(), calls=%async_computation.6 | async-start | bytes 25165824 | tf_op jit(solution)/shard_map/psum | solution.py:50
  82.1 239.9 %copy-start.4 = (f32[3072]{0:T(1024)S(1)}, f32[3072]{0:T(1024)}, u32[]{:S(2)}) copy-start(f32[3072]{0:T(1024)} %param.10) | copy-start | bytes 36868
  82.1 298.9 %reduce-scatter.5.cloned.1.call-start = ((), (), s32[]{:S(2)}) async-start(), calls=%async_computation.5 | async-start | bytes 3538944 | tf_op jit(solution)/shard_map/reduce_scatter | solution.py:70
  329.5 1.7 copy-start
  340.5 82.7 %reduce-scatter.3.cloned.1.call-start = ((), (), s32[]{:S(2)}) async-start(), calls=%async_computation.3 | async-start | bytes 3538944 | tf_op jit(solution)/shard_map/reduce_scatter | solution.py:54
  340.7 9.3 %copy-start.2 = (bf16[64,1536]{1,0:T(8,128)(2,1)S(1)}, bf16[64,1536]{1,0:T(8,128)(2,1)}, u32[]{:S(2)}) copy-start(bf16[64,1536]{1,0:T(8,128)(2,1)} %param.13) | copy-start | bytes 589828
  350.1 11.5 %copy-start.6 = (bf16[512,1536]{1,0:T(8,128)(2,1)S(1)}, bf16[512,1536]{1,0:T(8,128)(2,1)}, u32[]{:S(2)}) copy-start(bf16[512,1536]{1,0:T(8,128)(2,1)} %all-gather.5.cloned.1.call-done) | copy-start | bytes 4718596
  361.6 19.4 %copy-start.1 = (bf16[64,1536]{1,0:T(8,128)(2,1)S(1)}, bf16[64,1536]{1,0:T(8,128)(2,1)}, u32[]{:S(2)}) copy-start(bf16[64,1536]{1,0:T(8,128)(2,1)} %param.7) | copy-start | bytes 589828
  361.6 19.4 %copy-start.3 = (f32[1536]{0:T(1024)S(1)}, f32[1536]{0:T(1024)}, u32[]{:S(2)}) copy-start(f32[1536]{0:T(1024)} %param.8) | copy-start | bytes 18436
  361.6 61.6 %copy-start.5 = (f32[1536]{0:T(1024)S(1)}, f32[1536]{0:T(1024)}, u32[]{:S(2)}) copy-start(f32[1536]{0:T(1024)} %param.12) | copy-start | bytes 18436
Sparse Core Ops, SparseCore 0:
  21.6 24.4 all-gather.2
  47.7 24.5 all-gather.4
  82.2 239.7 all-reduce.5
  340.6 40.3 reduce-scatter.4
  383.2 40.0 reduce-scatter.2
where the time goes:
time: 432 us; the launch traced here: 431 us
  waiting for transfers between devices  292 us (68%)
  matrix products  59.1 us (14%)
  blocking collectives  48.8 us (11%)
  other arithmetic  15.2 us (4%)
  between operations  13.8 us (3%)
    psum x1, waiting for transfers between devices, shards(): hidden = lax.psum(partial_value, 'gx') + bias_up  240 us
    psum x1, blocking collectives, shards(): lax.psum((jnp.sum(grad_normed * standard, axis=0), jnp.sum(cotangent, axi...  27.6 us
    all_gather x1, waiting for transfers between devices, shards(): lax.all_gather(normed, 'gy', axis=0, tiled=True)  23.8 us
    dot_general x2, matrix products, over_rows(): lax.dot_general(left, right, (((0,), (0,)), ((), ())), preferred_element_...  21 us
    dot_general x2, matrix products, over_cols(): lax.dot_general(left, right, (((1,), (1,)), ((), ())), preferred_element_...  19.1 us
    all_gather x1, waiting for transfers between devices, shards(): piece = lax.all_gather(cotangent, 'gy', axis=0, tiled=True)  16.6 us
    psum x1, blocking collectives, shards(): lax.psum((jnp.sum(values, axis=1), jnp.sum(values * values, axis=1)), 'gx')  11.4 us
    psum x1, blocking collectives, shards(): lax.psum((jnp.sum(scaled, axis=1), jnp.sum(scaled * standard, axis=1)), '...  9.85 us
  transfers between devices with their start and end apart: 5, of which 5 were waited for; matrix products, arithmetic and copies ran while one was open for 10% of the time, Pallas kernels for 0%

commit v1 on v0

v1 whole, which is shorter than its diff:
```python
import jax
import jax.numpy as jnp
from jax import lax
from jax.experimental import pallas as pl
from jax.experimental.pallas import tpu as pltpu
from jax.sharding import PartitionSpec as P

D = 6144

epsilon = 1e-06
inv_root_two = 0.7071067811865476
inv_root_two_pi = 0.3989422804014327

bf16 = jnp.bfloat16
f32 = jnp.float32
VMEM_LIMIT = 40 * 1024 * 1024

NN = (((1,), (0,)), ((), ()))
NT = (((1,), (1,)), ((), ()))
TN = (((0,), (0,)), ((), ()))


def mm(left, right, dims):
    return lax.dot_general(left, right, dims, preferred_element_type=f32)


def cost(m, k, n, moved):
    return pl.CostEstimate(flops=2 * m * k * n, bytes_accessed=moved, transcendentals=0)


def params():
    return pltpu.CompilerParams(vmem_limit_bytes=VMEM_LIMIT)


def block_of(width, most=384):
    return most if width % most == 0 else width


def bits(n):
    return [1 << b for b in range(n.bit_length() - 1)]


def partial_product(x, w, me, shard, rels, dtype, by_rows):
    rows, depth = x.shape
    nb = block_of(shard)
    per = shard // nb
    steps = per * len(rels)
    index = jnp.concatenate([(me ^ r) * per + jnp.arange(per, dtype=jnp.int32) for r in rels])

    def kernel(index_ref, x_ref, w_ref, o_ref):
        o_ref[...] = mm(x_ref[...], w_ref[...], NT if by_rows else NN).astype(dtype)

    if by_rows:
        w_spec = pl.BlockSpec((nb, depth), lambda j, at: (at[j], 0))
    else:
        w_spec = pl.BlockSpec((depth, nb), lambda j, at: (0, at[j]))
    n = steps * nb
    return pl.pallas_call(
        kernel,
        grid_spec=pltpu.PrefetchScalarGridSpec(
            num_scalar_prefetch=1,
            grid=(steps,),
            in_specs=[pl.BlockSpec((rows, depth), lambda j, at: (0, 0)), w_spec],
            out_specs=pl.BlockSpec((rows, nb), lambda j, at: (0, j)),
        ),
        out_shape=jax.ShapeDtypeStruct((rows, n), dtype),
        compiler_params=params(),
        cost_estimate=cost(rows, depth, n, 2 * rows * depth + 2 * depth * n + 4 * rows * n),
    )(index, x, w)


def summed_product(near, far, w, me, by_rows):
    rows, wide = near.shape
    shard = wide // 2
    out = w.shape[1] if by_rows else w.shape[0]
    nb = 256
    half = rows // 2

    def kernel(me_ref, near_ref, far_ref, w0, w2, w1, w3, keep_ref, go_ref):
        dims = NN if by_rows else NT
        total = mm(near_ref[:, :shard], w0[...], dims)
        total += mm(near_ref[:, shard:], w2[...], dims)
        total += mm(far_ref[:, :shard], w1[...], dims)
        total += mm(far_ref[:, shard:], w3[...], dims)
        keep_ref[...] = total[:half]
        go_ref[...] = total[half:].astype(bf16)

    def w_spec(r):
        if by_rows:
            return pl.BlockSpec((shard, nb), lambda j, at: (at[0] ^ r, j))
        return pl.BlockSpec((nb, shard), lambda j, at: (j, at[0] ^ r))

    whole = pl.BlockSpec((rows, wide), lambda j, at: (0, 0))
    return pl.pallas_call(
        kernel,
        grid_spec=pltpu.PrefetchScalarGridSpec(
            num_scalar_prefetch=1,
            grid=(out // nb,),
            in_specs=[whole, whole, w_spec(0), w_spec(2), w_spec(1), w_spec(3)],
            out_specs=[pl.BlockSpec((half, nb), lambda j, at: (0, j))] * 2,
        ),
        out_shape=(jax.ShapeDtypeStruct((half, out), f32), jax.ShapeDtypeStruct((half, out), bf16)),
        compiler_params=params(),
        cost_estimate=cost(rows, 2 * wide, out, 4 * rows * wide + 4 * wide * out + 3 * rows * out),
    )(me.reshape(1), near, far, w, w, w, w)


def weight_grad_down(pieces, cots, me, rels, shard, units, so_far):
    nb = block_of(shard)
    per = shard // nb
    out = cots[0].shape[1]
    tokens = sum(c.shape[0] for c in cots)
    index = jnp.concatenate([(me ^ r) * per + jnp.arange(per, dtype=jnp.int32) for r in rels])

    def kernel(index_ref, p0, p1, c0, c1, *refs):
        refs[-1][...] = mm(p0[...], c0[...], TN) + mm(p1[...], c1[...], TN)

    in_specs = [pl.BlockSpec((p.shape[0], nb), lambda j, at: (0, j)) for p in pieces]
    in_specs += [pl.BlockSpec(c.shape, lambda j, at: (0, 0)) for c in cots]
    rest = ()
    if so_far is not None:
        in_specs.append(pl.BlockSpec(memory_space=pl.ANY))
        rest = (so_far,)
    return pl.pallas_call(
        kernel,
        grid_spec=pltpu.PrefetchScalarGridSpec(
            num_scalar_prefetch=1,
            grid=(per * len(rels),),
            in_specs=in_specs,
            out_specs=pl.BlockSpec((nb, out), lambda j, at: (at[j], 0)),
        ),
        out_shape=jax.ShapeDtypeStruct((units, out), f32),
        input_output_aliases={5: 0} if rest else {},
        compiler_params=params(),
        cost_estimate=cost(shard * len(rels), tokens, out, 4 * shard * len(rels) * out),
    )(index, *pieces, *cots, *rest)


def weight_grad_up(normeds, pieces, me, rels, shard, units, so_far):
    nb = block_of(shard)
    per = shard // nb
    out = normeds[0].shape[1]
    tokens = sum(c.shape[0] for c in normeds)
    index = jnp.concatenate([(me ^ r) * per + jnp.arange(per, dtype=jnp.int32) for r in rels])

    def kernel(index_ref, n0, n1, p0, p1, *refs):
        refs[-2][...] = mm(n0[...], p0[...], TN) + mm(n1[...], p1[...], TN)
        refs[-1][...] = jnp.sum(p0[...].astype(f32), axis=0, keepdims=True) + jnp.sum(
            p1[...].astype(f32), axis=0, keepdims=True
        )

    in_specs = [pl.BlockSpec(c.shape, lambda j, at: (0, 0)) for c in normeds]
    in_specs += [pl.BlockSpec((p.shape[0], nb), lambda j, at: (0, j)) for p in pieces]
    rest = ()
    if so_far is not None:
        in_specs += [pl.BlockSpec(memory_space=pl.ANY)] * 2
        rest = so_far
    return pl.pallas_call(
        kernel,
        grid_spec=pltpu.PrefetchScalarGridSpec(
            num_scalar_prefetch=1,
            grid=(per * len(rels),),
            in_specs=in_specs,
            out_specs=[
                pl.BlockSpec((out, nb), lambda j, at: (0, at[j])),
                pl.BlockSpec((1, nb), lambda j, at: (0, at[j])),
            ],
        ),
        out_shape=(jax.ShapeDtypeStruct((out, units), f32), jax.ShapeDtypeStruct((1, units), f32)),
        input_output_aliases={5: 0, 6: 1} if rest else {},
        compiler_params=params(),
        cost_estimate=cost(shard * len(rels), tokens, out, 4 * shard * len(rels) * out),
    )(index, *normeds, *pieces, *rest)


def solution(mesh):
    n_gx, n_gy = mesh.shape["gx"], mesh.shape["gy"]
    both = ("gx", "gy")

    def across(first):
        pairs = []
        for gx in range(n_gx):
            for gy in range(n_gy):
                flip = 1 if (gy % 2 == 0) == first else 2
                pairs.append((gx * n_gy + gy, (gx ^ flip) * n_gy + gy))
        return pairs

    first_pairs, second_pairs = across(True), across(False)

    def to_first(x):
        return lax.ppermute(x, both, first_pairs)

    def to_second(x):
        return lax.ppermute(x, both, second_pairs)

    def along_gy(x, m):
        return lax.ppermute(x, "gy", [(i, i ^ m) for i in range(n_gy)])

    def along_gx(x, m):
        return lax.ppermute(x, "gx", [(i, i ^ m) for i in range(n_gx)])

    def plane_sum(x):
        for step in bits(n_gx):
            x = x + along_gx(x, step)
        return x

    def gather_rows(own):
        near = jnp.concatenate([own, along_gy(own, 1)])
        even = jnp.concatenate([along_gy(own, 2 * k) for k in range(1, n_gy // 2)])
        return near, jnp.concatenate([even, along_gy(even, 1)])

    def scatter_plane(x, w, me, shard, by_rows):
        go = to_first(partial_product(x, w, me, shard, (2, 3), bf16, by_rows))
        keep = partial_product(x, w, me, shard, (0, 1), f32, by_rows)
        back = to_second((keep[:, shard:] + go[:, shard:].astype(f32)).astype(bf16))
        total = keep[:, :shard] + go[:, :shard].astype(f32) + back.astype(f32)
        for step in bits(n_gx)[2:]:
            total = total + along_gx(total, step)
        return total

    def gather_plane(x):
        near = jnp.concatenate([x, to_first(x)], axis=1)
        return near, to_second(near)

    def shards(patches, norm_gain, w_up, bias_up, w_down, bias_down, cotangent):
        rows = patches.shape[0]
        units = w_up.shape[1]
        shard = units // 4
        gx, gy = lax.axis_index("gx") % 4, lax.axis_index("gy")
        me = jnp.where(gy % 2 == 0, 2 * (gx % 2) + gx // 2, gx).astype(jnp.int32)

        cot = gather_rows(cotangent)
        values = patches.astype(f32)
        totals = plane_sum(jnp.stack([jnp.sum(values, axis=1), jnp.sum(values * values, axis=1)]))
        row_mean = (totals[0] / D)[:, None]
        variance = (totals[1] / D)[:, None] - row_mean * row_mean
        inv_std = lax.rsqrt(variance + epsilon)
        standard = (values - row_mean) * inv_std
        normed = gather_rows((standard * norm_gain).astype(bf16))

        bias = lax.dynamic_slice_in_dim(bias_up, me * shard, shard)

        def middle(c):
            grad_act = scatter_plane(cot[c], w_down, me, shard, True)
            hidden = scatter_plane(normed[c], w_up, me, shard, False) + bias
            upper = 0.5 * (1.0 + lax.erf(hidden * inv_root_two))
            act = (hidden * upper).astype(bf16)
            slope = upper + hidden * jnp.exp(-0.5 * hidden * hidden) * inv_root_two_pi
            return act, (grad_act * slope).astype(bf16)

        acts, grads = zip(*[middle(c) for c in range(2)])

        def send_home(keep, go):
            ready = (keep + along_gy(go, 1).astype(f32)).astype(bf16)
            return sum(
                along_gy(ready[(k - 1) * rows : k * rows], 2 * k).astype(f32) for k in range(1, n_gy // 2)
            )

        def at_home(keep, go):
            return keep + along_gy(go, 1).astype(f32)

        grad = [gather_plane(grads[c]) for c in range(2)]
        grad_normed = send_home(*summed_product(*grad[1], w_up, me, False))
        grad_normed += at_home(*summed_product(*grad[0], w_up, me, False))
        up = weight_grad_up(normed, (grad[0][0], grad[1][0]), me, (0, 2), shard, units, None)
        up = weight_grad_up(normed, (grad[0][1], grad[1][1]), me, (1, 3), shard, units, up)
        grad_w_up, grad_bias_up = up[0], up[1][0]

        act = [None, gather_plane(acts[1])]
        act[0] = gather_plane(acts[0])
        mlp_out = send_home(*summed_product(*act[1], w_down, me, True))
        mlp_out += at_home(*summed_product(*act[0], w_down, me, True))
        mlp_out = (mlp_out + bias_down).astype(bf16)
        down = weight_grad_down((act[0][0], act[1][0]), cot, me, (0, 2), shard, units, None)
        grad_w_down = weight_grad_down((act[0][1], act[1][1]), cot, me, (1, 3), shard, units, down)

        grad_bias_down = jnp.sum(cot[0].astype(f32), axis=0) + jnp.sum(cot[1].astype(f32), axis=0)

        grad_gain = jnp.sum(grad_normed * standard, axis=0)
        for step in bits(n_gy):
            grad_gain = grad_gain + along_gy(grad_gain, step)
        scaled = grad_normed * norm_gain
        sums = plane_sum(jnp.stack([jnp.sum(scaled, axis=1), jnp.sum(scaled * standard, axis=1)]))
        first_mean = (sums[0] / D)[:, None]
        second_mean = (sums[1] / D)[:, None]
        grad_patches = (inv_std * (scaled - first_mean - standard * second_mean)).astype(bf16)
        return mlp_out, grad_patches, grad_gain, grad_w_up, grad_bias_up, grad_w_down, grad_bias_down

    in_specs = (
        P("gy", "gx"),
        P("gx"),
        P("gx", "gy"),
        P("gy"),
        P("gy", "gx"),
        P("gx"),
        P("gy", "gx"),
    )
    out_specs = (
        P("gy", "gx"),
        P("gy", "gx"),
        P("gx"),
        P("gx", "gy"),
        P("gy"),
        P("gy", "gx"),
        P("gx"),
    )
    return jax.shard_map(shards, mesh=mesh, in_specs=in_specs, out_specs=out_specs, check_vma=False)
```

time: 432 us -> 260 us (0.60)
  waiting for transfers between devices: 292 us -> 76.2 us
  Pallas kernels: 0 us -> 85.4 us
  matrix products: 59.1 us -> 0 us
  blocking collectives: 48.8 us -> 0 us
  starting transfers between devices: 0.38 us -> 47.9 us
  local copies, waits for them, and re-layouts: 1.69 us -> 26.5 us
  between operations: 13.8 us -> 1.25 us
  other arithmetic: 15.2 us -> 21.8 us
    psum x1 -> x0, waiting for transfers between devices: 240 us -> none  [shards(): hidden = lax.psum(partial_value, 'gx') + bias_up]
    pallas_call x0 -> x16, Pallas kernels: none -> 85.4 us  [the longest x8 29.9 us: partial_product(): pl.pallas_call(kernel, grid_spec=pltpu.PrefetchScalarGridSpec(num_scalar_...]
    ppermute x0 -> x43, waiting for transfers between devices: none -> 76.2 us  [the longest x23 53.5 us: along_gy(): return lax.ppermute(x, 'gy', [(i, i ^ m) for i in range(n_gy)])]
    dot_general x6 -> x0, matrix products: 59.1 us -> none  [the longest x2 21 us: over_rows(): lax.dot_general(left, right, (((0,), (0,)), ((), ())), preferred_element_...]
    psum x3 -> x0, blocking collectives: 48.8 us -> none  [the longest x1 27.6 us: shards(): lax.psum((jnp.sum(grad_normed * standard, axis=0), jnp.sum(cotangent, axi...]
    ppermute x0 -> x43, starting transfers between devices: none -> 47.9 us  [the longest x23 21.3 us: along_gy(): return lax.ppermute(x, 'gy', [(i, i ^ m) for i in range(n_gy)])]
    all_gather x2 -> x0, waiting for transfers between devices: 40.3 us -> none  [the longest x1 23.8 us: shards(): lax.all_gather(normed, 'gy', axis=0, tiled=True)]
    unnamed x14 -> x89, local copies, waits for them, and re-layouts: 1.69 us -> 24.7 us
  transfers between devices with their start and end apart: 5 -> 43, of which waited for: 5 -> 16; matrix products, arithmetic and copies ran while one was open for 10% -> 9% of each run, Pallas kernels for 0% -> 33%
where the time goes in v1:
time: 260 us; the launch traced here: 259 us
  Pallas kernels  85.4 us (33%)
  waiting for transfers between devices  76.2 us (29%)
  starting transfers between devices  47.9 us (18%)
  local copies, waits for them, and re-layouts  26.5 us (10%)
  other arithmetic  21.8 us (8%)
    ppermute x23, waiting for transfers between devices, along_gy(): return lax.ppermute(x, 'gy', [(i, i ^ m) for i in range(n_gy)])  53.5 us
    pallas_call x8, Pallas kernels, partial_product(): pl.pallas_call(kernel, grid_spec=pltpu.PrefetchScalarGridSpec(num_scalar_...  29.9 us
    unnamed x89, local copies, waits for them, and re-layouts  24.7 us
    pallas_call x4, Pallas kernels, summed_product(): pl.pallas_call(kernel, grid_spec=pltpu.PrefetchScalarGridSpec(num_scalar_...  24.1 us
    ppermute x23, starting transfers between devices, along_gy(): return lax.ppermute(x, 'gy', [(i, i ^ m) for i in range(n_gy)])  21.3 us
    pallas_call x2, Pallas kernels, weight_grad_down(): pl.pallas_call(kernel, grid_spec=pltpu.PrefetchScalarGridSpec(num_scalar_...  15.9 us
    pallas_call x2, Pallas kernels, weight_grad_up(): pl.pallas_call(kernel, grid_spec=pltpu.PrefetchScalarGridSpec(num_scalar_...  15.4 us
    ppermute x8, waiting for transfers between devices, to_first(): return lax.ppermute(x, both, first_pairs)  13.2 us
  transfers between devices with their start and end apart: 43, of which 16 were waited for; matrix products, arithmetic and copies ran while one was open for 9% of the time, Pallas kernels for 33%

profile of v1, /device:TPU:0, one launch (start us, length us, event | category | flops | bytes accessed | tf_op | source)
XLA Modules:
  0.0 259.1 jit_solution(18404235018991361171)
XLA Ops:
  1.1 2.7 %collective-permute-start.20 = (bf16[64,1536]{1,0:T(8,128)(2,1)}, bf16[64,1536]{1,0:T(8,128)(2,1)S(1)}, u32[]{:S(2)}, u32[]{:S(2)}) collective-permute-start(bf16[64,1536]{1,0:T(8,128)(2,1)} %param.13), channel_id=1, source_target_pairs={{0,2},{1,3},{2,0},{3,1},{4,6},{5,7},{6,4},{7,5},{8,10},{9,11},{10,... | collective-permute-start | bytes 589832 | tf_op jit(solution)/shard_map/ppermute | solution.py:197
  3.8 2.6 collective-permute-start.21
  7.5 1.8 collective-permute-start
  11.1 1.8 collective-permute-start.1
  17.0 4.2 %collective-permute-done.21 = bf16[64,1536]{1,0:T(8,128)(2,1)S(1)} collective-permute-done((bf16[64,1536]{1,0:T(8,128)(2,1)}, bf16[64,1536]{1,0:T(8,128)(2,1)S(1)}, u32[]{:S(2)}, u32[]{:S(2)}) %collective-permute-start.21) | collective-permute-done | bytes 196640 | tf_op jit(solution)/shard_map/ppermute | solution.py:197
  21.2 2.5 collective-permute-start.4
  23.8 1.9 collective-permute-done.2
  25.7 12.3 %collective-permute-done.3 = bf16[64,1536]{1,0:T(8,128)(2,1)S(1)} collective-permute-done((bf16[64,1536]{1,0:T(8,128)(2,1)S(1)}, bf16[64,1536]{1,0:T(8,128)(2,1)S(1)}, u32[]{:S(2)}, u32[]{:S(2)}) %collective-permute-start.3) | collective-permute-done | bytes 196640 | tf_op jit(solution)/shard_map/ppermute | solution.py:197
  38.2 3.7 %copy-done.1 = bf16[3072,1536]{1,0:T(8,128)(2,1)S(1)} copy-done((bf16[3072,1536]{1,0:T(8,128)(2,1)S(1)}, bf16[3072,1536]{1,0:T(8,128)(2,1)}, u32[]{:S(2)}) %copy-start.1) | copy-done | bytes 9437208
  41.9 4.6 %shard_map.133 = bf16[384,1536]{1,0:T(8,128)(2,1)} custom-call(s32[4]{0:T(128)S(1)} %get-tuple-element.52.index_ref, bf16[384,1536]{1,0:T(8,128)(2,1)S(1)} %constant_dynamic-update-slice_fusion.4.x_ref.c1, bf16[3072,1536]{1,0:T(8,128)(2,1)S(1)} %copy-done.1), custom_call_target="tpu_custom_call" | custom-call | flops 1811939328 | bytes 8257536 | tf_op jit(solution)/shard_map/pallas_call | solution.py:58
  46.5 1.5 collective-permute-start.24
  48.0 5.2 %shard_map.127 = bf16[384,1536]{1,0:T(8,128)(2,1)} custom-call(s32[4]{0:T(128)S(1)} %get-tuple-element.52.index_ref, bf16[384,1536]{1,0:T(8,128)(2,1)S(1)} %constant_dynamic-update-slice_fusion.x_ref.n1, bf16[1536,3072]{1,0:T(8,128)(2,1)S(1)} %copy-done), custom_call_target="tpu_custom_call" | custom-call | flops 1811939328 | bytes 8257536 | tf_op jit(solution)/shard_map/pallas_call | solution.py:58
  54.8 3.7 %copy-done.2 = bf16[3072,1536]{1,0:T(8,128)(2,1)S(1)} copy-done((bf16[3072,1536]{1,0:T(8,128)(2,1)S(1)}, bf16[3072,1536]{1,0:T(8,128)(2,1)}, u32[]{:S(2)}) %copy-start.2) | copy-done | bytes 9437208
  58.4 2.7 %shard_map.136 = bf16[128,1536]{1,0:T(8,128)(2,1)S(1)} custom-call(s32[4]{0:T(128)S(1)} %get-tuple-element.52.index_ref, bf16[128,1536]{1,0:T(8,128)(2,1)S(1)} %constant_dynamic-update-slice_fusion.8.x_ref.c0, bf16[3072,1536]{1,0:T(8,128)(2,1)S(1)} %copy-done.2), custom_call_target="tpu_custom_call" | custom-call | flops 603979776 | bytes 5898240 | tf_op jit(solution)/shard_map/pallas_call | solution.py:58
  61.1 1.6 collective-permute-start.33
  63.6 3.5 %shard_map.130 = bf16[128,1536]{1,0:T(8,128)(2,1)} custom-call(s32[4]{0:T(128)S(1)} %get-tuple-element.52.index_ref, bf16[128,1536]{1,0:T(8,128)(2,1)S(1)} %pad_maximum_fusion.4.x_ref.n0, bf16[1536,3072]{1,0:T(8,128)(2,1)S(1)} %copy-done), custom_call_target="tpu_custom_call" | custom-call | flops 603979776 | bytes 5898240 | tf_op jit(solution)/shard_map/pallas_call | solution.py:58
  67.7 3.7 %copy-done.3 = bf16[3072,1536]{1,0:T(8,128)(2,1)S(1)} copy-done((bf16[3072,1536]{1,0:T(8,128)(2,1)S(1)}, bf16[3072,1536]{1,0:T(8,128)(2,1)}, u32[]{:S(2)}) %copy-start.3) | copy-done | bytes 9437208
  71.4 3.8 %shard_map.132 = f32[384,1536]{1,0:T(8,128)S(1)} custom-call(s32[4]{0:T(128)S(1)} %get-tuple-element.50.index_ref, bf16[384,1536]{1,0:T(8,128)(2,1)S(1)} %constant_dynamic-update-slice_fusion.4.x_ref.c1, bf16[3072,1536]{1,0:T(8,128)(2,1)S(1)} %copy-done.3), custom_call_target="tpu_custom_call" | custom-call | flops 1811939328 | bytes 8257536 | tf_op jit(solution)/shard_map/pallas_call | solution.py:58
  75.2 1.4 copy-done.9
  76.6 4.5 %shard_map.126 = f32[384,1536]{1,0:T(8,128)S(1)} custom-call(s32[4]{0:T(128)S(1)} %get-tuple-element.50.index_ref, bf16[384,1536]{1,0:T(8,128)(2,1)S(1)} %copy-done.6, bf16[1536,3072]{1,0:T(8,128)(2,1)S(1)} %copy-done), custom_call_target="tpu_custom_call" | custom-call | flops 1811939328 | bytes 8257536 | tf_op jit(solution)/shard_map/pallas_call | solution.py:58
  81.2 3.3 %fusion.6 = bf16[384,768]{1,0:T(8,128)(2,1)} fusion(f32[384,1536]{1,0:T(8,128)} %copy-done.9, bf16[384,1536]{1,0:T(8,128)(2,1)} %collective-permute-done.24), kind=kLoop, calls=%fused_computation.9 | loop fusion | flops 884736 | bytes 2359296 | tf_op jit(solution)/shard_map/convert_element_type | solution.py:215
  84.4 1.5 collective-permute-start.25
  86.0 2.1 fusion.8
  88.6 3.7 %copy-done.4 = bf16[3072,1536]{1,0:T(8,128)(2,1)S(1)} copy-done((bf16[3072,1536]{1,0:T(8,128)(2,1)S(1)}, bf16[3072,1536]{1,0:T(8,128)(2,1)}, u32[]{:S(2)}) %copy-start.4) | copy-done | bytes 9437208
  92.3 2.7 %shard_map.135 = f32[128,1536]{1,0:T(8,128)S(1)} custom-call(s32[4]{0:T(128)S(1)} %get-tuple-element.50.index_ref, bf16[128,1536]{1,0:T(8,128)(2,1)S(1)} %constant_dynamic-update-slice_fusion.8.x_ref.c0, bf16[3072,1536]{1,0:T(8,128)(2,1)S(1)} %copy-done.4), custom_call_target="tpu_custom_call" | custom-call | flops 603979776 | bytes 5898240 | tf_op jit(solution)/shard_map/pallas_call | solution.py:58
  95.9 2.9 %shard_map.129 = f32[128,1536]{1,0:T(8,128)S(1)} custom-call(s32[4]{0:T(128)S(1)} %get-tuple-element.50.index_ref, bf16[128,1536]{1,0:T(8,128)(2,1)S(1)} %pad_maximum_fusion.4.x_ref.n0, bf16[1536,3072]{1,0:T(8,128)(2,1)S(1)} %copy-done), custom_call_target="tpu_custom_call" | custom-call | flops 603979776 | bytes 5898240 | tf_op jit(solution)/shard_map/pallas_call | solution.py:58
  98.8 1.4 fusion.29
  100.2 1.6 collective-permute-start.34
  103.4 2.5 fusion.5
  105.9 1.5 collective-permute-start.26
  107.5 2.7 %collective-permute-done.16 = bf16[128,768]{1,0:T(8,128)(2,1)S(1)} collective-permute-done((bf16[128,768]{1,0:T(8,128)(2,1)S(1)}, bf16[128,768]{1,0:T(8,128)(2,1)S(1)}, u32[]{:S(2)}, u32[]{:S(2)}) %collective-permute-start.16) | collective-permute-done | bytes 196640 | tf_op jit(solution)/shard_map/ppermute | solution.py:194
  110.2 1.3 fusion.28
  111.5 1.7 collective-permute-start.17
  113.7 1.6 collective-permute-start.8
  115.4 2.6 %collective-permute-done.17 = bf16[128,768]{1,0:T(8,128)(2,1)S(1)} collective-permute-done((bf16[128,768]{1,0:T(8,128)(2,1)S(1)}, bf16[128,768]{1,0:T(8,128)(2,1)S(1)}, u32[]{:S(2)}, u32[]{:S(2)}) %collective-permute-start.17) | collective-permute-done | bytes 196640 | tf_op jit(solution)/shard_map/ppermute | solution.py:191
  118.0 1.6 collective-permute-start.18
  120.4 2.1 collective-permute-start.36
  122.4 10.5 %collective-permute-done.8 = bf16[384,768]{1,0:T(8,128)(2,1)S(1)} collective-permute-done((bf16[384,768]{1,0:T(8,128)(2,1)S(1)}, bf16[384,768]{1,0:T(8,128)(2,1)S(1)}, u32[]{:S(2)}, u32[]{:S(2)}) %collective-permute-start.8) | collective-permute-done | bytes 589856 | tf_op jit(solution)/shard_map/ppermute | solution.py:191
  134.1 2.0 collective-permute-start.9
  136.9 4.0 %shard_map.131 = (f32[64,1536]{1,0:T(8,128)S(1)}, bf16[64,1536]{1,0:T(8,128)(2,1)}) custom-call(s32[1]{0:T(128)} %bitcast.me_ref, bf16[128,1536]{1,0:T(8,128)(2,1)S(1)} %pad_maximum_fusion.5.near_ref.p0, bf16[128,1536]{1,0:T(8,128)(2,1)S(1)} %collective-permute-done.18.far_ref.p0, bf16[3072,1536]{1,0:T(8,128)(2,1)S(1)} %bitcast.21, ...), custom_call_target="tpu_custom_call" | custom-call | flops 1207959552 | bytes 10813440 | tf_op jit(solution)/shard_map/pallas_call | solution.py:94
  141.6 4.9 %collective-permute-done.36.far_ref.p0 = bf16[128,1536]{1,0:T(8,128)(2,1)} collective-permute-done((bf16[128,1536]{1,0:T(8,128)(2,1)S(1)}, bf16[128,1536]{1,0:T(8,128)(2,1)}, u32[]{:S(2)}, u32[]{:S(2)}) %collective-permute-start.36) | collective-permute-done | bytes 393248 | tf_op jit(solution)/shard_map/ppermute | solution.py:194
  147.5 6.3 %shard_map.137 = (f32[64,1536]{1,0:T(8,128)S(1)}, bf16[64,1536]{1,0:T(8,128)(2,1)}) custom-call(s32[1]{0:T(128)} %bitcast.me_ref, bf16[128,1536]{1,0:T(8,128)(2,1)S(1)} %copy-done.25, bf16[128,1536]{1,0:T(8,128)(2,1)} %collective-permute-done.36.far_ref.p0, bf16[1536,3072]{1,0:T(8,128)(2,1)S(1)} %copy-done, bf16[1536,3072]{1,0:T(8,128)(2,1)S(1)} %copy-done, ...), custom_call_target="tpu_custom_call" | custom-call | flops 1207959552 | bytes 10813440 | tf_op jit(solution)/shard_map/pallas_call | solution.py:94
  154.6 1.1 collective-permute-start.37
  155.8 7.3 %shard_map.138 = (f32[1536,3072]{1,0:T(8,128)}, f32[1,3072]{1,0:T(1,128)}) custom-call(s32[4]{0:T(128)S(1)} %get-tuple-element.49.index_ref, bf16[128,1536]{1,0:T(8,128)(2,1)S(1)} %pad_maximum_fusion.4.x_ref.n0, bf16[384,1536]{1,0:T(8,128)(2,1)S(1)} %copy-done.7, bf16[128,1536]{1,0:T(8,128)(2,1)S(1)} %copy-done.25, ...), custom_call_target="tpu_custom_call" | custom-call | flops 2415919104 | bytes 9437184 | tf_op jit(solution)/shard_map/pallas_call | solution.py:158
  163.1 8.0 %shard_map.140.refs_0_ = f32[3072,1536]{1,0:T(8,128)} custom-call(s32[4]{0:T(128)S(1)} %get-tuple-element.49.index_ref, bf16[128,1536]{1,0:T(8,128)(2,1)S(1)} %pad_maximum_fusion.5.near_ref.p0, bf16[384,1536]{1,0:T(8,128)(2,1)} %pad_maximum_fusion.near_ref.p1, bf16[128,1536]{1,0:T(8,128)(2,1)S(1)} %constant_dynamic-update-slice_fusion.8.x_ref.c0, ...), custom_call_target="tpu_custom_call" | custom-call | flops 2415919104 | bytes 9437184 | tf_op jit(solution)/shard_map/pallas_call | solution.py:124
  172.2 1.9 copy-done.14
  174.1 6.4 %shard_map.134 = (f32[192,1536]{1,0:T(8,128)S(1)}, bf16[192,1536]{1,0:T(8,128)(2,1)}) custom-call(s32[1]{0:T(128)} %bitcast.me_ref, bf16[384,1536]{1,0:T(8,128)(2,1)S(1)} %copy-done.17, bf16[384,1536]{1,0:T(8,128)(2,1)S(1)} %copy-done.14, bf16[1536,3072]{1,0:T(8,128)(2,1)S(1)} %copy-done, bf16[1536,3072]{1,0:T(8,128)(2,1)S(1)} %copy-done, ...), custom_call_target="tpu_custom_call" | custom-call | flops 3623878656 | bytes 13565952 | tf_op jit(solution)/shard_map/pallas_call | solution.py:94
  181.6 7.4 %shard_map.128 = (f32[192,1536]{1,0:T(8,128)S(1)}, bf16[192,1536]{1,0:T(8,128)(2,1)S(1)}) custom-call(s32[1]{0:T(128)} %bitcast.me_ref, bf16[384,1536]{1,0:T(8,128)(2,1)} %pad_maximum_fusion.near_ref.p1, bf16[384,1536]{1,0:T(8,128)(2,1)} %collective-permute-done.9.far_ref.p1, bf16[3072,1536]{1,0:T(8,128)(2,1)S(1)} %bitcast.23, ...), custom_call_target="tpu_custom_call" | custom-call | flops 3623878656 | bytes 13565952 | tf_op jit(solution)/shard_map/pallas_call | solution.py:94
  189.6 7.9 %shard_map.141 = f32[3072,1536]{1,0:T(8,128)} custom-call(s32[4]{0:T(128)S(1)} %get-tuple-element.51.index_ref, bf16[128,1536]{1,0:T(8,128)(2,1)S(1)} %copy-done.23, bf16[384,1536]{1,0:T(8,128)(2,1)} %collective-permute-done.9.far_ref.p1, bf16[128,1536]{1,0:T(8,128)(2,1)S(1)} %constant_dynamic-update-slice_fusion.8.x_ref.c0, ...), custom_call_target="tpu_custom_call", output_to_operand_aliasing={{}: (5, {})} | custom-call | flops 2415919104 | bytes 9437184 | tf_op jit(solution)/shard_map/pallas_call | solution.py:124
  197.5 8.1 %shard_map.139 = (f32[1536,3072]{1,0:T(8,128)}, f32[1,3072]{1,0:T(1,128)}) custom-call(s32[4]{0:T(128)S(1)} %get-tuple-element.51.index_ref, bf16[128,1536]{1,0:T(8,128)(2,1)S(1)} %pad_maximum_fusion.4.x_ref.n0, bf16[384,1536]{1,0:T(8,128)(2,1)S(1)} %copy-done.8, ...), custom_call_target="tpu_custom_call", output_to_operand_aliasing={{0}: (5, {}), {1}: (6, {})} | custom-call | flops 2415919104 | bytes 9437184 | tf_op jit(solution)/shard_map/pallas_call | solution.py:158
  205.8 2.5 collective-permute-start.31
  208.3 3.0 %collective-permute-start.30 = (bf16[64,1536]{1,0:T(8,128)(2,1)S(1)}, bf16[64,1536]{1,0:T(8,128)(2,1)S(1)}, u32[]{:S(2)}, u32[]{:S(2)}) collective-permute-start(bf16[64,1536]{1,0:T(8,128)(2,1)S(1)} %get-tuple-element.43), channel_id=1, source_target_pairs={{0,4},{1,5},{2,6},{3,7},{4,0},{5,1},{6,2},{7,3},{8,12},{9,13},{10,... | collective-permute-start | bytes 589832 | tf_op jit(solution)/shard_map/ppermute | solution.py:197
  211.6 3.3 %collective-permute-done.31 = bf16[64,1536]{1,0:T(8,128)(2,1)S(1)} collective-permute-done((bf16[64,1536]{1,0:T(8,128)(2,1)S(1)}, bf16[64,1536]{1,0:T(8,128)(2,1)S(1)}, u32[]{:S(2)}, u32[]{:S(2)}) %collective-permute-start.31) | collective-permute-done | bytes 196640 | tf_op jit(solution)/shard_map/ppermute | solution.py:197
  214.9 12.2 %collective-permute-done.30 = bf16[64,1536]{1,0:T(8,128)(2,1)S(1)} collective-permute-done((bf16[64,1536]{1,0:T(8,128)(2,1)S(1)}, bf16[64,1536]{1,0:T(8,128)(2,1)S(1)}, u32[]{:S(2)}, u32[]{:S(2)}) %collective-permute-start.30) | collective-permute-done | bytes 196640 | tf_op jit(solution)/shard_map/ppermute | solution.py:197
  227.2 1.3 fusion.22
  228.5 1.5 collective-permute-start.38
  230.1 2.5 collective-permute-start.13
  232.6 1.9 collective-permute-start.11
  234.6 1.6 collective-permute-start.39
  236.2 3.7 %collective-permute-done.13 = bf16[64,1536]{1,0:T(8,128)(2,1)S(1)} collective-permute-done((bf16[64,1536]{1,0:T(8,128)(2,1)S(1)}, bf16[64,1536]{1,0:T(8,128)(2,1)S(1)}, u32[]{:S(2)}, u32[]{:S(2)}) %collective-permute-start.13) | collective-permute-done | bytes 196640 | tf_op jit(solution)/shard_map/ppermute | solution.py:197
  239.8 8.6 %collective-permute-done.12 = bf16[64,1536]{1,0:T(8,128)(2,1)S(1)} collective-permute-done((bf16[64,1536]{1,0:T(8,128)(2,1)S(1)}, bf16[64,1536]{1,0:T(8,128)(2,1)S(1)}, u32[]{:S(2)}, u32[]{:S(2)}) %collective-permute-start.12) | collective-permute-done | bytes 196640 | tf_op jit(solution)/shard_map/ppermute | solution.py:197
  248.5 1.7 add_convert_fusion.2
  250.3 3.6 %collective-permute-done.41 = f32[1536]{0:T(1024)S(1)} collective-permute-done((f32[1536]{0:T(1024)S(1)}, f32[1536]{0:T(1024)S(1)}, u32[]{:S(2)}, u32[]{:S(2)}) %collective-permute-start.41) | collective-permute-done | bytes 6176 | tf_op jit(solution)/shard_map/ppermute | solution.py:197
  254.8 3.7 %collective-permute-done.42 = f32[1536]{0:T(1024)S(1)} collective-permute-done((f32[1536]{0:T(1024)S(1)}, f32[1536]{0:T(1024)S(1)}, u32[]{:S(2)}, u32[]{:S(2)}) %collective-permute-start.42) | collective-permute-done | bytes 6176 | tf_op jit(solution)/shard_map/ppermute | solution.py:197
  (173 shorter events, 24.3 us)
Async XLA Ops:
  0.6 53.2 %collective-permute-start.32 = (bf16[64,1536]{1,0:T(8,128)(2,1)}, bf16[64,1536]{1,0:T(8,128)(2,1)}, u32[]{:S(2)}, u32[]{:S(2)}) collective-permute-start(bf16[64,1536]{1,0:T(8,128)(2,1)} %param.13), channel_id=1, source_target_pairs={{0,1},{1,0},{2,3},{3,2},{4,5},{5,4},{6,7},{7,6},{8,9},{9,8},{10,11... | collective-permute-start | bytes 589832 | tf_op jit(solution)/shard_map/ppermute | solution.py:197
  1.1 14.8 %collective-permute-start.20 = (bf16[64,1536]{1,0:T(8,128)(2,1)}, bf16[64,1536]{1,0:T(8,128)(2,1)S(1)}, u32[]{:S(2)}, u32[]{:S(2)}) collective-permute-start(bf16[64,1536]{1,0:T(8,128)(2,1)} %param.13), channel_id=1, source_target_pairs={{0,2},{1,3},{2,0},{3,1},{4,6},{5,7},{6,4},{7,5},{8,10},{9,11},{10,... | collective-permute-start | bytes 589832 | tf_op jit(solution)/shard_map/ppermute | solution.py:197
  3.8 17.3 %collective-permute-start.21 = (bf16[64,1536]{1,0:T(8,128)(2,1)}, bf16[64,1536]{1,0:T(8,128)(2,1)S(1)}, u32[]{:S(2)}, u32[]{:S(2)}) collective-permute-start(bf16[64,1536]{1,0:T(8,128)(2,1)} %param.13), channel_id=1, source_target_pairs={{0,4},{1,5},{2,6},{3,7},{4,0},{5,1},{6,2},{7,3},{8,12},{9,13},{10,... | collective-permute-start | bytes 589832 | tf_op jit(solution)/shard_map/ppermute | solution.py:197
  6.4 14.8 %collective-permute-start.22 = (bf16[64,1536]{1,0:T(8,128)(2,1)}, bf16[64,1536]{1,0:T(8,128)(2,1)S(1)}, u32[]{:S(2)}, u32[]{:S(2)}) collective-permute-start(bf16[64,1536]{1,0:T(8,128)(2,1)} %param.13), channel_id=1, source_target_pairs={{0,6},{1,7},{2,4},{3,5},{4,2},{5,3},{6,0},{7,1},{8,14},{9,15},{10,... | collective-permute-start | bytes 589832 | tf_op jit(solution)/shard_map/ppermute | solution.py:197
  7.5 3.6 %collective-permute-start = (f32[2,64]{1,0:T(2,128)S(1)}, f32[2,64]{1,0:T(2,128)S(1)}, u32[]{:S(2)}, u32[]{:S(2)}) collective-permute-start(f32[2,64]{1,0:T(2,128)S(1)} %pad_maximum_fusion.7), channel_id=1, source_target_pairs={{0,8},{8,0},{16,24},{24,16},{1,9},{9,1},{17,25},{25,17},{2,10},{10... | collective-permute-start | bytes 1544 | tf_op jit(solution)/shard_map/ppermute | solution.py:200
  11.1 3.6 %collective-permute-start.1 = (f32[2,64]{1,0:T(2,128)S(1)}, f32[2,64]{1,0:T(2,128)S(1)}, u32[]{:S(2)}, u32[]{:S(2)}) collective-permute-start(f32[2,64]{1,0:T(2,128)S(1)} %fusion.37), channel_id=1, source_target_pairs={{0,16},{8,24},{16,0},{24,8},{1,17},{9,25},{17,1},{25,9},{2,18},{10... | collective-permute-start | bytes 1544 | tf_op jit(solution)/shard_map/ppermute | solution.py:200
  15.9 46.8 %collective-permute-start.14 = (bf16[64,1536]{1,0:T(8,128)(2,1)S(1)}, bf16[64,1536]{1,0:T(8,128)(2,1)}, u32[]{:S(2)}, u32[]{:S(2)}) collective-permute-start(bf16[64,1536]{1,0:T(8,128)(2,1)S(1)} %fusion.17), channel_id=1, source_target_pairs={{0,1},{1,0},{2,3},{3,2},{4,5},{5,4},{6,7},{7,6},{8,9},{9,8},{10,11... | collective-permute-start | bytes 589832 | tf_op jit(solution)/shard_map/ppermute | solution.py:197
  16.0 9.7 %collective-permute-start.2 = (bf16[64,1536]{1,0:T(8,128)(2,1)S(1)}, bf16[64,1536]{1,0:T(8,128)(2,1)S(1)}, u32[]{:S(2)}, u32[]{:S(2)}) collective-permute-start(bf16[64,1536]{1,0:T(8,128)(2,1)S(1)} %fusion.17), channel_id=1, source_target_pairs={{0,2},{1,3},{2,0},{3,1},{4,6},{5,7},{6,4},{7,5},{8,10},{9,11},{10,... | collective-permute-start | bytes 589832 | tf_op jit(solution)/shard_map/ppermute | solution.py:197
  21.1 16.9 %collective-permute-start.3 = (bf16[64,1536]{1,0:T(8,128)(2,1)S(1)}, bf16[64,1536]{1,0:T(8,128)(2,1)S(1)}, u32[]{:S(2)}, u32[]{:S(2)}) collective-permute-start(bf16[64,1536]{1,0:T(8,128)(2,1)S(1)} %fusion.17), channel_id=1, source_target_pairs={{0,4},{1,5},{2,6},{3,7},{4,0},{5,1},{6,2},{7,3},{8,12},{9,13},{10,... | collective-permute-start | bytes 589832 | tf_op jit(solution)/shard_map/ppermute | solution.py:197
  21.2 16.8 %collective-permute-start.4 = (bf16[64,1536]{1,0:T(8,128)(2,1)S(1)}, bf16[64,1536]{1,0:T(8,128)(2,1)S(1)}, u32[]{:S(2)}, u32[]{:S(2)}) collective-permute-start(bf16[64,1536]{1,0:T(8,128)(2,1)S(1)} %fusion.17), channel_id=1, source_target_pairs={{0,6},{1,7},{2,4},{3,5},{4,2},{5,3},{6,0},{7,1},{8,14},{9,15},{10,... | collective-permute-start | bytes 589832 | tf_op jit(solution)/shard_map/ppermute | solution.py:197
  25.7 12.5 %collective-permute-start.23 = (bf16[192,1536]{1,0:T(8,128)(2,1)S(1)}, bf16[192,1536]{1,0:T(8,128)(2,1)S(1)}, u32[]{:S(2)}, u32[]{:S(2)}) collective-permute-start(bf16[192,1536]{1,0:T(8,128)(2,1)S(1)} %pad_maximum_fusion.3), channel_id=1, source_target_pairs={{0,1},{1,0},{2,3},{3,2},{4,5},{5,4},{6,7},{7,6},{8,9},{9,8},{10,11... | collective-permute-start | bytes 1769480 | tf_op jit(solution)/shard_map/ppermute | solution.py:197
  38.0 9.9 %collective-permute-start.5 = (bf16[192,1536]{1,0:T(8,128)(2,1)S(1)}, bf16[192,1536]{1,0:T(8,128)(2,1)S(1)}, u32[]{:S(2)}, u32[]{:S(2)}) collective-permute-start(bf16[192,1536]{1,0:T(8,128)(2,1)S(1)} %pad_maximum_fusion.2), channel_id=1, source_target_pairs={{0,1},{1,0},{2,3},{3,2},{4,5},{5,4},{6,7},{7,6},{8,9},{9,8},{10,11... | collective-permute-start | bytes 1769480 | tf_op jit(solution)/shard_map/ppermute | solution.py:197
  46.5 34.7 %collective-permute-start.24 = (bf16[384,1536]{1,0:T(8,128)(2,1)}, bf16[384,1536]{1,0:T(8,128)(2,1)}, u32[]{:S(2)}, u32[]{:S(2)}) collective-permute-start(bf16[384,1536]{1,0:T(8,128)(2,1)} %shard_map.133), channel_id=1, source_target_pairs={{0,8},{1,17},{2,10},{3,19},{4,12},{5,21},{6,14},{7,23},{8,0},{9,25... | collective-permute-start | bytes 3538952 | tf_op jit(solution)/shard_map/ppermute | solution.py:191
  53.3 32.7 %collective-permute-start.6 = (bf16[384,1536]{1,0:T(8,128)(2,1)}, bf16[384,1536]{1,0:T(8,128)(2,1)}, u32[]{:S(2)}, u32[]{:S(2)}) collective-permute-start(bf16[384,1536]{1,0:T(8,128)(2,1)} %shard_map.127), channel_id=1, source_target_pairs={{0,8},{1,17},{2,10},{3,19},{4,12},{5,21},{6,14},{7,23},{8,0},{9,25... | collective-permute-start | bytes 3538952 | tf_op jit(solution)/shard_map/ppermute | solution.py:191
  61.1 37.7 %collective-permute-start.33 = (bf16[128,1536]{1,0:T(8,128)(2,1)S(1)}, bf16[128,1536]{1,0:T(8,128)(2,1)}, u32[]{:S(2)}, u32[]{:S(2)}) collective-permute-start(bf16[128,1536]{1,0:T(8,128)(2,1)S(1)} %shard_map.136), channel_id=1, source_target_pairs={{0,8},{1,17},{2,10},{3,19},{4,12},{5,21},{6,14},{7,23},{8,0},{9,25... | collective-permute-start | bytes 1179656 | tf_op jit(solution)/shard_map/ppermute | solution.py:191
  67.2 34.6 %collective-permute-start.15 = (bf16[128,1536]{1,0:T(8,128)(2,1)}, bf16[128,1536]{1,0:T(8,128)(2,1)}, u32[]{:S(2)}, u32[]{:S(2)}) collective-permute-start(bf16[128,1536]{1,0:T(8,128)(2,1)} %shard_map.130), channel_id=1, source_target_pairs={{0,8},{1,17},{2,10},{3,19},{4,12},{5,21},{6,14},{7,23},{8,0},{9,25... | collective-permute-start | bytes 1179656 | tf_op jit(solution)/shard_map/ppermute | solution.py:191
  84.4 18.9 %collective-permute-start.25 = (bf16[384,768]{1,0:T(8,128)(2,1)}, bf16[384,768]{1,0:T(8,128)(2,1)}, u32[]{:S(2)}, u32[]{:S(2)}) collective-permute-start(bf16[384,768]{1,0:T(8,128)(2,1)} %fusion.6), channel_id=1, source_target_pairs={{0,16},{1,9},{2,18},{3,11},{4,20},{5,13},{6,22},{7,15},{8,24},{9,1... | collective-permute-start | bytes 1769480 | tf_op jit(solution)/shard_map/ppermute | solution.py:194
  88.1 15.3 %collective-permute-start.7 = (bf16[384,768]{1,0:T(8,128)(2,1)}, bf16[384,768]{1,0:T(8,128)(2,1)}, u32[]{:S(2)}, u32[]{:S(2)}) collective-permute-start(bf16[384,768]{1,0:T(8,128)(2,1)} %fusion.8), channel_id=1, source_target_pairs={{0,16},{1,9},{2,18},{3,11},{4,20},{5,13},{6,22},{7,15},{8,24},{9,1... | collective-permute-start | bytes 1769480 | tf_op jit(solution)/shard_map/ppermute | solution.py:194
  95.9 7.5 %copy-start.10 = (f32[384,1536]{1,0:T(8,128)S(1)}, f32[384,1536]{1,0:T(8,128)}, u32[]{:S(2)}) copy-start(f32[384,1536]{1,0:T(8,128)} %copy-done.9) | copy-start | bytes 7077892
  95.9 7.5 %copy-start.12 = (f32[384,1536]{1,0:T(8,128)S(1)}, f32[384,1536]{1,0:T(8,128)}, u32[]{:S(2)}) copy-start(f32[384,1536]{1,0:T(8,128)} %copy-done.11) | copy-start | bytes 7077892
  95.9 41.0 %slice-start = ((s8[9437184]{0:T(1024)(128)(4,1)}), s8[1048576]{0:T(1024)(128)(4,1)S(1)}, s32[]{:S(2)}) async-start(s8[9437184]{0:T(1024)(128)(4,1)} %bitcast.20), calls=%async_computation | async-start | bytes 2097152
  95.9 41.0 %slice-start.1 = ((s8[9437184]{0:T(1024)(128)(4,1)}), s8[4194304]{0:T(1024)(128)(4,1)S(1)}, s32[]{:S(2)}) async-start(s8[9437184]{0:T(1024)(128)(4,1)} %bitcast.20), calls=%async_computation.1 | async-start | bytes 8388608
  100.2 7.3 %collective-permute-start.34 = (bf16[128,768]{1,0:T(8,128)(2,1)S(1)}, bf16[128,768]{1,0:T(8,128)(2,1)S(1)}, u32[]{:S(2)}, u32[]{:S(2)}) collective-permute-start(bf16[128,768]{1,0:T(8,128)(2,1)S(1)} %fusion.29), channel_id=1, source_target_pairs={{0,16},{1,9},{2,18},{3,11},{4,20},{5,13},{6,22},{7,15},{8,24},{9,1... | collective-permute-start | bytes 589832 | tf_op jit(solution)/shard_map/ppermute | solution.py:194
  102.8 7.4 %collective-permute-start.16 = (bf16[128,768]{1,0:T(8,128)(2,1)S(1)}, bf16[128,768]{1,0:T(8,128)(2,1)S(1)}, u32[]{:S(2)}, u32[]{:S(2)}) collective-permute-start(bf16[128,768]{1,0:T(8,128)(2,1)S(1)} %fusion.31), channel_id=1, source_target_pairs={{0,16},{1,9},{2,18},{3,11},{4,20},{5,13},{6,22},{7,15},{8,24},{9,1... | collective-permute-start | bytes 589832 | tf_op jit(solution)/shard_map/ppermute | solution.py:194
  105.9 31.0 %slice-start.2 = ((s8[9437184]{0:T(1024)(128)(4,1)}), s8[4194304]{0:T(1024)(128)(4,1)S(1)}, s32[]{:S(2)}) async-start(s8[9437184]{0:T(1024)(128)(4,1)} %bitcast.20), calls=%async_computation.2 | async-start | bytes 8388608
  105.9 13.7 %collective-permute-start.26 = (bf16[384,768]{1,0:T(8,128)(2,1)S(1)}, bf16[384,768]{1,0:T(8,128)(2,1)S(1)}, u32[]{:S(2)}, u32[]{:S(2)}) collective-permute-start(bf16[384,768]{1,0:T(8,128)(2,1)S(1)} %get-tuple-element.37), channel_id=1, source_target_pairs={{0,8},{1,17},{2,10},{3,19},{4,12},{5,21},{6,14},{7,23},{8,0},{9,25... | collective-permute-start | bytes 1769480 | tf_op jit(solution)/shard_map/ppermute | solution.py:191
  111.5 6.5 %collective-permute-start.17 = (bf16[128,768]{1,0:T(8,128)(2,1)S(1)}, bf16[128,768]{1,0:T(8,128)(2,1)S(1)}, u32[]{:S(2)}, u32[]{:S(2)}) collective-permute-start(bf16[128,768]{1,0:T(8,128)(2,1)S(1)} %get-tuple-element.40), channel_id=1, source_target_pairs={{0,8},{1,17},{2,10},{3,19},{4,12},{5,21},{6,14},{7,23},{8,0},{9,25... | collective-permute-start | bytes 589832 | tf_op jit(solution)/shard_map/ppermute | solution.py:191
  113.3 7.1 %collective-permute-start.35 = (bf16[128,768]{1,0:T(8,128)(2,1)S(1)}, bf16[128,768]{1,0:T(8,128)(2,1)S(1)}, u32[]{:S(2)}, u32[]{:S(2)}) collective-permute-start(bf16[128,768]{1,0:T(8,128)(2,1)S(1)} %get-tuple-element.39), channel_id=1, source_target_pairs={{0,8},{1,17},{2,10},{3,19},{4,12},{5,21},{6,14},{7,23},{8,0},{9,25... | collective-permute-start | bytes 589832 | tf_op jit(solution)/shard_map/ppermute | solution.py:191
  113.7 19.2 %collective-permute-start.8 = (bf16[384,768]{1,0:T(8,128)(2,1)S(1)}, bf16[384,768]{1,0:T(8,128)(2,1)S(1)}, u32[]{:S(2)}, u32[]{:S(2)}) collective-permute-start(bf16[384,768]{1,0:T(8,128)(2,1)S(1)} %get-tuple-element.38), channel_id=1, source_target_pairs={{0,8},{1,17},{2,10},{3,19},{4,12},{5,21},{6,14},{7,23},{8,0},{9,25... | collective-permute-start | bytes 1769480 | tf_op jit(solution)/shard_map/ppermute | solution.py:191
  118.0 18.9 %collective-permute-start.18 = (bf16[128,1536]{1,0:T(8,128)(2,1)S(1)}, bf16[128,1536]{1,0:T(8,128)(2,1)S(1)}, u32[]{:S(2)}, u32[]{:S(2)}) collective-permute-start(bf16[128,1536]{1,0:T(8,128)(2,1)S(1)} %pad_maximum_fusion.5.near_ref.p0), channel_id=1, source_target_pairs={{0,16},{1,9},{2,18},{3,11},{4,20},{5,13},{6,22},{7,15},{8,24},{9,1... | collective-permute-start | bytes 1179656 | tf_op jit(solution)/shard_map/ppermute | solution.py:194
  119.7 36.1 %copy-start.16 = (bf16[384,1536]{1,0:T(8,128)(2,1)}, bf16[384,1536]{1,0:T(8,128)(2,1)S(1)}, u32[]{:S(2)}) copy-start(bf16[384,1536]{1,0:T(8,128)(2,1)S(1)} %pad_maximum_fusion.1.near_ref.p1) | copy-start | bytes 3538948
  119.7 51.4 %collective-permute-start.27 = (bf16[384,1536]{1,0:T(8,128)(2,1)S(1)}, bf16[384,1536]{1,0:T(8,128)(2,1)S(1)}, u32[]{:S(2)}, u32[]{:S(2)}) collective-permute-start(bf16[384,1536]{1,0:T(8,128)(2,1)S(1)} %pad_maximum_fusion.1.near_ref.p1), channel_id=1, source_target_pairs={{0,16},{1,9},{2,18},{3,11},{4,20},{5,13},{6,22},{7,15},{8,24},{9,1... | collective-permute-start | bytes 3538952 | tf_op jit(solution)/shard_map/ppermute | solution.py:194
  120.4 13.7 %copy-start.24 = (bf16[128,1536]{1,0:T(8,128)(2,1)}, bf16[128,1536]{1,0:T(8,128)(2,1)S(1)}, u32[]{:S(2)}) copy-start(bf16[128,1536]{1,0:T(8,128)(2,1)S(1)} %pad_maximum_fusion.6.near_ref.p0) | copy-start | bytes 1179652
  120.4 26.2 %collective-permute-start.36 = (bf16[128,1536]{1,0:T(8,128)(2,1)S(1)}, bf16[128,1536]{1,0:T(8,128)(2,1)}, u32[]{:S(2)}, u32[]{:S(2)}) collective-permute-start(bf16[128,1536]{1,0:T(8,128)(2,1)S(1)} %pad_maximum_fusion.6.near_ref.p0), channel_id=1, source_target_pairs={{0,16},{1,9},{2,18},{3,11},{4,20},{5,13},{6,22},{7,15},{8,24},{9,1... | collective-permute-start | bytes 1179656 | tf_op jit(solution)/shard_map/ppermute | solution.py:194
  134.1 47.5 %collective-permute-start.9 = (bf16[384,1536]{1,0:T(8,128)(2,1)}, bf16[384,1536]{1,0:T(8,128)(2,1)}, u32[]{:S(2)}, u32[]{:S(2)}) collective-permute-start(bf16[384,1536]{1,0:T(8,128)(2,1)} %pad_maximum_fusion.near_ref.p1), channel_id=1, source_target_pairs={{0,16},{1,9},{2,18},{3,11},{4,20},{5,13},{6,22},{7,15},{8,24},{9,1... | collective-permute-start | bytes 3538952 | tf_op jit(solution)/shard_map/ppermute | solution.py:194
  141.6 14.2 %copy-start.7 = (bf16[384,1536]{1,0:T(8,128)(2,1)S(1)}, bf16[384,1536]{1,0:T(8,128)(2,1)}, u32[]{:S(2)}) copy-start(bf16[384,1536]{1,0:T(8,128)(2,1)} %copy-done.5) | copy-start | bytes 3538948
  141.6 93.0 %collective-permute-start.19 = (bf16[64,1536]{1,0:T(8,128)(2,1)}, bf16[64,1536]{1,0:T(8,128)(2,1)}, u32[]{:S(2)}, u32[]{:S(2)}) collective-permute-start(bf16[64,1536]{1,0:T(8,128)(2,1)} %get-tuple-element.22), channel_id=1, source_target_pairs={{0,1},{1,0},{2,3},{3,2},{4,5},{5,4},{6,7},{7,6},{8,9},{9,8},{10,11... | collective-permute-start | bytes 589832 | tf_op jit(solution)/shard_map/ppermute | solution.py:197
  154.6 57.0 %collective-permute-start.37 = (bf16[64,1536]{1,0:T(8,128)(2,1)}, bf16[64,1536]{1,0:T(8,128)(2,1)}, u32[]{:S(2)}, u32[]{:S(2)}) collective-permute-start(bf16[64,1536]{1,0:T(8,128)(2,1)} %get-tuple-element.26), channel_id=1, source_target_pairs={{0,1},{1,0},{2,3},{3,2},{4,5},{5,4},{6,7},{7,6},{8,9},{9,8},{10,11... | collective-permute-start | bytes 589832 | tf_op jit(solution)/shard_map/ppermute | solution.py:197
  163.0 9.1 %copy-start.17 = (bf16[384,1536]{1,0:T(8,128)(2,1)S(1)}, bf16[384,1536]{1,0:T(8,128)(2,1)}, u32[]{:S(2)}) copy-start(bf16[384,1536]{1,0:T(8,128)(2,1)} %copy-done.16) | copy-start | bytes 3538948
  163.1 18.5 %slice-start.3 = ((s8[9437184]{0:T(1024)(128)(4,1)}), s8[1048576]{0:T(1024)(128)(4,1)S(1)}, s32[]{:S(2)}) async-start(s8[9437184]{0:T(1024)(128)(4,1)} %bitcast.22), calls=%async_computation.3 | async-start | bytes 2097152
  163.1 18.5 %slice-start.4 = ((s8[9437184]{0:T(1024)(128)(4,1)}), s8[4194304]{0:T(1024)(128)(4,1)S(1)}, s32[]{:S(2)}) async-start(s8[9437184]{0:T(1024)(128)(4,1)} %bitcast.22), calls=%async_computation.4 | async-start | bytes 8388608
  171.1 10.5 %slice-start.5 = ((s8[9437184]{0:T(1024)(128)(4,1)}), s8[4194304]{0:T(1024)(128)(4,1)S(1)}, s32[]{:S(2)}) async-start(s8[9437184]{0:T(1024)(128)(4,1)} %bitcast.22), calls=%async_computation.5 | async-start | bytes 8388608
  181.5 8.0 %copy-start.23 = (bf16[128,1536]{1,0:T(8,128)(2,1)S(1)}, bf16[128,1536]{1,0:T(8,128)(2,1)}, u32[]{:S(2)}) copy-start(bf16[128,1536]{1,0:T(8,128)(2,1)} %copy-done.22) | copy-start | bytes 1179652
  181.5 24.0 %collective-permute-start.28 = (bf16[192,1536]{1,0:T(8,128)(2,1)}, bf16[192,1536]{1,0:T(8,128)(2,1)S(1)}, u32[]{:S(2)}, u32[]{:S(2)}) collective-permute-start(bf16[192,1536]{1,0:T(8,128)(2,1)} %get-tuple-element.24), channel_id=1, source_target_pairs={{0,1},{1,0},{2,3},{3,2},{4,5},{5,4},{6,7},{7,6},{8,9},{9,8},{10,11... | collective-permute-start | bytes 1769480 | tf_op jit(solution)/shard_map/ppermute | solution.py:197
  189.0 22.3 %collective-permute-start.10 = (bf16[192,1536]{1,0:T(8,128)(2,1)S(1)}, bf16[192,1536]{1,0:T(8,128)(2,1)S(1)}, u32[]{:S(2)}, u32[]{:S(2)}) collective-permute-start(bf16[192,1536]{1,0:T(8,128)(2,1)S(1)} %get-tuple-element.20), channel_id=1, source_target_pairs={{0,1},{1,0},{2,3},{3,2},{4,5},{5,4},{6,7},{7,6},{8,9},{9,8},{10,11... | collective-permute-start | bytes 1769480 | tf_op jit(solution)/shard_map/ppermute | solution.py:197
  189.6 7.9 %copy-start.8 = (bf16[384,1536]{1,0:T(8,128)(2,1)S(1)}, bf16[384,1536]{1,0:T(8,128)(2,1)}, u32[]{:S(2)}) copy-start(bf16[384,1536]{1,0:T(8,128)(2,1)} %copy-done.5) | copy-start | bytes 3538948
  189.6 7.9 %copy-start.15 = (bf16[384,1536]{1,0:T(8,128)(2,1)S(1)}, bf16[384,1536]{1,0:T(8,128)(2,1)}, u32[]{:S(2)}) copy-start(bf16[384,1536]{1,0:T(8,128)(2,1)} %copy-done.13) | copy-start | bytes 3538948
  197.5 8.1 %copy-start.27 = (f32[192,1536]{1,0:T(8,128)S(1)}, f32[192,1536]{1,0:T(8,128)}, u32[]{:S(2)}) copy-start(f32[192,1536]{1,0:T(8,128)} %copy-done.26) | copy-start | bytes 3538948
  205.8 9.1 %collective-permute-start.31 = (bf16[64,1536]{1,0:T(8,128)(2,1)S(1)}, bf16[64,1536]{1,0:T(8,128)(2,1)S(1)}, u32[]{:S(2)}, u32[]{:S(2)}) collective-permute-start(bf16[64,1536]{1,0:T(8,128)(2,1)S(1)} %get-tuple-element.42), channel_id=1, source_target_pairs={{0,6},{1,7},{2,4},{3,5},{4,2},{5,3},{6,0},{7,1},{8,14},{9,15},{10,... | collective-permute-start | bytes 589832 | tf_op jit(solution)/shard_map/ppermute | solution.py:197
  208.3 18.8 %collective-permute-start.30 = (bf16[64,1536]{1,0:T(8,128)(2,1)S(1)}, bf16[64,1536]{1,0:T(8,128)(2,1)S(1)}, u32[]{:S(2)}, u32[]{:S(2)}) collective-permute-start(bf16[64,1536]{1,0:T(8,128)(2,1)S(1)} %get-tuple-element.43), channel_id=1, source_target_pairs={{0,4},{1,5},{2,6},{3,7},{4,0},{5,1},{6,2},{7,3},{8,12},{9,13},{10,... | collective-permute-start | bytes 589832 | tf_op jit(solution)/shard_map/ppermute | solution.py:197
  211.3 15.8 %collective-permute-start.29 = (bf16[64,1536]{1,0:T(8,128)(2,1)S(1)}, bf16[64,1536]{1,0:T(8,128)(2,1)S(1)}, u32[]{:S(2)}, u32[]{:S(2)}) collective-permute-start(bf16[64,1536]{1,0:T(8,128)(2,1)S(1)} %get-tuple-element.41), channel_id=1, source_target_pairs={{0,2},{1,3},{2,0},{3,1},{4,6},{5,7},{6,4},{7,5},{8,10},{9,11},{10,... | collective-permute-start | bytes 589832 | tf_op jit(solution)/shard_map/ppermute | solution.py:197
  211.4 15.7 %copy-start.31 = (f32[64,1536]{1,0:T(8,128)S(1)}, f32[64,1536]{1,0:T(8,128)}, u32[]{:S(2)}) copy-start(f32[64,1536]{1,0:T(8,128)} %copy-done.30) | copy-start | bytes 1179652
  211.4 15.7 %copy-start.32 = (bf16[64,1536]{1,0:T(8,128)(2,1)S(1)}, bf16[64,1536]{1,0:T(8,128)(2,1)}, u32[]{:S(2)}) copy-start(bf16[64,1536]{1,0:T(8,128)(2,1)} %param.7) | copy-start | bytes 589828
  211.4 15.7 %copy-start.33 = (f32[1536]{0:T(1024)S(1)}, f32[1536]{0:T(1024)}, u32[]{:S(2)}) copy-start(f32[1536]{0:T(1024)} %param.8) | copy-start | bytes 18436
  227.1 21.3 %copy-start.29 = (f32[64,1536]{1,0:T(8,128)S(1)}, f32[64,1536]{1,0:T(8,128)}, u32[]{:S(2)}) copy-start(f32[64,1536]{1,0:T(8,128)} %copy-done.28) | copy-start | bytes 1179652
  227.1 21.3 %copy-start.34 = (f32[1536]{0:T(1024)S(1)}, f32[1536]{0:T(1024)}, u32[]{:S(2)}) copy-start(f32[1536]{0:T(1024)} %param.12) | copy-start | bytes 18436
  228.5 6.0 %collective-permute-start.38 = (f32[2,64]{1,0:T(2,128)S(1)}, f32[2,64]{1,0:T(2,128)S(1)}, u32[]{:S(2)}, u32[]{:S(2)}) collective-permute-start(f32[2,64]{1,0:T(2,128)S(1)} %pad_maximum_fusion.8), channel_id=1, source_target_pairs={{0,8},{8,0},{16,24},{24,16},{1,9},{9,1},{17,25},{25,17},{2,10},{10... | collective-permute-start | bytes 1544 | tf_op jit(solution)/shard_map/ppermute | solution.py:200
  230.1 9.8 %collective-permute-start.13 = (bf16[64,1536]{1,0:T(8,128)(2,1)S(1)}, bf16[64,1536]{1,0:T(8,128)(2,1)S(1)}, u32[]{:S(2)}, u32[]{:S(2)}) collective-permute-start(bf16[64,1536]{1,0:T(8,128)(2,1)S(1)} %get-tuple-element.45), channel_id=1, source_target_pairs={{0,6},{1,7},{2,4},{3,5},{4,2},{5,3},{6,0},{7,1},{8,14},{9,15},{10,... | collective-permute-start | bytes 589832 | tf_op jit(solution)/shard_map/ppermute | solution.py:197
  232.6 15.8 %collective-permute-start.12 = (bf16[64,1536]{1,0:T(8,128)(2,1)S(1)}, bf16[64,1536]{1,0:T(8,128)(2,1)S(1)}, u32[]{:S(2)}, u32[]{:S(2)}) collective-permute-start(bf16[64,1536]{1,0:T(8,128)(2,1)S(1)} %get-tuple-element.46), channel_id=1, source_target_pairs={{0,4},{1,5},{2,6},{3,7},{4,0},{5,1},{6,2},{7,3},{8,12},{9,13},{10,... | collective-permute-start | bytes 589832 | tf_op jit(solution)/shard_map/ppermute | solution.py:197
  232.6 15.8 %collective-permute-start.11 = (bf16[64,1536]{1,0:T(8,128)(2,1)S(1)}, bf16[64,1536]{1,0:T(8,128)(2,1)S(1)}, u32[]{:S(2)}, u32[]{:S(2)}) collective-permute-start(bf16[64,1536]{1,0:T(8,128)(2,1)S(1)} %get-tuple-element.44), channel_id=1, source_target_pairs={{0,2},{1,3},{2,0},{3,1},{4,6},{5,7},{6,4},{7,5},{8,10},{9,11},{10,... | collective-permute-start | bytes 589832 | tf_op jit(solution)/shard_map/ppermute | solution.py:197
  234.5 15.7 %collective-permute-start.40 = (f32[1536]{0:T(1024)S(1)}, f32[1536]{0:T(1024)S(1)}, u32[]{:S(2)}, u32[]{:S(2)}) collective-permute-start(f32[1536]{0:T(1024)S(1)} %get-tuple-element.31), channel_id=1, source_target_pairs={{0,1},{1,0},{2,3},{3,2},{4,5},{5,4},{6,7},{7,6},{8,9},{9,8},{10,11... | collective-permute-start | bytes 18440 | tf_op jit(solution)/shard_map/ppermute | solution.py:197
  234.6 15.6 %collective-permute-start.39 = (f32[2,64]{1,0:T(2,128)S(1)}, f32[2,64]{1,0:T(2,128)S(1)}, u32[]{:S(2)}, u32[]{:S(2)}) collective-permute-start(f32[2,64]{1,0:T(2,128)S(1)} %fusion.36), channel_id=1, source_target_pairs={{0,16},{8,24},{16,0},{24,8},{1,17},{9,25},{17,1},{25,9},{2,18},{10... | collective-permute-start | bytes 1544 | tf_op jit(solution)/shard_map/ppermute | solution.py:200
  250.2 3.7 %collective-permute-start.41 = (f32[1536]{0:T(1024)S(1)}, f32[1536]{0:T(1024)S(1)}, u32[]{:S(2)}, u32[]{:S(2)}) collective-permute-start(f32[1536]{0:T(1024)S(1)} %add.277), channel_id=1, source_target_pairs={{0,2},{1,3},{2,0},{3,1},{4,6},{5,7},{6,4},{7,5},{8,10},{9,11},{10,... | collective-permute-start | bytes 18440 | tf_op jit(solution)/shard_map/ppermute | solution.py:197
  253.9 4.5 %collective-permute-start.42 = (f32[1536]{0:T(1024)S(1)}, f32[1536]{0:T(1024)S(1)}, u32[]{:S(2)}, u32[]{:S(2)}) collective-permute-start(f32[1536]{0:T(1024)S(1)} %add.278), channel_id=1, source_target_pairs={{0,4},{1,5},{2,6},{3,7},{4,0},{5,1},{6,2},{7,3},{8,12},{9,13},{10,... | collective-permute-start | bytes 18440 | tf_op jit(solution)/shard_map/ppermute | solution.py:197
  (20 other events, 66.7 us)

commit v2 on v0

v2 whole, which is shorter than its diff:
```python
import jax
import jax.numpy as jnp
from jax import lax
from jax.experimental import pallas as pl
from jax.experimental.pallas import tpu as pltpu
from jax.sharding import PartitionSpec as P

D = 6144

epsilon = 1e-06
inv_root_two = 0.7071067811865476
inv_root_two_pi = 0.3989422804014327

bf16 = jnp.bfloat16
f32 = jnp.float32
VMEM_LIMIT = 16 * 1024 * 1024

NN = (((1,), (0,)), ((), ()))
NT = (((1,), (1,)), ((), ()))
TN = (((0,), (0,)), ((), ()))


def mm(left, right, dims):
    return lax.dot_general(left, right, dims, preferred_element_type=f32)


def call(kernel, name, out_shape, in_specs, out_specs, flops, moved, scratch=(), aliases=None):
    return pl.pallas_call(
        kernel,
        name=name,
        out_shape=out_shape,
        in_specs=in_specs,
        out_specs=out_specs,
        scratch_shapes=scratch,
        input_output_aliases=aliases or {},
        compiler_params=pltpu.CompilerParams(vmem_limit_bytes=VMEM_LIMIT),
        cost_estimate=pl.CostEstimate(flops=0, bytes_accessed=0, transcendentals=0),
    )


IN_VMEM = pl.BlockSpec(memory_space=pltpu.VMEM)
IN_SMEM = pl.BlockSpec(memory_space=pltpu.SMEM)
IN_HBM = pl.BlockSpec(memory_space=pltpu.HBM)


def bits(n):
    return [1 << b for b in range(n.bit_length() - 1)]


def after(x, *others):
    return lax.optimization_barrier((x, *others))[0]


def block_at(me, rel, size):
    return pl.ds(pl.multiple_of((me ^ rel) * size, size), size)


def pieces_of(x_refs):
    return jnp.concatenate([x[...] for x in x_refs], axis=0)


def load_and_multiply(name, xs, w, me, shard, by_rows):
    rows, depth = sum(x.shape[0] for x in xs), xs[0].shape[1]

    def kernel(me_ref, *refs):
        x_refs, (w_ref, go_ref, keep_ref, all_ref, held_ref, sem) = refs[: len(xs)], refs[len(xs) :]

        def view(ref, r):
            at = block_at(me_ref[0], r, shard)
            return ref.at[at, :] if by_rows else ref.at[:, at]

        order, parts = (2, 3, 0, 1), 4
        copies = {}
        for r in order:
            for p in range(parts):
                source, target = view(w_ref, r), view(held_ref, r)
                span = pl.ds(p * (source.shape[0] // parts), source.shape[0] // parts)
                copies[r, p] = pltpu.make_async_copy(source.at[span, :], target.at[span, :], sem.at[r, p])
                copies[r, p].start()
        all_ref[...] = pieces_of(x_refs)
        for r, o_ref in zip(order, (go_ref, go_ref, keep_ref, keep_ref)):
            for p in range(parts):
                copies[r, p].wait()
            part = mm(all_ref[...], view(held_ref, r)[...], NT if by_rows else NN)
            o_ref[:, (r % 2) * shard : (r % 2 + 1) * shard] = part.astype(o_ref.dtype)

    return call(
        kernel,
        name,
        (
            jax.ShapeDtypeStruct((rows, 2 * shard), bf16),
            jax.ShapeDtypeStruct((rows, 2 * shard), f32),
            jax.ShapeDtypeStruct((rows, depth), bf16),
            pltpu.VMEM(w.shape, w.dtype),
        ),
        [IN_SMEM] + [IN_VMEM] * len(xs) + [IN_HBM],
        [IN_VMEM] * 4,
        8 * rows * depth * shard,
        2 * w.size,
        scratch=[pltpu.SemaphoreType.DMA((4, 4))],
    )(me, *xs, w)


def multiply(name, xs, w, me, shard, rels, dtype, by_rows):
    rows, depth = sum(x.shape[0] for x in xs), xs[0].shape[1]
    whole = len(xs) > 1

    def kernel(me_ref, *refs):
        x_refs, (w_ref, o_ref) = refs[: len(xs)], refs[len(xs) : len(xs) + 2]
        x_ref = x_refs[0]
        if whole:
            x_ref = refs[-1]
            x_ref[...] = pieces_of(x_refs)
        for j, r in enumerate(rels):
            at = block_at(me_ref[0], r, shard)
            block = w_ref[at, :] if by_rows else w_ref[:, at]
            o_ref[:, j * shard : (j + 1) * shard] = mm(x_ref[...], block, NT if by_rows else NN).astype(dtype)

    out_shape = [jax.ShapeDtypeStruct((rows, shard * len(rels)), dtype)]
    if whole:
        out_shape.append(jax.ShapeDtypeStruct((rows, depth), bf16))
    return call(
        kernel,
        name,
        out_shape,
        [IN_SMEM] + [IN_VMEM] * (len(xs) + 1),
        [IN_VMEM] * len(out_shape),
        2 * rows * depth * shard * len(rels),
        4 * rows * shard * len(rels),
    )(me, *xs, w)


def summed(near, far, w_ref, me, shard, cols, by_rows):
    total = None
    for r, ref, start in ((0, near, 0), (2, near, shard), (1, far, 0), (3, far, shard)):
        at = block_at(me, r, shard)
        block = w_ref[at, cols] if by_rows else w_ref[cols, at]
        term = mm(ref[:, start : start + shard], block, NN if by_rows else NT)
        total = term if total is None else total + term
    return total


def down_product(name, near, far, w_down, me):
    rows, wide = near.shape
    out = w_down.shape[1]
    half, shard, nb = rows // 2, wide // 2, 256

    def kernel(me_ref, near_ref, far_ref, w_ref, keep_ref, go_ref):
        for c in range(0, out, nb):
            cols = slice(c, c + nb)
            total = summed(near_ref, far_ref, w_ref, me_ref[0], shard, cols, True)
            keep_ref[:, cols] = total[:half]
            go_ref[:, cols] = total[half:].astype(bf16)

    return call(
        kernel,
        name,
        (jax.ShapeDtypeStruct((half, out), f32), jax.ShapeDtypeStruct((half, out), bf16)),
        [IN_SMEM] + [IN_VMEM] * 3,
        [IN_VMEM] * 2,
        4 * rows * wide * out,
        4 * rows * wide + 3 * rows * out,
    )(me, near, far, w_down)


def normed_grad(name, near, far, w_up, normed, me):
    rows, wide = near.shape
    out = w_up.shape[0]
    half, shard, nb = rows // 2, wide // 2, 256

    def kernel(me_ref, near_ref, far_ref, w_ref, n_ref, keep_ref, go_ref, gain_ref):
        for c in range(0, out, nb):
            cols = slice(c, c + nb)
            total = summed(near_ref, far_ref, w_ref, me_ref[0], shard, cols, False)
            keep_ref[:, cols] = total[:half]
            go_ref[:, cols] = total[half:].astype(bf16)
            gain_ref[:, cols] = jnp.sum(total * n_ref[:, cols].astype(f32), axis=0, keepdims=True)

    return call(
        kernel,
        name,
        (
            jax.ShapeDtypeStruct((half, out), f32),
            jax.ShapeDtypeStruct((half, out), bf16),
            jax.ShapeDtypeStruct((1, out), f32),
        ),
        [IN_SMEM] + [IN_VMEM] * 4,
        [IN_VMEM] * 3,
        4 * rows * wide * out,
        4 * rows * wide + 3 * rows * out,
    )(me, near, far, w_up, normed)


def stream_out(steps, compute, place, buf, sem):
    copies = []
    for i in range(steps):
        if i >= 2:
            copies[i - 2].wait()
        buf[i % 2] = compute(i)
        copies.append(pltpu.make_async_copy(buf.at[i % 2], place(i), sem.at[i % 2]))
        copies[i].start()
    for c in copies[-2:]:
        c.wait()


def weight_grad_down(name, pieces, cots, me, rels, shard, units, so_far):
    nb = shard // 2
    out = cots[0].shape[1]
    tokens = sum(c.shape[0] for c in cots)
    steps = 2 * len(rels)

    def kernel(me_ref, p0, p1, c0, c1, *refs):
        o_ref, buf, sem = refs[-3:]

        def compute(i):
            cols = slice(i * nb, (i + 1) * nb)
            return mm(p0[:, cols], c0[...], TN) + mm(p1[:, cols], c1[...], TN)

        def place(i):
            start = (me_ref[0] ^ rels[i // 2]) * shard + (i % 2) * nb
            return o_ref.at[pl.ds(pl.multiple_of(start, nb), nb), :]

        stream_out(steps, compute, place, buf, sem)

    rest = () if so_far is None else (so_far,)
    return call(
        kernel,
        name,
        jax.ShapeDtypeStruct((units, out), f32),
        [IN_SMEM] + [IN_VMEM] * 4 + [IN_HBM] * len(rest),
        IN_HBM,
        2 * tokens * nb * steps * out,
        4 * nb * steps * out,
        scratch=[pltpu.VMEM((2, nb, out), f32), pltpu.SemaphoreType.DMA((2,))],
        aliases={5: 0} if rest else None,
    )(me, *pieces, *cots, *rest)


def weight_grad_up(normed, nears, fars, me, units):
    out = normed[0].shape[1]
    tokens = sum(n.shape[0] for n in nears)
    shard = nears[0].shape[1] // 2
    nb = 256
    steps = out // nb

    def kernel(me_ref, n0, n1, near0, near1, far0, far1, o_ref, sum_ref, buf, sem):
        four = ((0, near0, near1, 0), (2, near0, near1, shard), (1, far0, far1, 0), (3, far0, far1, shard))
        for r, p0, p1, start in four:
            at = slice(start, start + shard)
            total = jnp.sum(p0[:, at].astype(f32), axis=0, keepdims=True)
            total += jnp.sum(p1[:, at].astype(f32), axis=0, keepdims=True)
            sum_ref[:, block_at(me_ref[0], r, shard)] = total

        copies = []
        for i in range(steps):
            if i >= 2:
                copies[i - 2].wait()
            rows = slice(i * nb, (i + 1) * nb)
            t0, t1 = n0[:, rows].T, n1[:, rows].T
            for r, p0, p1, start in four:
                at = slice(start, start + shard)
                term = mm(t0, p0[:, at], NN) + mm(t1, p1[:, at], NN)
                buf[i % 2, :, block_at(me_ref[0], r, shard)] = term
            copies.append(pltpu.make_async_copy(buf.at[i % 2], o_ref.at[rows, :], sem.at[i % 2]))
            copies[i].start()
        for c in copies[-2:]:
            c.wait()

    return call(
        kernel,
        "weight_grad_up",
        (jax.ShapeDtypeStruct((out, units), f32), jax.ShapeDtypeStruct((1, units), f32)),
        [IN_SMEM] + [IN_VMEM] * 6,
        [IN_HBM, IN_VMEM],
        2 * tokens * units * out,
        4 * units * out,
        scratch=[pltpu.VMEM((2, nb, units), f32), pltpu.SemaphoreType.DMA((2,))],
    )(me, *normed, *nears, *fars)


def solution(mesh):
    n_gx, n_gy = mesh.shape["gx"], mesh.shape["gy"]
    both = ("gx", "gy")
    chips = n_gy // 2

    def across(first):
        pairs = []
        for gx in range(n_gx):
            for gy in range(n_gy):
                flip = 1 if (gy % 2 == 0) == first else 2
                pairs.append((gx * n_gy + gy, (gx ^ flip) * n_gy + gy))
        return pairs

    first_pairs, second_pairs = across(True), across(False)

    def to_first(x):
        return lax.ppermute(x, both, first_pairs)

    def to_second(x):
        return lax.ppermute(x, both, second_pairs)

    def along_gy(x, m):
        return lax.ppermute(x, "gy", [(i, i ^ m) for i in range(n_gy)])

    def along_gx(x, m):
        return lax.ppermute(x, "gx", [(i, i ^ m) for i in range(n_gx)])

    def plane_sum(x):
        for step in bits(n_gx):
            x = x + along_gx(x, step)
        return x

    def over_groups(total):
        for step in bits(n_gx)[2:]:
            total = total + along_gx(total, step)
        return total

    def for_second(keep, came, shard):
        return (keep[:, shard:] + came[:, shard:].astype(f32)).astype(bf16)

    def plane_total(keep, came, back, shard):
        return over_groups(keep[:, :shard] + came[:, :shard].astype(f32) + back.astype(f32))

    def shards(patches, norm_gain, w_up, bias_up, w_down, bias_down, cotangent):
        rows = patches.shape[0]
        units = w_up.shape[1]
        shard = units // 4
        gx, gy = lax.axis_index("gx") % 4, lax.axis_index("gy")
        me = jnp.where(gy % 2 == 0, 2 * (gx % 2) + gx // 2, gx).astype(jnp.int32)
        bias = lax.dynamic_slice_in_dim(bias_up, me * shard, shard)
        me = me.reshape(1)

        w_up = pltpu.with_memory_space_constraint(w_up, pltpu.HBM)
        w_down = pltpu.with_memory_space_constraint(w_down, pltpu.HBM)

        def gather(own):
            z1 = along_gy(own, 2)
            w = [own, z1, along_gy(own, 1), along_gy(z1, 1)]
            even = [own]
            for step in bits(chips)[1:]:
                even += [along_gy(e, 2 * step) for e in even]
            even = even[1:]
            even += [along_gy(e, 2) for e in even]
            even = jnp.concatenate(even)
            return w, [even, along_gy(even, 1)]

        cot_w, cot_x = gather(cotangent)
        values = patches.astype(f32)
        totals = plane_sum(jnp.stack([jnp.sum(values, axis=1), jnp.sum(values * values, axis=1)]))
        go, keep_gw, cot_w, w_down = load_and_multiply("grad_act_w", cot_w, w_down, me, shard, True)
        came_gw = to_first(go)
        totals = after(totals, go)

        row_mean = (totals[0] / D)[:, None]
        variance = (totals[1] / D)[:, None] - row_mean * row_mean
        inv_std = lax.rsqrt(variance + epsilon)
        standard = (values - row_mean) * inv_std
        normed_w, normed_x = gather((standard * norm_gain).astype(bf16))
        back_gw = to_second(for_second(keep_gw, came_gw, shard))
        go, cot_x = multiply("grad_act_x_go", cot_x, w_down, me, shard, (2, 3), bf16, True)
        came_gx = to_first(go)
        keep_gx = multiply("grad_act_x_keep", [cot_x], w_down, me, shard, (0, 1), f32, True)[0]
        normed_w[0] = after(normed_w[0], keep_gx)
        go, keep_hw, normed_w, w_up = load_and_multiply("hidden_w", normed_w, w_up, me, shard, False)
        came_hw = to_first(go)
        back_hw = to_second(for_second(keep_hw, came_hw, shard))
        back_gx = to_second(for_second(keep_gx, came_gx, shard))

        def middle(grad_act, hidden):
            hidden = hidden + bias
            upper = 0.5 * (1.0 + lax.erf(hidden * inv_root_two))
            act = (hidden * upper).astype(bf16)
            slope = upper + hidden * jnp.exp(-0.5 * hidden * hidden) * inv_root_two_pi
            return act, (grad_act * slope).astype(bf16)

        go, normed_x = multiply("hidden_x_go", normed_x, w_up, me, shard, (2, 3), bf16, False)
        came_hx = to_first(go)
        act_w, grad_w = middle(
            plane_total(keep_gw, came_gw, back_gw, shard), plane_total(keep_hw, came_hw, back_hw, shard)
        )
        keep_hx = multiply(
            "hidden_x_keep", [after(normed_x, act_w, grad_w)], w_up, me, shard, (0, 1), f32, False
        )[0]
        grad_near_w = jnp.concatenate([grad_w, to_first(grad_w)], axis=1)
        near_w = jnp.concatenate([act_w, to_first(act_w)], axis=1)
        back_hx = to_second(for_second(keep_hx, came_hx, shard))
        grad_far_w = to_second(grad_near_w)
        far_w = to_second(near_w)
        act_x, grad_x = middle(
            plane_total(keep_gx, after(came_gx, near_w, grad_near_w), back_gx, shard),
            plane_total(keep_hx, came_hx, back_hx, shard),
        )
        grad_near_x = jnp.concatenate([grad_x, to_first(grad_x)], axis=1)
        near_x = jnp.concatenate([act_x, to_first(act_x)], axis=1)
        grad_far_x = to_second(grad_near_x)
        far_x = to_second(near_x)

        def pair_sum(keep, go):
            return keep + along_gy(go, 1).astype(f32)

        def from_neighbour(sums):
            half = chips // 2 - 1
            sums = sums[: half * rows] + along_gy(sums[half * rows :].astype(bf16), 2).astype(f32)
            return [sums[i * rows : (i + 1) * rows] for i in range(half)]

        def from_far(held):
            held = [0.0] + held
            for step in reversed(bits(chips)[1:]):
                size = len(held) // 2
                came = [along_gy(h.astype(bf16), 2 * step).astype(f32) for h in held[size:]]
                held = [h + c for h, c in zip(held[:size], came)]
            return held[0]

        def at_home(sums):
            return sums[:rows] + along_gy(sums[rows:].astype(bf16), 2).astype(f32)

        keep, go, gain_w = normed_grad("normed_grad_w", grad_near_w, grad_far_w, w_up, normed_w, me)
        grad_sums_w = pair_sum(keep, go)
        keep, go = down_product("mlp_w", near_w, after(far_w, go), w_down, me)
        sums_w = pair_sum(keep, go)
        cot_w = after(cot_w, grad_sums_w, sums_w)
        down = weight_grad_down("wgrad_near", (near_w, near_x), (cot_w, cot_x), me, (0, 2), shard, units, None)
        keep, go, gain_x = normed_grad("normed_grad_x", grad_near_x, after(grad_far_x, down), w_up, normed_x, me)
        grad_sums_x = pair_sum(keep, go)
        keep, go = down_product("mlp_x", near_x, after(far_x, grad_sums_x), w_down, me)
        sums_x = pair_sum(keep, go)
        far_w = after(far_w, sums_x)
        grad_w_down = weight_grad_down("wgrad_far", (far_w, far_x), (cot_w, cot_x), me, (1, 3), shard, units, down)
        grad_held, held = from_neighbour(grad_sums_x), from_neighbour(sums_x)
        grad_w_up, grad_bias_up = weight_grad_up(
            (after(normed_w, grad_w_down, *grad_held, *held), normed_x),
            (grad_near_w, grad_near_x),
            (grad_far_w, grad_far_x),
            me,
            units,
        )
        grad_normed = at_home(grad_sums_w) + from_far(grad_held)
        mlp_out = (at_home(sums_w) + from_far(held) + bias_down).astype(bf16)
        grad_gain = (gain_w + gain_x)[0] / norm_gain
        for step in bits(n_gy):
            grad_gain = grad_gain + along_gy(grad_gain, step)

        grad_bias_down = jnp.sum(cot_w.astype(f32), axis=0) + jnp.sum(cot_x.astype(f32), axis=0)

        scaled = grad_normed * norm_gain
        sums = plane_sum(jnp.stack([jnp.sum(scaled, axis=1), jnp.sum(scaled * standard, axis=1)]))
        first_mean = (sums[0] / D)[:, None]
        second_mean = (sums[1] / D)[:, None]
        grad_patches = (inv_std * (scaled - first_mean - standard * second_mean)).astype(bf16)
        return mlp_out, grad_patches, grad_gain, grad_w_up, grad_bias_up[0], grad_w_down, grad_bias_down

    in_specs = (
        P("gy", "gx"),
        P("gx"),
        P("gx", "gy"),
        P("gy"),
        P("gy", "gx"),
        P("gx"),
        P("gy", "gx"),
    )
    out_specs = (
        P("gy", "gx"),
        P("gy", "gx"),
        P("gx"),
        P("gx", "gy"),
        P("gy"),
        P("gy", "gx"),
        P("gx"),
    )
    return jax.shard_map(shards, mesh=mesh, in_specs=in_specs, out_specs=out_specs, check_vma=False)
```

time: 432 us -> 184 us (0.43)
  waiting for transfers between devices: 292 us -> 60 us
  matrix products: 59.1 us -> 0 us
  Pallas kernels: 0 us -> 50.3 us
  blocking collectives: 48.8 us -> 0 us
  starting transfers between devices: 0.38 us -> 47.1 us
  between operations: 13.8 us -> 1.17 us
  local copies, waits for them, and re-layouts: 1.69 us -> 10.5 us
    psum x1 -> x0, waiting for transfers between devices: 240 us -> none  [shards(): hidden = lax.psum(partial_value, 'gx') + bias_up]
    ppermute x0 -> x45, waiting for transfers between devices: none -> 60 us  [the longest x25 23.9 us: along_gy(): return lax.ppermute(x, 'gy', [(i, i ^ m) for i in range(n_gy)])]
    dot_general x6 -> x0, matrix products: 59.1 us -> none  [the longest x2 21 us: over_rows(): lax.dot_general(left, right, (((0,), (0,)), ((), ())), preferred_element_...]
    pallas_call x0 -> x13, Pallas kernels: none -> 50.3 us  [the longest x2 11.6 us: load_and_multiply(): call(kernel, name, (jax.ShapeDtypeStruct((rows, 2 * shard), bf16), jax.Sh...]
    psum x3 -> x0, blocking collectives: 48.8 us -> none  [the longest x1 27.6 us: shards(): lax.psum((jnp.sum(grad_normed * standard, axis=0), jnp.sum(cotangent, axi...]
    ppermute x0 -> x45, starting transfers between devices: none -> 47.1 us  [the longest x25 22.2 us: along_gy(): return lax.ppermute(x, 'gy', [(i, i ^ m) for i in range(n_gy)])]
    all_gather x2 -> x0, waiting for transfers between devices: 40.3 us -> none  [the longest x1 23.8 us: shards(): lax.all_gather(normed, 'gy', axis=0, tiled=True)]
    reduce_scatter x2 -> x0, waiting for transfers between devices: 11.5 us -> none  [the longest x1 9.84 us: shards(): lax.psum_scatter(over_cols(block, w_up), 'gy', scatter_dimension=0, tiled...]
  transfers between devices with their start and end apart: 5 -> 45, of which waited for: 5 -> 19; matrix products, arithmetic and copies ran while one was open for 10% -> 8% of each run, Pallas kernels for 0% -> 26%
where the time goes in v2:
time: 184 us
  waiting for transfers between devices  60 us (33%)
  Pallas kernels  50.3 us (27%)
  starting transfers between devices  47.1 us (26%)
  other arithmetic  14.4 us (8%)
  local copies, waits for them, and re-layouts  10.5 us (6%)
    ppermute x25, waiting for transfers between devices, along_gy(): return lax.ppermute(x, 'gy', [(i, i ^ m) for i in range(n_gy)])  23.9 us
    ppermute x25, starting transfers between devices, along_gy(): return lax.ppermute(x, 'gy', [(i, i ^ m) for i in range(n_gy)])  22.2 us
    ppermute x8, waiting for transfers between devices, to_second(): return lax.ppermute(x, both, second_pairs)  16.9 us
    ppermute x8, waiting for transfers between devices, to_first(): return lax.ppermute(x, both, first_pairs)  14.4 us
    pallas_call x2, Pallas kernels, load_and_multiply(): call(kernel, name, (jax.ShapeDtypeStruct((rows, 2 * shard), bf16), jax.Sh...  11.6 us
    pallas_call x2, Pallas kernels, weight_grad_down(): call(kernel, name, jax.ShapeDtypeStruct((units, out), f32), [IN_SMEM] + [...  10.5 us
    ppermute x8, starting transfers between devices, to_first(): return lax.ppermute(x, both, first_pairs)  9.84 us
    pallas_call x1, Pallas kernels, weight_grad_up(): call(kernel, 'weight_grad_up', (jax.ShapeDtypeStruct((out, units), f32),...  9.72 us
  transfers between devices with their start and end apart: 45, of which 19 were waited for; matrix products, arithmetic and copies ran while one was open for 8% of the time, Pallas kernels for 26%

profile of v2, /device:TPU:0, one launch (start us, length us, event | category | flops | bytes accessed | tf_op | source)
XLA Modules:
  0.0 183.5 jit_solution(9893763325783898828)
XLA Ops:
  0.6 3.1 %collective-permute-start.2 = (bf16[64,1536]{1,0:T(8,128)(2,1)}, bf16[64,1536]{1,0:T(8,128)(2,1)S(1)}, u32[]{:S(2)}, u32[]{:S(2)}) collective-permute-start(bf16[64,1536]{1,0:T(8,128)(2,1)} %refs_0_.1), channel_id=1, source_target_pairs={{0,2},{1,3},{2,0},{3,1},{4,6},{5,7},{6,4},{7,5},{8,10},{9,11},{10,... | collective-permute-start | bytes 589832 | tf_op jit(solution)/shard_map/ppermute | solution.py:303
  3.7 2.6 %collective-permute-start.5 = (bf16[64,1536]{1,0:T(8,128)(2,1)}, bf16[64,1536]{1,0:T(8,128)(2,1)S(1)}, u32[]{:S(2)}, u32[]{:S(2)}) collective-permute-start(bf16[64,1536]{1,0:T(8,128)(2,1)} %refs_0_.1), channel_id=1, source_target_pairs={{0,4},{1,5},{2,6},{3,7},{4,0},{5,1},{6,2},{7,3},{8,12},{9,13},{10,... | collective-permute-start | bytes 589832 | tf_op jit(solution)/shard_map/ppermute | solution.py:303
  6.3 1.1 convert_reduce_fusion.2
  7.4 1.6 collective-permute-start
  9.0 2.1 %collective-permute-done = f32[2,64]{1,0:T(2,128)S(1)} collective-permute-done((f32[2,64]{1,0:T(2,128)S(1)}, f32[2,64]{1,0:T(2,128)S(1)}, u32[]{:S(2)}, u32[]{:S(2)}) %collective-permute-start) | collective-permute-done | bytes 544 | tf_op jit(solution)/shard_map/ppermute | solution.py:306
  11.1 1.6 collective-permute-start.1
  12.6 2.0 %collective-permute-done.1 = f32[2,64]{1,0:T(2,128)S(1)} collective-permute-done((f32[2,64]{1,0:T(2,128)S(1)}, f32[2,64]{1,0:T(2,128)S(1)}, u32[]{:S(2)}, u32[]{:S(2)}) %collective-permute-start.1) | collective-permute-done | bytes 544 | tf_op jit(solution)/shard_map/ppermute | solution.py:306
  14.8 1.6 collective-permute-done.5
  16.5 0.9 copy-done.8
  17.4 5.8 %grad_act_w.1 = (bf16[256,1536]{1,0:T(8,128)(2,1)S(1)}, f32[256,1536]{1,0:T(8,128)S(1)}, bf16[256,1536]{1,0:T(8,128)(2,1)S(1)}, bf16[3072,1536]{1,0:T(8,128)(2,1)S(1)}) custom-call(s32[1]{0:T(128)} %bitcast.me_ref, bf16[64,1536]{1,0:T(8,128)(2,1)S(1)} %copy-done.8, bf16[64,1536]{1,0:T(8,128)(2,1)S(1)} %collective-permute-done.2.refs_1_, ...), custom_call_target="tpu_custom_call" | custom-call | tf_op jit(solution)/shard_map/grad_act_w/pallas_call | solution.py:87
  23.6 2.1 %collective-permute-start.8 = (bf16[64,1536]{1,0:T(8,128)(2,1)S(1)}, bf16[64,1536]{1,0:T(8,128)(2,1)S(1)}, u32[]{:S(2)}, u32[]{:S(2)}) collective-permute-start(bf16[64,1536]{1,0:T(8,128)(2,1)S(1)} %fusion.22.refs_0_), channel_id=1, source_target_pairs={{0,2},{1,3},{2,0},{3,1},{4,6},{5,7},{6,4},{7,5},{8,10},{9,11},{10,... | collective-permute-start | bytes 589832 | tf_op jit(solution)/shard_map/ppermute | solution.py:303
  25.6 1.5 collective-permute-start.15
  27.1 4.1 %collective-permute-done.8.refs_1_ = bf16[64,1536]{1,0:T(8,128)(2,1)S(1)} collective-permute-done((bf16[64,1536]{1,0:T(8,128)(2,1)S(1)}, bf16[64,1536]{1,0:T(8,128)(2,1)S(1)}, u32[]{:S(2)}, u32[]{:S(2)}) %collective-permute-start.8) | collective-permute-done | bytes 196640 | tf_op jit(solution)/shard_map/ppermute | solution.py:303
  31.2 2.8 %collective-permute-start.21 = (bf16[64,1536]{1,0:T(8,128)(2,1)S(1)}, bf16[64,1536]{1,0:T(8,128)(2,1)S(1)}, u32[]{:S(2)}, u32[]{:S(2)}) collective-permute-start(bf16[64,1536]{1,0:T(8,128)(2,1)S(1)} %fusion.22.refs_0_), channel_id=1, source_target_pairs={{0,4},{1,5},{2,6},{3,7},{4,0},{5,1},{6,2},{7,3},{8,12},{9,13},{10,... | collective-permute-start | bytes 589832 | tf_op jit(solution)/shard_map/ppermute | solution.py:303
  34.0 2.3 %grad_act_x_go.1 = (bf16[256,1536]{1,0:T(8,128)(2,1)}, bf16[256,1536]{1,0:T(8,128)(2,1)S(1)}) custom-call(s32[1]{0:T(128)} %bitcast.me_ref, bf16[128,1536]{1,0:T(8,128)(2,1)S(1)} %constant_dynamic-update-slice_fusion.refs_0_, bf16[128,1536]{1,0:T(8,128)(2,1)S(1)} %collective-permute-done.7.refs_1_, bf16[3072,1536]{1,0:T(8,128)(2,1)S(1)} %get-tuple-element.43.refs_2_.refs_1_.w_ref), custom_call_target="tpu_custom_call" | custom-call | tf_op jit(solution)/shard_map/grad_act_x_go/pallas_call | solution.py:122
  36.3 1.4 grad_act_x_keep.1
  37.7 1.2 copy-done.4
  38.9 5.8 %hidden_w.1 = (bf16[256,1536]{1,0:T(8,128)(2,1)S(1)}, f32[256,1536]{1,0:T(8,128)S(1)}, bf16[256,1536]{1,0:T(8,128)(2,1)S(1)}, bf16[1536,3072]{1,0:T(8,128)(2,1)S(1)}) custom-call(s32[1]{0:T(128)} %bitcast.me_ref, bf16[64,1536]{1,0:T(8,128)(2,1)S(1)} %fusion.22.refs_0_, bf16[64,1536]{1,0:T(8,128)(2,1)S(1)} %collective-permute-done.8.refs_1_, ...), custom_call_target="tpu_custom_call" | custom-call | tf_op jit(solution)/shard_map/hidden_w/pallas_call | solution.py:87
  44.6 1.6 collective-permute-start.11
  46.5 6.5 %collective-permute-done.22 = bf16[64,1536]{1,0:T(8,128)(2,1)S(1)} collective-permute-done((bf16[64,1536]{1,0:T(8,128)(2,1)S(1)}, bf16[64,1536]{1,0:T(8,128)(2,1)S(1)}, u32[]{:S(2)}, u32[]{:S(2)}) %collective-permute-start.22) | collective-permute-done | bytes 196640 | tf_op jit(solution)/shard_map/ppermute | solution.py:303
  53.1 1.5 collective-permute-start.28
  54.6 1.0 add_convert_fusion
  56.7 1.0 add_convert_fusion.1
  57.7 1.5 collective-permute-start.12
  59.2 2.4 %hidden_x_go.1 = (bf16[256,1536]{1,0:T(8,128)(2,1)}, bf16[256,1536]{1,0:T(8,128)(2,1)S(1)}) custom-call(s32[1]{0:T(128)} %bitcast.me_ref, bf16[128,1536]{1,0:T(8,128)(2,1)S(1)} %constant_dynamic-update-slice_fusion.2.refs_0_, bf16[128,1536]{1,0:T(8,128)(2,1)S(1)} %collective-permute-done.23.refs_1_, ...), custom_call_target="tpu_custom_call" | custom-call | tf_op jit(solution)/shard_map/hidden_x_go/pallas_call | solution.py:122
  61.6 3.7 %copy-done.1 = bf16[1536,3072]{1,0:T(8,128)(2,1)} copy-done((bf16[1536,3072]{1,0:T(8,128)(2,1)}, bf16[1536,3072]{1,0:T(8,128)(2,1)S(1)}, u32[]{:S(2)}) %copy-start.1) | copy-done | bytes 9437208
  65.3 1.5 collective-permute-start.24
  68.0 8.4 %collective-permute-done.12 = bf16[256,768]{1,0:T(8,128)(2,1)} collective-permute-done((bf16[256,768]{1,0:T(8,128)(2,1)}, bf16[256,768]{1,0:T(8,128)(2,1)}, u32[]{:S(2)}, u32[]{:S(2)}) %collective-permute-start.12) | collective-permute-done | bytes 393248 | tf_op jit(solution)/shard_map/ppermute | solution.py:300
  76.4 2.4 %fusion.5 = (bf16[256,768]{1,0:T(8,128)(2,1)S(1)}, bf16[256,768]{1,0:T(8,128)(2,1)S(1)}) fusion(bf16[256,768]{1,0:T(8,128)(2,1)} %collective-permute-done.16, f32[256,1536]{1,0:T(8,128)} %copy-done.6, bf16[256,1536]{1,0:T(8,128)(2,1)} %copy-done.10, f32[768]{0:T(1024)S(1)} %dynamic_slice.3, bf16[256,768]{1,0:T(8,128)(2,1)} %collective-permute-done.12, ...), kind=kLoop, calls=%fused_computation.9 | loop fusion | flops 4128768 | bytes 3935232 | tf_op jit(solution)/shard_map/convert_element_type | solution.py:374
  79.4 1.1 fusion.12
  81.2 1.5 collective-permute-start.13
  82.6 3.7 %copy-done.2 = bf16[1536,3072]{1,0:T(8,128)(2,1)S(1)} copy-done((bf16[1536,3072]{1,0:T(8,128)(2,1)S(1)}, bf16[1536,3072]{1,0:T(8,128)(2,1)}, u32[]{:S(2)}) %copy-start.2) | copy-done | bytes 9437208
  86.3 1.6 hidden_x_keep.1
  87.9 1.8 fusion.14
  89.7 1.6 collective-permute-start.25
  92.0 6.9 %collective-permute-done.13 = bf16[256,768]{1,0:T(8,128)(2,1)S(1)} collective-permute-done((bf16[256,768]{1,0:T(8,128)(2,1)S(1)}, bf16[256,768]{1,0:T(8,128)(2,1)S(1)}, u32[]{:S(2)}, u32[]{:S(2)}) %collective-permute-start.13) | collective-permute-done | bytes 393248 | tf_op jit(solution)/shard_map/ppermute | solution.py:297
  99.0 1.9 %fusion.11 = (bf16[256,768]{1,0:T(8,128)(2,1)S(1)}, bf16[256,768]{1,0:T(8,128)(2,1)S(1)}) fusion(f32[256,1536]{1,0:T(8,128)S(1)} %copy-done.5, bf16[256,768]{1,0:T(8,128)(2,1)S(1)} %collective-permute-done.29, bf16[256,1536]{1,0:T(8,128)(2,1)} %collective-permute-done.28, f32[768]{0:T(1024)S(1)} %dynamic_slice.3, ...), kind=kLoop, calls=%fused_computation.15 | loop fusion | flops 4128768 | bytes 3935232 | tf_op jit(solution)/shard_map/convert_element_type | solution.py:374
  100.9 1.6 collective-permute-start.30
  102.5 1.9 %collective-permute-start.14 = (bf16[256,1536]{1,0:T(8,128)(2,1)S(1)}, bf16[256,1536]{1,0:T(8,128)(2,1)S(1)}, u32[]{:S(2)}, u32[]{:S(2)}) collective-permute-start(bf16[256,1536]{1,0:T(8,128)(2,1)S(1)} %pad_maximum_fusion.near_ref.p0), channel_id=1, source_target_pairs={{0,16},{1,9},{2,18},{3,11},{4,20},{5,13},{6,22},{7,15},{8,24},{9,1... | collective-permute-start | bytes 2359304 | tf_op jit(solution)/shard_map/ppermute | solution.py:300
  104.4 5.8 %collective-permute-done.18.far_ref.far0 = bf16[256,1536]{1,0:T(8,128)(2,1)S(1)} collective-permute-done((bf16[256,1536]{1,0:T(8,128)(2,1)S(1)}, bf16[256,1536]{1,0:T(8,128)(2,1)S(1)}, u32[]{:S(2)}, u32[]{:S(2)}) %collective-permute-start.18) | collective-permute-done | bytes 786464 | tf_op jit(solution)/shard_map/ppermute | solution.py:300
  110.3 2.7 %normed_grad_w.1 = (f32[128,1536]{1,0:T(8,128)S(1)}, bf16[128,1536]{1,0:T(8,128)(2,1)S(1)}, f32[1,1536]{1,0:T(1,128)S(1)}) custom-call(s32[1]{0:T(128)} %bitcast.me_ref, bf16[256,1536]{1,0:T(8,128)(2,1)S(1)} %pad_maximum_fusion.1.near_ref.near0, bf16[256,1536]{1,0:T(8,128)(2,1)S(1)} %collective-permute-done.18.far_ref.far0, ...), custom_call_target="tpu_custom_call" | custom-call | tf_op jit(solution)/shard_map/normed_grad_w/pallas_call | solution.py:179
  113.3 1.2 collective-permute-start.31
  114.6 6.9 %collective-permute-done.26 = bf16[256,768]{1,0:T(8,128)(2,1)S(1)} collective-permute-done((bf16[256,768]{1,0:T(8,128)(2,1)S(1)}, bf16[256,768]{1,0:T(8,128)(2,1)S(1)}, u32[]{:S(2)}, u32[]{:S(2)}) %collective-permute-start.26) | collective-permute-done | bytes 393248 | tf_op jit(solution)/shard_map/ppermute | solution.py:297
  121.5 2.3 %collective-permute-done.14.far_ref.p0 = bf16[256,1536]{1,0:T(8,128)(2,1)S(1)} collective-permute-done((bf16[256,1536]{1,0:T(8,128)(2,1)S(1)}, bf16[256,1536]{1,0:T(8,128)(2,1)S(1)}, u32[]{:S(2)}, u32[]{:S(2)}) %collective-permute-start.14) | collective-permute-done | bytes 786464 | tf_op jit(solution)/shard_map/ppermute | solution.py:300
  123.8 2.6 %mlp_w.1 = (f32[128,1536]{1,0:T(8,128)S(1)}, bf16[128,1536]{1,0:T(8,128)(2,1)S(1)}) custom-call(s32[1]{0:T(128)} %bitcast.me_ref, bf16[256,1536]{1,0:T(8,128)(2,1)S(1)} %pad_maximum_fusion.near_ref.p0, bf16[256,1536]{1,0:T(8,128)(2,1)S(1)} %collective-permute-done.14.far_ref.p0, bf16[3072,1536]{1,0:T(8,128)(2,1)S(1)} %bitcast.21), custom_call_target="tpu_custom_call" | custom-call | tf_op jit(solution)/shard_map/mlp_w/pallas_call | solution.py:155
  127.3 1.3 collective-permute-done.19
  128.6 5.3 %wgrad_near.1.refs_0_ = f32[3072,1536]{1,0:T(8,128)} custom-call(s32[1]{0:T(128)} %bitcast.me_ref, bf16[256,1536]{1,0:T(8,128)(2,1)S(1)} %pad_maximum_fusion.near_ref.p0, bf16[256,1536]{1,0:T(8,128)(2,1)S(1)} %pad_maximum_fusion.2.p1.near_ref, bf16[256,1536]{1,0:T(8,128)(2,1)S(1)} %get-tuple-element.62.c0, bf16[256,1536]{1,0:T(8,128)(2,1)S(1)} %get-tuple-element.44.refs_0_.c1), custom_call_target="tpu_custom_call" | custom-call | tf_op jit(solution)/shard_map/wgrad_near/pallas_call | solution.py:226
  133.9 2.7 %normed_grad_x.1 = (f32[128,1536]{1,0:T(8,128)S(1)}, bf16[128,1536]{1,0:T(8,128)(2,1)S(1)}, f32[1,1536]{1,0:T(1,128)S(1)}) custom-call(s32[1]{0:T(128)} %bitcast.me_ref, bf16[256,1536]{1,0:T(8,128)(2,1)S(1)} %pad_maximum_fusion.3.near_ref.near1, bf16[256,1536]{1,0:T(8,128)(2,1)S(1)} %collective-permute-done.31.far_ref.far1, ...), custom_call_target="tpu_custom_call" | custom-call | tf_op jit(solution)/shard_map/normed_grad_x/pallas_call | solution.py:179
  137.0 1.3 collective-permute-done.33
  138.9 1.3 collective-permute-start.27
  140.2 1.8 collective-permute-start.37
  142.0 4.3 %collective-permute-done.38 = bf16[64,1536]{1,0:T(8,128)(2,1)S(1)} collective-permute-done((bf16[64,1536]{1,0:T(8,128)(2,1)S(1)}, bf16[64,1536]{1,0:T(8,128)(2,1)S(1)}, u32[]{:S(2)}, u32[]{:S(2)}) %collective-permute-start.38) | collective-permute-done | bytes 196640 | tf_op jit(solution)/shard_map/ppermute | solution.py:303
  146.8 1.2 collective-permute-done.42
  148.0 1.6 collective-permute-start.43
  149.8 2.5 %collective-permute-done.43 = f32[1536]{0:T(1024)S(1)} collective-permute-done((f32[1536]{0:T(1024)S(1)}, f32[1536]{0:T(1024)S(1)}, u32[]{:S(2)}, u32[]{:S(2)}) %collective-permute-start.43) | collective-permute-done | bytes 6176 | tf_op jit(solution)/shard_map/ppermute | solution.py:303
  152.2 2.5 %collective-permute-start.44 = (f32[1536]{0:T(1024)S(1)}, f32[1536]{0:T(1024)S(1)}, u32[]{:S(2)}, u32[]{:S(2)}) collective-permute-start(f32[1536]{0:T(1024)S(1)} %add.199), channel_id=1, source_target_pairs={{0,4},{1,5},{2,6},{3,7},{4,0},{5,1},{6,2},{7,3},{8,12},{9,13},{10,... | collective-permute-start | bytes 18440 | tf_op jit(solution)/shard_map/ppermute | solution.py:303
  154.7 2.8 %mlp_x.1 = (f32[128,1536]{1,0:T(8,128)S(1)}, bf16[128,1536]{1,0:T(8,128)(2,1)S(1)}) custom-call(s32[1]{0:T(128)} %bitcast.me_ref, bf16[256,1536]{1,0:T(8,128)(2,1)S(1)} %pad_maximum_fusion.2.p1.near_ref, bf16[256,1536]{1,0:T(8,128)(2,1)S(1)} %collective-permute-done.27.far_ref.p1, bf16[3072,1536]{1,0:T(8,128)(2,1)S(1)} %bitcast.21), custom_call_target="tpu_custom_call" | custom-call | tf_op jit(solution)/shard_map/mlp_x/pallas_call | solution.py:155
  157.9 1.4 collective-permute-start.40
  161.5 1.2 collective-permute-start.41
  162.9 1.4 collective-permute-start.35
  164.3 5.3 %wgrad_far.1 = f32[3072,1536]{1,0:T(8,128)} custom-call(s32[1]{0:T(128)} %bitcast.me_ref, bf16[256,1536]{1,0:T(8,128)(2,1)S(1)} %collective-permute-done.14.far_ref.p0, bf16[256,1536]{1,0:T(8,128)(2,1)S(1)} %collective-permute-done.27.far_ref.p1, bf16[256,1536]{1,0:T(8,128)(2,1)S(1)} %get-tuple-element.62.c0, ...), custom_call_target="tpu_custom_call", output_to_operand_aliasing={{}: (5, {})} | custom-call | tf_op jit(solution)/shard_map/wgrad_far/pallas_call | solution.py:226
  169.6 1.2 collective-permute-done.35
  170.8 1.3 collective-permute-start.36
  173.0 9.7 %weight_grad_up.1 = (f32[1536,3072]{1,0:T(8,128)}, f32[1,3072]{1,0:T(1,128)}) custom-call(s32[1]{0:T(128)} %bitcast.me_ref, bf16[256,1536]{1,0:T(8,128)(2,1)S(1)} %get-tuple-element.72.n_ref.n0, bf16[256,1536]{1,0:T(8,128)(2,1)S(1)} %get-tuple-element.56.refs_0_.n_ref.n1, bf16[256,1536]{1,0:T(8,128)(2,1)S(1)} %pad_maximum_fusion.1.near_ref.near0, ...), custom_call_target="tpu_custom_call" | custom-call | tf_op jit(solution)/shard_map/weight_grad_up/pallas_call | solution.py:269
  (121 shorter events, 12.4 us)
Async XLA Ops:
  0.6 14.1 %collective-permute-start.2 = (bf16[64,1536]{1,0:T(8,128)(2,1)}, bf16[64,1536]{1,0:T(8,128)(2,1)S(1)}, u32[]{:S(2)}, u32[]{:S(2)}) collective-permute-start(bf16[64,1536]{1,0:T(8,128)(2,1)} %refs_0_.1), channel_id=1, source_target_pairs={{0,2},{1,3},{2,0},{3,1},{4,6},{5,7},{6,4},{7,5},{8,10},{9,11},{10,... | collective-permute-start | bytes 589832 | tf_op jit(solution)/shard_map/ppermute | solution.py:303
  3.7 12.7 %collective-permute-start.3 = (bf16[64,1536]{1,0:T(8,128)(2,1)}, bf16[64,1536]{1,0:T(8,128)(2,1)S(1)}, u32[]{:S(2)}, u32[]{:S(2)}) collective-permute-start(bf16[64,1536]{1,0:T(8,128)(2,1)} %refs_0_.1), channel_id=1, source_target_pairs={{0,1},{1,0},{2,3},{3,2},{4,5},{5,4},{6,7},{7,6},{8,9},{9,8},{10,11... | collective-permute-start | bytes 589832 | tf_op jit(solution)/shard_map/ppermute | solution.py:303
  3.7 12.7 %collective-permute-start.5 = (bf16[64,1536]{1,0:T(8,128)(2,1)}, bf16[64,1536]{1,0:T(8,128)(2,1)S(1)}, u32[]{:S(2)}, u32[]{:S(2)}) collective-permute-start(bf16[64,1536]{1,0:T(8,128)(2,1)} %refs_0_.1), channel_id=1, source_target_pairs={{0,4},{1,5},{2,6},{3,7},{4,0},{5,1},{6,2},{7,3},{8,12},{9,13},{10,... | collective-permute-start | bytes 589832 | tf_op jit(solution)/shard_map/ppermute | solution.py:303
  7.4 3.6 %collective-permute-start = (f32[2,64]{1,0:T(2,128)S(1)}, f32[2,64]{1,0:T(2,128)S(1)}, u32[]{:S(2)}, u32[]{:S(2)}) collective-permute-start(f32[2,64]{1,0:T(2,128)S(1)} %pad_maximum_fusion.4), channel_id=1, source_target_pairs={{0,8},{8,0},{16,24},{24,16},{1,9},{9,1},{17,25},{25,17},{2,10},{10... | collective-permute-start | bytes 1544 | tf_op jit(solution)/shard_map/ppermute | solution.py:306
  11.1 3.6 %collective-permute-start.1 = (f32[2,64]{1,0:T(2,128)S(1)}, f32[2,64]{1,0:T(2,128)S(1)}, u32[]{:S(2)}, u32[]{:S(2)}) collective-permute-start(f32[2,64]{1,0:T(2,128)S(1)} %fusion.35), channel_id=1, source_target_pairs={{0,16},{8,24},{16,0},{24,8},{1,17},{9,25},{17,1},{25,9},{2,18},{10... | collective-permute-start | bytes 1544 | tf_op jit(solution)/shard_map/ppermute | solution.py:306
  14.7 1.7 collective-permute-start.4
  16.4 6.9 %collective-permute-start.6 = (bf16[64,1536]{1,0:T(8,128)(2,1)S(1)}, bf16[64,1536]{1,0:T(8,128)(2,1)S(1)}, u32[]{:S(2)}, u32[]{:S(2)}) collective-permute-start(bf16[64,1536]{1,0:T(8,128)(2,1)S(1)} %collective-permute-done.5), channel_id=1, source_target_pairs={{0,2},{1,3},{2,0},{3,1},{4,6},{5,7},{6,4},{7,5},{8,10},{9,11},{10,... | collective-permute-start | bytes 589832 | tf_op jit(solution)/shard_map/ppermute | solution.py:303
  16.4 0.9 copy-start.8
  17.4 6.0 %copy-start.9 = (bf16[64,1536]{1,0:T(8,128)(2,1)S(1)}, bf16[64,1536]{1,0:T(8,128)(2,1)}, u32[]{:S(2)}) copy-start(bf16[64,1536]{1,0:T(8,128)(2,1)} %param.7) | copy-start | bytes 589828
  17.4 6.0 %copy-start.12 = (f32[1536]{0:T(1024)S(1)}, f32[1536]{0:T(1024)}, u32[]{:S(2)}) copy-start(f32[1536]{0:T(1024)} %param.8) | copy-start | bytes 18436
  23.2 13.0 %copy-start = (bf16[3072,1536]{1,0:T(8,128)(2,1)}, bf16[3072,1536]{1,0:T(8,128)(2,1)S(1)}, u32[]{:S(2)}) copy-start(bf16[3072,1536]{1,0:T(8,128)(2,1)S(1)} %get-tuple-element.43.refs_2_.refs_1_.w_ref) | copy-start | bytes 28311556
  23.2 31.4 %copy-start.6 = (f32[256,1536]{1,0:T(8,128)}, f32[256,1536]{1,0:T(8,128)S(1)}, u32[]{:S(2)}) copy-start(f32[256,1536]{1,0:T(8,128)S(1)} %get-tuple-element.48) | copy-start | bytes 4718596
  23.3 10.6 %collective-permute-start.7 = (bf16[128,1536]{1,0:T(8,128)(2,1)S(1)}, bf16[128,1536]{1,0:T(8,128)(2,1)S(1)}, u32[]{:S(2)}, u32[]{:S(2)}) collective-permute-start(bf16[128,1536]{1,0:T(8,128)(2,1)S(1)} %constant_dynamic-update-slice_fusion.refs_0_), channel_id=1, source_target_pairs={{0,1},{1,0},{2,3},{3,2},{4,5},{5,4},{6,7},{7,6},{8,9},{9,8},{10,11... | collective-permute-start | bytes 1179656 | tf_op jit(solution)/shard_map/ppermute | solution.py:303
  23.6 7.6 %collective-permute-start.8 = (bf16[64,1536]{1,0:T(8,128)(2,1)S(1)}, bf16[64,1536]{1,0:T(8,128)(2,1)S(1)}, u32[]{:S(2)}, u32[]{:S(2)}) collective-permute-start(bf16[64,1536]{1,0:T(8,128)(2,1)S(1)} %fusion.22.refs_0_), channel_id=1, source_target_pairs={{0,2},{1,3},{2,0},{3,1},{4,6},{5,7},{6,4},{7,5},{8,10},{9,11},{10,... | collective-permute-start | bytes 589832 | tf_op jit(solution)/shard_map/ppermute | solution.py:303
  25.6 29.0 %collective-permute-start.15 = (bf16[256,1536]{1,0:T(8,128)(2,1)S(1)}, bf16[256,1536]{1,0:T(8,128)(2,1)S(1)}, u32[]{:S(2)}, u32[]{:S(2)}) collective-permute-start(bf16[256,1536]{1,0:T(8,128)(2,1)S(1)} %get-tuple-element.41), channel_id=1, source_target_pairs={{0,8},{1,17},{2,10},{3,19},{4,12},{5,21},{6,14},{7,23},{8,0},{9,25... | collective-permute-start | bytes 2359304 | tf_op jit(solution)/shard_map/ppermute | solution.py:297
  27.1 11.7 %collective-permute-start.9 = (bf16[64,1536]{1,0:T(8,128)(2,1)S(1)}, bf16[64,1536]{1,0:T(8,128)(2,1)S(1)}, u32[]{:S(2)}, u32[]{:S(2)}) collective-permute-start(bf16[64,1536]{1,0:T(8,128)(2,1)S(1)} %fusion.22.refs_0_), channel_id=1, source_target_pairs={{0,1},{1,0},{2,3},{3,2},{4,5},{5,4},{6,7},{7,6},{8,9},{9,8},{10,11... | collective-permute-start | bytes 589832 | tf_op jit(solution)/shard_map/ppermute | solution.py:303
  31.2 7.7 %collective-permute-start.10 = (bf16[64,1536]{1,0:T(8,128)(2,1)S(1)}, bf16[64,1536]{1,0:T(8,128)(2,1)S(1)}, u32[]{:S(2)}, u32[]{:S(2)}) collective-permute-start(bf16[64,1536]{1,0:T(8,128)(2,1)S(1)} %collective-permute-done.8.refs_1_), channel_id=1, source_target_pairs={{0,1},{1,0},{2,3},{3,2},{4,5},{5,4},{6,7},{7,6},{8,9},{9,8},{10,11... | collective-permute-start | bytes 589832 | tf_op jit(solution)/shard_map/ppermute | solution.py:303
  31.2 15.0 %collective-permute-start.21 = (bf16[64,1536]{1,0:T(8,128)(2,1)S(1)}, bf16[64,1536]{1,0:T(8,128)(2,1)S(1)}, u32[]{:S(2)}, u32[]{:S(2)}) collective-permute-start(bf16[64,1536]{1,0:T(8,128)(2,1)S(1)} %fusion.22.refs_0_), channel_id=1, source_target_pairs={{0,4},{1,5},{2,6},{3,7},{4,0},{5,1},{6,2},{7,3},{8,12},{9,13},{10,... | collective-permute-start | bytes 589832 | tf_op jit(solution)/shard_map/ppermute | solution.py:303
  37.7 1.2 copy-start.4
  44.6 13.0 %copy-start.7 = (f32[256,1536]{1,0:T(8,128)}, f32[256,1536]{1,0:T(8,128)S(1)}, u32[]{:S(2)}) copy-start(f32[256,1536]{1,0:T(8,128)S(1)} %get-tuple-element.46) | copy-start | bytes 4718596
  44.6 12.1 %collective-permute-start.11 = (bf16[256,1536]{1,0:T(8,128)(2,1)S(1)}, bf16[256,1536]{1,0:T(8,128)(2,1)S(1)}, u32[]{:S(2)}, u32[]{:S(2)}) collective-permute-start(bf16[256,1536]{1,0:T(8,128)(2,1)S(1)} %get-tuple-element.47), channel_id=1, source_target_pairs={{0,8},{1,17},{2,10},{3,19},{4,12},{5,21},{6,14},{7,23},{8,0},{9,25... | collective-permute-start | bytes 2359304 | tf_op jit(solution)/shard_map/ppermute | solution.py:297
  46.2 6.8 %collective-permute-start.22 = (bf16[64,1536]{1,0:T(8,128)(2,1)S(1)}, bf16[64,1536]{1,0:T(8,128)(2,1)S(1)}, u32[]{:S(2)}, u32[]{:S(2)}) collective-permute-start(bf16[64,1536]{1,0:T(8,128)(2,1)S(1)} %collective-permute-done.21), channel_id=1, source_target_pairs={{0,2},{1,3},{2,0},{3,1},{4,6},{5,7},{6,4},{7,5},{8,10},{9,11},{10,... | collective-permute-start | bytes 589832 | tf_op jit(solution)/shard_map/ppermute | solution.py:303
  53.0 6.2 %collective-permute-start.23 = (bf16[128,1536]{1,0:T(8,128)(2,1)S(1)}, bf16[128,1536]{1,0:T(8,128)(2,1)S(1)}, u32[]{:S(2)}, u32[]{:S(2)}) collective-permute-start(bf16[128,1536]{1,0:T(8,128)(2,1)S(1)} %constant_dynamic-update-slice_fusion.2.refs_0_), channel_id=1, source_target_pairs={{0,1},{1,0},{2,3},{3,2},{4,5},{5,4},{6,7},{7,6},{8,9},{9,8},{10,11... | collective-permute-start | bytes 1179656 | tf_op jit(solution)/shard_map/ppermute | solution.py:303
  53.1 26.4 %collective-permute-start.28 = (bf16[256,1536]{1,0:T(8,128)(2,1)}, bf16[256,1536]{1,0:T(8,128)(2,1)}, u32[]{:S(2)}, u32[]{:S(2)}) collective-permute-start(bf16[256,1536]{1,0:T(8,128)(2,1)} %get-tuple-element.58), channel_id=1, source_target_pairs={{0,8},{1,17},{2,10},{3,19},{4,12},{5,21},{6,14},{7,23},{8,0},{9,25... | collective-permute-start | bytes 2359304 | tf_op jit(solution)/shard_map/ppermute | solution.py:297
  54.6 3.0 %copy-start.10 = (bf16[256,1536]{1,0:T(8,128)(2,1)}, bf16[256,1536]{1,0:T(8,128)(2,1)S(1)}, u32[]{:S(2)}) copy-start(bf16[256,1536]{1,0:T(8,128)(2,1)S(1)} %collective-permute-done.15) | copy-start | bytes 2359300
  55.6 12.4 %collective-permute-start.16 = (bf16[256,768]{1,0:T(8,128)(2,1)}, bf16[256,768]{1,0:T(8,128)(2,1)}, u32[]{:S(2)}, u32[]{:S(2)}) collective-permute-start(bf16[256,768]{1,0:T(8,128)(2,1)} %add_convert_fusion), channel_id=1, source_target_pairs={{0,16},{1,9},{2,18},{3,11},{4,20},{5,13},{6,22},{7,15},{8,24},{9,1... | collective-permute-start | bytes 1179656 | tf_op jit(solution)/shard_map/ppermute | solution.py:300
  56.7 2.5 %copy-start.11 = (bf16[256,1536]{1,0:T(8,128)(2,1)}, bf16[256,1536]{1,0:T(8,128)(2,1)S(1)}, u32[]{:S(2)}) copy-start(bf16[256,1536]{1,0:T(8,128)(2,1)S(1)} %collective-permute-done.11) | copy-start | bytes 2359300
  57.7 18.7 %collective-permute-start.12 = (bf16[256,768]{1,0:T(8,128)(2,1)}, bf16[256,768]{1,0:T(8,128)(2,1)}, u32[]{:S(2)}, u32[]{:S(2)}) collective-permute-start(bf16[256,768]{1,0:T(8,128)(2,1)} %add_convert_fusion.1), channel_id=1, source_target_pairs={{0,16},{1,9},{2,18},{3,11},{4,20},{5,13},{6,22},{7,15},{8,24},{9,1... | collective-permute-start | bytes 1179656 | tf_op jit(solution)/shard_map/ppermute | solution.py:300
  61.6 3.7 %copy-start.1 = (bf16[1536,3072]{1,0:T(8,128)(2,1)}, bf16[1536,3072]{1,0:T(8,128)(2,1)S(1)}, u32[]{:S(2)}) copy-start(bf16[1536,3072]{1,0:T(8,128)(2,1)S(1)} %get-tuple-element.49.w_ref.refs_2_.refs_1_) | copy-start | bytes 28311556
  65.3 22.6 %collective-permute-start.24 = (bf16[256,1536]{1,0:T(8,128)(2,1)}, bf16[256,1536]{1,0:T(8,128)(2,1)}, u32[]{:S(2)}, u32[]{:S(2)}) collective-permute-start(bf16[256,1536]{1,0:T(8,128)(2,1)} %get-tuple-element.57), channel_id=1, source_target_pairs={{0,8},{1,17},{2,10},{3,19},{4,12},{5,21},{6,14},{7,23},{8,0},{9,25... | collective-permute-start | bytes 2359304 | tf_op jit(solution)/shard_map/ppermute | solution.py:297
  67.6 11.8 %copy-start.5 = (f32[256,1536]{1,0:T(8,128)S(1)}, f32[256,1536]{1,0:T(8,128)}, u32[]{:S(2)}) copy-start(f32[256,1536]{1,0:T(8,128)} %copy-done.4) | copy-start | bytes 4718596
  78.8 12.5 %collective-permute-start.17 = (bf16[256,768]{1,0:T(8,128)(2,1)S(1)}, bf16[256,768]{1,0:T(8,128)(2,1)S(1)}, u32[]{:S(2)}, u32[]{:S(2)}) collective-permute-start(bf16[256,768]{1,0:T(8,128)(2,1)S(1)} %get-tuple-element.82), channel_id=1, source_target_pairs={{0,8},{1,17},{2,10},{3,19},{4,12},{5,21},{6,14},{7,23},{8,0},{9,25... | collective-permute-start | bytes 1179656 | tf_op jit(solution)/shard_map/ppermute | solution.py:297
  80.6 18.5 %collective-permute-start.29 = (bf16[256,768]{1,0:T(8,128)(2,1)S(1)}, bf16[256,768]{1,0:T(8,128)(2,1)S(1)}, u32[]{:S(2)}, u32[]{:S(2)}) collective-permute-start(bf16[256,768]{1,0:T(8,128)(2,1)S(1)} %fusion.12), channel_id=1, source_target_pairs={{0,16},{1,9},{2,18},{3,11},{4,20},{5,13},{6,22},{7,15},{8,24},{9,1... | collective-permute-start | bytes 1179656 | tf_op jit(solution)/shard_map/ppermute | solution.py:300
  81.2 17.8 %collective-permute-start.13 = (bf16[256,768]{1,0:T(8,128)(2,1)S(1)}, bf16[256,768]{1,0:T(8,128)(2,1)S(1)}, u32[]{:S(2)}, u32[]{:S(2)}) collective-permute-start(bf16[256,768]{1,0:T(8,128)(2,1)S(1)} %get-tuple-element.83), channel_id=1, source_target_pairs={{0,8},{1,17},{2,10},{3,19},{4,12},{5,21},{6,14},{7,23},{8,0},{9,25... | collective-permute-start | bytes 1179656 | tf_op jit(solution)/shard_map/ppermute | solution.py:297
  82.6 3.7 %copy-start.2 = (bf16[1536,3072]{1,0:T(8,128)(2,1)S(1)}, bf16[1536,3072]{1,0:T(8,128)(2,1)}, u32[]{:S(2)}) copy-start(bf16[1536,3072]{1,0:T(8,128)(2,1)} %copy-done.1) | copy-start | bytes 28311556
  86.3 23.9 %copy-start.3 = (bf16[1536,3072]{1,0:T(8,128)(2,1)S(1)}, bf16[1536,3072]{1,0:T(8,128)(2,1)}, u32[]{:S(2)}) copy-start(bf16[1536,3072]{1,0:T(8,128)(2,1)} %copy-done.1) | copy-start | bytes 28311556
  87.9 35.9 %slice-start = ((s8[9437184]{0:T(1024)(128)(4,1)}), s8[4194304]{0:T(1024)(128)(4,1)S(1)}, s32[]{:S(2)}) async-start(s8[9437184]{0:T(1024)(128)(4,1)} %bitcast.20), calls=%async_computation | async-start | bytes 8388608
  89.7 9.3 %collective-permute-start.25 = (bf16[256,768]{1,0:T(8,128)(2,1)S(1)}, bf16[256,768]{1,0:T(8,128)(2,1)S(1)}, u32[]{:S(2)}, u32[]{:S(2)}) collective-permute-start(bf16[256,768]{1,0:T(8,128)(2,1)S(1)} %fusion.14), channel_id=1, source_target_pairs={{0,16},{1,9},{2,18},{3,11},{4,20},{5,13},{6,22},{7,15},{8,24},{9,1... | collective-permute-start | bytes 1179656 | tf_op jit(solution)/shard_map/ppermute | solution.py:300
  91.4 18.9 %collective-permute-start.18 = (bf16[256,1536]{1,0:T(8,128)(2,1)S(1)}, bf16[256,1536]{1,0:T(8,128)(2,1)S(1)}, u32[]{:S(2)}, u32[]{:S(2)}) collective-permute-start(bf16[256,1536]{1,0:T(8,128)(2,1)S(1)} %pad_maximum_fusion.1.near_ref.near0), channel_id=1, source_target_pairs={{0,16},{1,9},{2,18},{3,11},{4,20},{5,13},{6,22},{7,15},{8,24},{9,1... | collective-permute-start | bytes 2359304 | tf_op jit(solution)/shard_map/ppermute | solution.py:300
  99.0 24.8 %slice-start.1 = ((s8[9437184]{0:T(1024)(128)(4,1)}), s8[4194304]{0:T(1024)(128)(4,1)S(1)}, s32[]{:S(2)}) async-start(s8[9437184]{0:T(1024)(128)(4,1)} %bitcast.20), calls=%async_computation.1 | async-start | bytes 8388608
  100.9 12.4 %collective-permute-start.30 = (bf16[256,768]{1,0:T(8,128)(2,1)S(1)}, bf16[256,768]{1,0:T(8,128)(2,1)S(1)}, u32[]{:S(2)}, u32[]{:S(2)}) collective-permute-start(bf16[256,768]{1,0:T(8,128)(2,1)S(1)} %get-tuple-element.80), channel_id=1, source_target_pairs={{0,8},{1,17},{2,10},{3,19},{4,12},{5,21},{6,14},{7,23},{8,0},{9,25... | collective-permute-start | bytes 1179656 | tf_op jit(solution)/shard_map/ppermute | solution.py:297
  102.5 21.3 %collective-permute-start.14 = (bf16[256,1536]{1,0:T(8,128)(2,1)S(1)}, bf16[256,1536]{1,0:T(8,128)(2,1)S(1)}, u32[]{:S(2)}, u32[]{:S(2)}) collective-permute-start(bf16[256,1536]{1,0:T(8,128)(2,1)S(1)} %pad_maximum_fusion.near_ref.p0), channel_id=1, source_target_pairs={{0,16},{1,9},{2,18},{3,11},{4,20},{5,13},{6,22},{7,15},{8,24},{9,1... | collective-permute-start | bytes 2359304 | tf_op jit(solution)/shard_map/ppermute | solution.py:300
  104.3 17.1 %collective-permute-start.26 = (bf16[256,768]{1,0:T(8,128)(2,1)S(1)}, bf16[256,768]{1,0:T(8,128)(2,1)S(1)}, u32[]{:S(2)}, u32[]{:S(2)}) collective-permute-start(bf16[256,768]{1,0:T(8,128)(2,1)S(1)} %get-tuple-element.81), channel_id=1, source_target_pairs={{0,8},{1,17},{2,10},{3,19},{4,12},{5,21},{6,14},{7,23},{8,0},{9,25... | collective-permute-start | bytes 1179656 | tf_op jit(solution)/shard_map/ppermute | solution.py:297
  110.3 13.6 %slice-start.2 = ((s8[9437184]{0:T(1024)(128)(4,1)}), s8[1048576]{0:T(1024)(128)(4,1)S(1)}, s32[]{:S(2)}) async-start(s8[9437184]{0:T(1024)(128)(4,1)} %bitcast.20), calls=%async_computation.2 | async-start | bytes 2097152
  112.9 14.3 %collective-permute-start.32 = (bf16[128,1536]{1,0:T(8,128)(2,1)S(1)}, bf16[128,1536]{1,0:T(8,128)(2,1)S(1)}, u32[]{:S(2)}, u32[]{:S(2)}) collective-permute-start(bf16[128,1536]{1,0:T(8,128)(2,1)S(1)} %get-tuple-element.51), channel_id=1, source_target_pairs={{0,1},{1,0},{2,3},{3,2},{4,5},{5,4},{6,7},{7,6},{8,9},{9,8},{10,11... | collective-permute-start | bytes 1179656 | tf_op jit(solution)/shard_map/ppermute | solution.py:303
  113.3 20.5 %collective-permute-start.31 = (bf16[256,1536]{1,0:T(8,128)(2,1)S(1)}, bf16[256,1536]{1,0:T(8,128)(2,1)S(1)}, u32[]{:S(2)}, u32[]{:S(2)}) collective-permute-start(bf16[256,1536]{1,0:T(8,128)(2,1)S(1)} %pad_maximum_fusion.3.near_ref.near1), channel_id=1, source_target_pairs={{0,16},{1,9},{2,18},{3,11},{4,20},{5,13},{6,22},{7,15},{8,24},{9,1... | collective-permute-start | bytes 2359304 | tf_op jit(solution)/shard_map/ppermute | solution.py:300
  126.4 2.1 %collective-permute-start.19 = (bf16[128,1536]{1,0:T(8,128)(2,1)S(1)}, bf16[128,1536]{1,0:T(8,128)(2,1)S(1)}, u32[]{:S(2)}, u32[]{:S(2)}) collective-permute-start(bf16[128,1536]{1,0:T(8,128)(2,1)S(1)} %get-tuple-element.54), channel_id=1, source_target_pairs={{0,1},{1,0},{2,3},{3,2},{4,5},{5,4},{6,7},{7,6},{8,9},{9,8},{10,11... | collective-permute-start | bytes 1179656 | tf_op jit(solution)/shard_map/ppermute | solution.py:303
  136.6 1.8 collective-permute-start.33
  138.5 7.8 %collective-permute-start.38 = (bf16[64,1536]{1,0:T(8,128)(2,1)S(1)}, bf16[64,1536]{1,0:T(8,128)(2,1)S(1)}, u32[]{:S(2)}, u32[]{:S(2)}) collective-permute-start(bf16[64,1536]{1,0:T(8,128)(2,1)S(1)} %slice.203), channel_id=1, source_target_pairs={{0,2},{1,3},{2,0},{3,1},{4,6},{5,7},{6,4},{7,5},{8,10},{9,11},{10,... | collective-permute-start | bytes 589832 | tf_op jit(solution)/shard_map/ppermute | solution.py:303
  138.9 15.8 %collective-permute-start.27 = (bf16[256,1536]{1,0:T(8,128)(2,1)S(1)}, bf16[256,1536]{1,0:T(8,128)(2,1)S(1)}, u32[]{:S(2)}, u32[]{:S(2)}) collective-permute-start(bf16[256,1536]{1,0:T(8,128)(2,1)S(1)} %pad_maximum_fusion.2.p1.near_ref), channel_id=1, source_target_pairs={{0,16},{1,9},{2,18},{3,11},{4,20},{5,13},{6,22},{7,15},{8,24},{9,1... | collective-permute-start | bytes 2359304 | tf_op jit(solution)/shard_map/ppermute | solution.py:300
  140.2 17.4 %collective-permute-start.37 = (bf16[64,1536]{1,0:T(8,128)(2,1)S(1)}, bf16[64,1536]{1,0:T(8,128)(2,1)S(1)}, u32[]{:S(2)}, u32[]{:S(2)}) collective-permute-start(bf16[64,1536]{1,0:T(8,128)(2,1)S(1)} %slice.204), channel_id=1, source_target_pairs={{0,2},{1,3},{2,0},{3,1},{4,6},{5,7},{6,4},{7,5},{8,10},{9,11},{10,... | collective-permute-start | bytes 589832 | tf_op jit(solution)/shard_map/ppermute | solution.py:303
  146.4 11.3 %collective-permute-start.39 = (bf16[64,1536]{1,0:T(8,128)(2,1)S(1)}, bf16[64,1536]{1,0:T(8,128)(2,1)S(1)}, u32[]{:S(2)}, u32[]{:S(2)}) collective-permute-start(bf16[64,1536]{1,0:T(8,128)(2,1)S(1)} %slice_add_fusion.4), channel_id=1, source_target_pairs={{0,4},{1,5},{2,6},{3,7},{4,0},{5,1},{6,2},{7,3},{8,12},{9,13},{10,... | collective-permute-start | bytes 589832 | tf_op jit(solution)/shard_map/ppermute | solution.py:303
  146.7 1.2 collective-permute-start.42
  148.0 4.2 %collective-permute-start.43 = (f32[1536]{0:T(1024)S(1)}, f32[1536]{0:T(1024)S(1)}, u32[]{:S(2)}, u32[]{:S(2)}) collective-permute-start(f32[1536]{0:T(1024)S(1)} %add.198), channel_id=1, source_target_pairs={{0,2},{1,3},{2,0},{3,1},{4,6},{5,7},{6,4},{7,5},{8,10},{9,11},{10,... | collective-permute-start | bytes 18440 | tf_op jit(solution)/shard_map/ppermute | solution.py:303
  152.2 8.0 %collective-permute-start.44 = (f32[1536]{0:T(1024)S(1)}, f32[1536]{0:T(1024)S(1)}, u32[]{:S(2)}, u32[]{:S(2)}) collective-permute-start(f32[1536]{0:T(1024)S(1)} %add.199), channel_id=1, source_target_pairs={{0,4},{1,5},{2,6},{3,7},{4,0},{5,1},{6,2},{7,3},{8,12},{9,13},{10,... | collective-permute-start | bytes 18440 | tf_op jit(solution)/shard_map/ppermute | solution.py:303
  157.5 5.2 %collective-permute-start.34 = (bf16[128,1536]{1,0:T(8,128)(2,1)S(1)}, bf16[128,1536]{1,0:T(8,128)(2,1)S(1)}, u32[]{:S(2)}, u32[]{:S(2)}) collective-permute-start(bf16[128,1536]{1,0:T(8,128)(2,1)S(1)} %get-tuple-element.68), channel_id=1, source_target_pairs={{0,1},{1,0},{2,3},{3,2},{4,5},{5,4},{6,7},{7,6},{8,9},{9,8},{10,11... | collective-permute-start | bytes 1179656 | tf_op jit(solution)/shard_map/ppermute | solution.py:303
  157.9 3.6 %collective-permute-start.40 = (f32[2,64]{1,0:T(2,128)S(1)}, f32[2,64]{1,0:T(2,128)S(1)}, u32[]{:S(2)}, u32[]{:S(2)}) collective-permute-start(f32[2,64]{1,0:T(2,128)S(1)} %pad_maximum_fusion.5), channel_id=1, source_target_pairs={{0,8},{8,0},{16,24},{24,16},{1,9},{9,1},{17,25},{25,17},{2,10},{10... | collective-permute-start | bytes 1544 | tf_op jit(solution)/shard_map/ppermute | solution.py:306
  159.5 23.2 %collective-permute-start.20 = (bf16[64,1536]{1,0:T(8,128)(2,1)S(1)}, bf16[64,1536]{1,0:T(8,128)(2,1)S(1)}, u32[]{:S(2)}, u32[]{:S(2)}) collective-permute-start(bf16[64,1536]{1,0:T(8,128)(2,1)S(1)} %slice.206), channel_id=1, source_target_pairs={{0,2},{1,3},{2,0},{3,1},{4,6},{5,7},{6,4},{7,5},{8,10},{9,11},{10,... | collective-permute-start | bytes 589832 | tf_op jit(solution)/shard_map/ppermute | solution.py:303
  161.5 8.0 %collective-permute-start.41 = (f32[2,64]{1,0:T(2,128)S(1)}, f32[2,64]{1,0:T(2,128)S(1)}, u32[]{:S(2)}, u32[]{:S(2)}) collective-permute-start(f32[2,64]{1,0:T(2,128)S(1)} %fusion.34), channel_id=1, source_target_pairs={{0,16},{8,24},{16,0},{24,8},{1,17},{9,25},{17,1},{25,9},{2,18},{10... | collective-permute-start | bytes 1544 | tf_op jit(solution)/shard_map/ppermute | solution.py:306
  162.9 7.9 %collective-permute-start.35 = (bf16[64,1536]{1,0:T(8,128)(2,1)S(1)}, bf16[64,1536]{1,0:T(8,128)(2,1)S(1)}, u32[]{:S(2)}, u32[]{:S(2)}) collective-permute-start(bf16[64,1536]{1,0:T(8,128)(2,1)S(1)} %slice.205), channel_id=1, source_target_pairs={{0,2},{1,3},{2,0},{3,1},{4,6},{5,7},{6,4},{7,5},{8,10},{9,11},{10,... | collective-permute-start | bytes 589832 | tf_op jit(solution)/shard_map/ppermute | solution.py:303
  170.8 11.9 %collective-permute-start.36 = (bf16[64,1536]{1,0:T(8,128)(2,1)S(1)}, bf16[64,1536]{1,0:T(8,128)(2,1)S(1)}, u32[]{:S(2)}, u32[]{:S(2)}) collective-permute-start(bf16[64,1536]{1,0:T(8,128)(2,1)S(1)} %slice_add_fusion.6), channel_id=1, source_target_pairs={{0,4},{1,5},{2,6},{3,7},{4,0},{5,1},{6,2},{7,3},{8,12},{9,13},{10,... | collective-permute-start | bytes 589832 | tf_op jit(solution)/shard_map/ppermute | solution.py:303
  173.0 9.8 %copy-start.13 = (f32[1536]{0:T(1024)S(1)}, f32[1536]{0:T(1024)}, u32[]{:S(2)}) copy-start(f32[1536]{0:T(1024)} %param.12) | copy-start | bytes 18436

commit v3 on v2

v3 whole, which is shorter than its diff:
```python
import jax
import jax.numpy as jnp
from jax import lax
from jax.experimental import pallas as pl
from jax.experimental.pallas import tpu as pltpu
from jax.sharding import PartitionSpec as P

D = 6144

epsilon = 1e-06
inv_root_two = 0.7071067811865476
inv_root_two_pi = 0.3989422804014327

bf16 = jnp.bfloat16
f32 = jnp.float32
MIB = 1024 * 1024

NN = (((1,), (0,)), ((), ()))
NT = (((1,), (1,)), ((), ()))
TN = (((0,), (0,)), ((), ()))


def mm(left, right, dims):
    return lax.dot_general(left, right, dims, preferred_element_type=f32)


def call(kernel, name, out_shape, in_specs, out_specs, flops, moved, scratch=(), aliases=None, limit=8):
    return pl.pallas_call(
        kernel,
        name=name,
        out_shape=out_shape,
        in_specs=in_specs,
        out_specs=out_specs,
        scratch_shapes=scratch,
        input_output_aliases=aliases or {},
        compiler_params=pltpu.CompilerParams(vmem_limit_bytes=limit * MIB),
        cost_estimate=pl.CostEstimate(flops=0, bytes_accessed=0, transcendentals=0),
    )


IN_VMEM = pl.BlockSpec(memory_space=pltpu.VMEM)
IN_SMEM = pl.BlockSpec(memory_space=pltpu.SMEM)
IN_HBM = pl.BlockSpec(memory_space=pltpu.HBM)


def bits(n):
    return [1 << b for b in range(n.bit_length() - 1)]


def after(x, *others):
    return lax.optimization_barrier((x, *others))[0]


def block_at(me, rel, size):
    return pl.ds(pl.multiple_of((me ^ rel) * size, size), size)


def pieces_of(x_refs):
    return jnp.concatenate([x[...] for x in x_refs], axis=0)


def load_and_multiply(name, xs, w, me, shard, rels, dtype, by_rows):
    rows, depth = sum(x.shape[0] for x in xs), xs[0].shape[1]
    n, parts, whole = len(rels), 4, len(xs) > 1

    def kernel(me_ref, *refs):
        x_refs, (w_ref, o_ref, held_ref), sem = refs[: len(xs)], refs[len(xs) : len(xs) + 3], refs[-1]
        copies = {}
        for i, r in enumerate(rels):
            at, to = block_at(me_ref[0], r, shard), slice(i * shard, (i + 1) * shard)
            source, target = (w_ref.at[at, :], held_ref.at[to, :]) if by_rows else (w_ref.at[:, at], held_ref.at[:, to])
            size = source.shape[0] // parts
            for p in range(parts):
                span = pl.ds(p * size, size)
                copies[i, p] = pltpu.make_async_copy(source.at[span, :], target.at[span, :], sem.at[i, p])
                copies[i, p].start()
        x_ref = x_refs[0]
        if whole:
            x_ref = refs[len(xs) + 3]
            x_ref[...] = pieces_of(x_refs)
        for i in range(n):
            for p in range(parts):
                copies[i, p].wait()
            to = slice(i * shard, (i + 1) * shard)
            block = held_ref[to, :] if by_rows else held_ref[:, to]
            o_ref[:, to] = mm(x_ref[...], block, NT if by_rows else NN).astype(dtype)

    out_shape = [
        jax.ShapeDtypeStruct((rows, n * shard), dtype),
        pltpu.VMEM((n * shard, depth) if by_rows else (depth, n * shard), w.dtype),
    ]
    if whole:
        out_shape.append(jax.ShapeDtypeStruct((rows, depth), bf16))
    return call(
        kernel,
        name,
        out_shape,
        [IN_SMEM] + [IN_VMEM] * len(xs) + [IN_HBM],
        [IN_VMEM] * len(out_shape),
        2 * rows * depth * shard * n,
        2 * depth * shard * n,
        scratch=[pltpu.SemaphoreType.DMA((n, parts))],
    )(me, *xs, pltpu.with_memory_space_constraint(w, pltpu.HBM))


def multiply(name, xs, w_go, w_keep, shard, by_rows):
    rows, depth = sum(x.shape[0] for x in xs), xs[0].shape[1]

    def kernel(*refs):
        x_refs, (go_w, keep_w, go_ref, keep_ref, all_ref) = refs[: len(xs)], refs[len(xs) :]
        all_ref[...] = pieces_of(x_refs)
        for w_ref, o_ref in ((go_w, go_ref), (keep_w, keep_ref)):
            for c in (slice(0, shard), slice(shard, 2 * shard)):
                block = w_ref[c, :] if by_rows else w_ref[:, c]
                o_ref[:, c] = mm(all_ref[...], block, NT if by_rows else NN).astype(o_ref.dtype)

    return call(
        kernel,
        name,
        (
            jax.ShapeDtypeStruct((rows, 2 * shard), bf16),
            jax.ShapeDtypeStruct((rows, 2 * shard), f32),
            jax.ShapeDtypeStruct((rows, depth), bf16),
        ),
        [IN_VMEM] * (len(xs) + 2),
        [IN_VMEM] * 3,
        8 * rows * depth * shard,
        12 * rows * shard,
    )(*xs, w_go, w_keep)


def summed(near, far, w_ref, me, shard, cols, by_rows):
    total = None
    for r, ref, start in ((0, near, 0), (2, near, shard), (1, far, 0), (3, far, shard)):
        at = block_at(me, r, shard)
        block = w_ref[at, cols] if by_rows else w_ref[cols, at]
        term = mm(ref[:, start : start + shard], block, NN if by_rows else NT)
        total = term if total is None else total + term
    return total


def down_product(name, near, far, w_down, me):
    rows, wide = near.shape
    out = w_down.shape[1]
    half, shard, nb = rows // 2, wide // 2, 256

    def kernel(me_ref, near_ref, far_ref, w_ref, keep_ref, go_ref):
        for c in range(0, out, nb):
            cols = slice(c, c + nb)
            total = summed(near_ref, far_ref, w_ref, me_ref[0], shard, cols, True)
            keep_ref[:, cols] = total[:half]
            go_ref[:, cols] = total[half:].astype(bf16)

    return call(
        kernel,
        name,
        (jax.ShapeDtypeStruct((half, out), f32), jax.ShapeDtypeStruct((half, out), bf16)),
        [IN_SMEM] + [IN_VMEM] * 3,
        [IN_VMEM] * 2,
        4 * rows * wide * out,
        4 * rows * wide + 3 * rows * out,
    )(me, near, far, w_down)


def normed_grad(name, near, far, w_up, normed, me, gain=None):
    rows, wide = near.shape
    out = w_up.shape[0]
    half, shard, nb = rows // 2, wide // 2, 256
    more = () if gain is None else (gain,)

    def kernel(me_ref, near_ref, far_ref, w_ref, n_ref, *refs):
        keep_ref, go_ref, gain_ref = refs[-3:]
        for c in range(0, out, nb):
            cols = slice(c, c + nb)
            total = summed(near_ref, far_ref, w_ref, me_ref[0], shard, cols, False)
            keep_ref[:, cols] = total[:half]
            go_ref[:half, cols] = total[half:].astype(bf16)
            sums = jnp.sum(total * n_ref[:, cols].astype(f32), axis=0, keepdims=True)
            if more:
                sums += refs[0][:, cols]
                rounded = sums.astype(bf16).astype(f32)
                rest = (sums - rounded).astype(bf16).astype(f32)
                tail = [jnp.broadcast_to(rounded, (8, nb)), jnp.broadcast_to(rest, (8, nb))]
                go_ref[half:, cols] = jnp.concatenate(tail, axis=0).astype(bf16)
                sums = rounded + rest
            gain_ref[:, cols] = sums

    return call(
        kernel,
        name,
        (
            jax.ShapeDtypeStruct((half, out), f32),
            jax.ShapeDtypeStruct((half + 16 * len(more), out), bf16),
            jax.ShapeDtypeStruct((1, out), f32),
        ),
        [IN_SMEM] + [IN_VMEM] * (4 + len(more)),
        [IN_VMEM] * 3,
        4 * rows * wide * out,
        4 * rows * wide + 3 * rows * out,
    )(me, near, far, w_up, normed, *more)


def stream_out(steps, compute, place, buf, sem):
    copies = []
    for i in range(steps):
        if i >= 2:
            copies[i - 2].wait()
        buf[i % 2] = compute(i)
        copies.append(pltpu.make_async_copy(buf.at[i % 2], place(i), sem.at[i % 2]))
        copies[i].start()
    for c in copies[-2:]:
        c.wait()


def weight_grad_down(name, pieces, cots, me, rels, shard, units, so_far):
    nb = shard // 2
    out = cots[0].shape[1]
    tokens = sum(c.shape[0] for c in cots)
    steps = 2 * len(rels)

    def kernel(me_ref, p0, p1, c0, c1, *refs):
        o_ref, buf, sem = refs[-3:]

        def compute(i):
            cols = slice(i * nb, (i + 1) * nb)
            return mm(p0[:, cols], c0[...], TN) + mm(p1[:, cols], c1[...], TN)

        def place(i):
            start = (me_ref[0] ^ rels[i // 2]) * shard + (i % 2) * nb
            return o_ref.at[pl.ds(pl.multiple_of(start, nb), nb), :]

        stream_out(steps, compute, place, buf, sem)

    rest = () if so_far is None else (so_far,)
    return call(
        kernel,
        name,
        jax.ShapeDtypeStruct((units, out), f32),
        [IN_SMEM] + [IN_VMEM] * 4 + [IN_HBM] * len(rest),
        IN_HBM,
        2 * tokens * nb * steps * out,
        4 * nb * steps * out,
        scratch=[pltpu.VMEM((2, nb, out), f32), pltpu.SemaphoreType.DMA((2,))],
        aliases={5: 0} if rest else None,
        limit=12,
    )(me, *pieces, *cots, *rest)


def weight_grad_up(name, normed, nears, fars, me, units, span, so_far):
    out = normed[0].shape[1]
    tokens = sum(n.shape[0] for n in nears)
    shard = nears[0].shape[1] // 2
    nb = 256
    sums = so_far is None

    def kernel(me_ref, n0, n1, near0, near1, far0, far1, *refs):
        buf, sem = refs[-2:]
        o_ref = refs[0] if sums else refs[1]
        four = ((0, near0, near1, 0), (2, near0, near1, shard), (1, far0, far1, 0), (3, far0, far1, shard))
        copies = []
        for i, first in enumerate(span):
            if i >= 2:
                copies[i - 2].wait()
            rows = slice(first, first + nb)
            t0, t1 = n0[:, rows].T, n1[:, rows].T
            for r, p0, p1, start in four:
                at = slice(start, start + shard)
                term = mm(t0, p0[:, at], NN) + mm(t1, p1[:, at], NN)
                buf[i % 2, :, block_at(me_ref[0], r, shard)] = term
            copies.append(pltpu.make_async_copy(buf.at[i % 2], o_ref.at[rows, :], sem.at[i % 2]))
            copies[i].start()
        if sums:
            for r, p0, p1, start in four:
                at = slice(start, start + shard)
                total = jnp.sum(p0[:, at].astype(f32), axis=0, keepdims=True)
                total += jnp.sum(p1[:, at].astype(f32), axis=0, keepdims=True)
                refs[1][:, block_at(me_ref[0], r, shard)] = total
        for c in copies[-2:]:
            c.wait()

    out_shape = [jax.ShapeDtypeStruct((out, units), f32)]
    if sums:
        out_shape.append(jax.ShapeDtypeStruct((1, units), f32))
    return call(
        kernel,
        name,
        out_shape,
        [IN_SMEM] + [IN_VMEM] * 6 + ([] if sums else [IN_HBM]),
        [IN_HBM, IN_VMEM] if sums else [IN_HBM],
        2 * tokens * units * nb * len(span),
        4 * units * nb * len(span),
        scratch=[pltpu.VMEM((2, nb, units), f32), pltpu.SemaphoreType.DMA((2,))],
        aliases=None if sums else {7: 0},
        limit=14,
    )(me, *normed, *nears, *fars, *([] if sums else [so_far]))


def solution(mesh):
    n_gx, n_gy = mesh.shape["gx"], mesh.shape["gy"]
    both = ("gx", "gy")
    chips = n_gy // 2

    def across(first):
        pairs = []
        for gx in range(n_gx):
            for gy in range(n_gy):
                flip = 1 if (gy % 2 == 0) == first else 2
                pairs.append((gx * n_gy + gy, (gx ^ flip) * n_gy + gy))
        return pairs

    first_pairs, second_pairs = across(True), across(False)

    def to_first(x):
        return lax.ppermute(x, both, first_pairs)

    def to_second(x):
        return lax.ppermute(x, both, second_pairs)

    def along_gy(x, m):
        return lax.ppermute(x, "gy", [(i, i ^ m) for i in range(n_gy)])

    def along_gx(x, m):
        return lax.ppermute(x, "gx", [(i, i ^ m) for i in range(n_gx)])

    def plane_sum(x, least=1):
        for step in bits(n_gx)[least - 1 :]:
            x = x + along_gx(x, step)
        return x

    def over_groups(total):
        for step in bits(n_gx)[2:]:
            total = total + along_gx(total, step)
        return total

    def for_second(keep, came, shard):
        return (keep[:, shard:] + came[:, shard:].astype(f32)).astype(bf16)

    def plane_total(keep, came, back, shard):
        return over_groups(keep[:, :shard] + came[:, :shard].astype(f32) + back.astype(f32))

    def shards(patches, norm_gain, w_up, bias_up, w_down, bias_down, cotangent):
        rows = patches.shape[0]
        units = w_up.shape[1]
        shard = units // 4
        gx, gy = lax.axis_index("gx") % 4, lax.axis_index("gy")
        me = jnp.where(gy % 2 == 0, 2 * (gx % 2) + gx // 2, gx).astype(jnp.int32)
        bias = lax.dynamic_slice_in_dim(bias_up, me * shard, shard)
        me = me.reshape(1)

        w_up = pltpu.with_memory_space_constraint(w_up, pltpu.HBM)
        w_down = pltpu.with_memory_space_constraint(w_down, pltpu.HBM)

        def gather(own, first=()):
            z1 = along_gy(own, 2)
            if first:
                z1 = after(z1, *first)
            return [own, z1, along_gy(own, 1), along_gy(z1, 1)]

        def gather_far(own, first=()):
            even = [own]
            for step in bits(chips)[1:]:
                even += [along_gy(e, 2 * step) for e in even]
            even = even[1:]
            if first:
                even[0] = after(even[0], *first)
            even += [along_gy(e, 2) for e in even]
            even = jnp.concatenate(even)
            return [even, along_gy(even, 1)]

        cot_w = gather(cotangent)
        values = patches.astype(f32)
        totals = jnp.stack([jnp.sum(values, axis=1), jnp.sum(values * values, axis=1)])
        totals = totals + along_gx(totals, 1)
        late_down = pltpu.with_memory_space_constraint(w_down, pltpu.VMEM)
        late_up = pltpu.with_memory_space_constraint(w_up, pltpu.VMEM)
        go, down_go, cot_w = load_and_multiply("grad_act_w_go", cot_w, w_down, me, shard, (2, 3), bf16, True)
        came_gw = to_first(go)
        cot_x = gather_far(cotangent, [go])
        keep_gw, down_keep = load_and_multiply("grad_act_w_keep", [cot_w], w_down, me, shard, (0, 1), f32, True)
        totals = plane_sum(after(totals, go), 2)

        row_mean = (totals[0] / D)[:, None]
        variance = (totals[1] / D)[:, None] - row_mean * row_mean
        inv_std = lax.rsqrt(variance + epsilon)
        standard = (values - row_mean) * inv_std
        own = (standard * norm_gain).astype(bf16)
        second_gw = for_second(keep_gw, came_gw, shard)
        back_gw = to_second(second_gw)
        normed_w = gather(own, [second_gw])
        normed_x = gather_far(own)
        go, keep_gx, cot_x = multiply("grad_act_x", cot_x, down_go, down_keep, shard, True)
        came_gx = to_first(go)
        normed_w[0] = after(normed_w[0], go)
        go, up_go, normed_w = load_and_multiply("hidden_w_go", normed_w, w_up, me, shard, (2, 3), bf16, False)
        came_hw = to_first(go)
        keep_hw, up_keep = load_and_multiply("hidden_w_keep", [normed_w], w_up, me, shard, (0, 1), f32, False)
        second_gx = for_second(keep_gx, came_gx, shard)
        back_gx = to_second(second_gx)

        def middle(grad_act, hidden):
            hidden = hidden + bias
            upper = 0.5 * (1.0 + lax.erf(hidden * inv_root_two))
            act = (hidden * upper).astype(bf16)
            slope = upper + hidden * jnp.exp(-0.5 * hidden * hidden) * inv_root_two_pi
            return act, (grad_act * slope).astype(bf16)

        go, keep_hx, normed_x = multiply("hidden_x", normed_x, up_go, up_keep, shard, False)
        came_hx = to_first(go)
        second_hw = for_second(keep_hw, after(came_hw, second_gx, go), shard)
        back_hw = to_second(second_hw)
        second_hx = for_second(keep_hx, came_hx, shard)
        back_hx = to_second(second_hx)
        act_w, grad_w = middle(
            plane_total(keep_gw, after(came_gw, back_gx), back_gw, shard),
            plane_total(keep_hw, came_hw, after(back_hw, second_hx), shard),
        )
        grad_near_w = jnp.concatenate([grad_w, to_first(grad_w)], axis=1)
        near_w = jnp.concatenate([act_w, to_first(act_w)], axis=1)
        act_x, grad_x = middle(
            plane_total(keep_gx, after(came_gx, act_w, grad_w), back_gx, shard),
            plane_total(keep_hx, came_hx, back_hx, shard),
        )
        grad_near_x = jnp.concatenate([grad_x, after(to_first(grad_x), grad_near_w, near_w)], axis=1)
        near_x = jnp.concatenate([act_x, after(to_first(act_x), grad_near_x)], axis=1)
        grad_far_x = to_second(grad_near_x)
        far_x = to_second(near_x)
        grad_far_w = to_second(after(grad_near_w, near_x))
        far_w = to_second(after(near_w, near_x))

        def pair_sum(keep, go):
            return keep + along_gy(go, 1).astype(f32)

        def swap(block, m, gain):
            if gain is None:
                return along_gy(block.astype(bf16), m).astype(f32), None
            n = block.shape[0]
            rounded = lax.reduce_precision(gain, 8, 7)
            rest = lax.reduce_precision(gain - rounded, 8, 7)
            tail = [jnp.broadcast_to(g, (8, g.shape[1])) for g in (rounded, rest)]
            came = along_gy(jnp.concatenate([block] + tail).astype(bf16), m).astype(f32)
            return came[:n], (rounded + rest) + (came[n : n + 1] + came[n + 8 : n + 9])

        def from_neighbour(sums, gain=None, *first):
            half = chips // 2 - 1
            came, gain = swap(sums[half * rows :], 2, gain)
            came = after(came, *first) if first else came
            sums = sums[: half * rows] + came
            return [sums[i * rows : (i + 1) * rows] for i in range(half)], gain

        def from_far(held, gain=None):
            held = [0.0] + held
            for step in reversed(bits(chips)[1:]):
                size = len(held) // 2
                for i in range(size):
                    came, total = swap(held[size + i], 2 * step, gain if i == 0 else None)
                    held[i] = held[i] + came
                    if i == 0:
                        first = total
                held, gain = held[:size], first
            return held[0], gain

        down = weight_grad_down("wgrad_near", (near_w, near_x), (cot_w, cot_x), me, (0, 2), shard, units, None)
        keep, go, gain_x = normed_grad("normed_grad_x", grad_near_x, after(grad_far_x, down), late_up, normed_x, me)
        grad_sums_x = pair_sum(keep, go)
        keep, go = down_product("mlp_x", near_x, after(far_x, go), late_down, me)
        sums_x = pair_sum(keep, go)
        keep, go, gain = normed_grad(
            "normed_grad_w", grad_near_w, after(grad_far_w, go), late_up, normed_w, me, gain_x
        )
        n = keep.shape[0]
        normed = (after(normed_w, go, sums_x, grad_sums_x), normed_x)
        came = along_gy(go, 1).astype(f32)
        grad_sums_w = keep + came[:n]
        gain = gain + (came[n : n + 1] + came[n + 8 : n + 9])
        nears, fars = (grad_near_w, grad_near_x), (grad_far_w, grad_far_x)
        steps = range(0, patches.shape[1], 256)
        some, others = steps[: len(steps) // 2], steps[len(steps) // 2 :]
        grad_w_up, grad_bias_up = weight_grad_up("wgrad_up_1", normed, nears, fars, me, units, some, None)
        grad_held, _ = from_neighbour(grad_sums_x, None, grad_bias_up)
        held, _ = from_neighbour(sums_x, None, grad_bias_up)
        keep, go = down_product("mlp_w", near_w, after(far_w, grad_bias_up, grad_sums_w, *grad_held, *held), late_down, me)
        sums_w = pair_sum(keep, go)
        far_w = after(far_w, go, *held)
        grad_w_down = weight_grad_down("wgrad_far", (far_w, far_x), (cot_w, cot_x), me, (1, 3), shard, units, down)
        grad_far, _ = from_far(grad_held)
        came, gain = swap(grad_sums_w[rows:], 2, gain)
        grad_normed = grad_sums_w[:rows] + after(came, grad_w_down) + grad_far
        scaled = grad_normed * norm_gain
        sums = jnp.stack([jnp.sum(scaled, axis=1), jnp.sum(scaled * standard, axis=1)])
        normed = (after(normed_w, grad_w_down, sums_w, sums), normed_x)
        grad_w_up = weight_grad_up("wgrad_up_2", normed, nears, fars, me, units, others, grad_w_up)[0]
        sums = sums + after(along_gx(sums, 1), grad_w_up)
        mlp_home = sums_w[:rows] + after(along_gy(sums_w[rows:].astype(bf16), 2), grad_w_up).astype(f32)
        held = [after(h, grad_w_down) for h in held]
        mlp_out = (mlp_home + from_far(held)[0] + bias_down).astype(bf16)
        for step in bits(chips)[1:]:
            gain = gain + along_gy(gain, 2 * step)
        grad_gain = gain[0] / norm_gain

        grad_bias_down = jnp.sum(cot_w.astype(f32), axis=0) + jnp.sum(cot_x.astype(f32), axis=0)

        sums = plane_sum(sums, 2)
        first_mean = (sums[0] / D)[:, None]
        second_mean = (sums[1] / D)[:, None]
        grad_patches = (inv_std * (scaled - first_mean - standard * second_mean)).astype(bf16)
        return mlp_out, grad_patches, grad_gain, grad_w_up, grad_bias_up[0], grad_w_down, grad_bias_down

    in_specs = (
        P("gy", "gx"),
        P("gx"),
        P("gx", "gy"),
        P("gy"),
        P("gy", "gx"),
        P("gx"),
        P("gy", "gx"),
    )
    out_specs = (
        P("gy", "gx"),
        P("gy", "gx"),
        P("gx"),
        P("gx", "gy"),
        P("gy"),
        P("gy", "gx"),
        P("gx"),
    )
    return jax.shard_map(shards, mesh=mesh, in_specs=in_specs, out_specs=out_specs, check_vma=False)
```

time: 184 us -> 176 us (0.957)
  local copies, waits for them, and re-layouts: 10.5 us -> 4.65 us
  waiting for transfers between devices: 60 us -> 55.4 us
  Pallas kernels: 50.3 us -> 52.8 us
    ppermute x25 -> x23, waiting for transfers between devices: 23.9 us -> 16.8 us  [along_gy(): return lax.ppermute(x, 'gy', [(i, i ^ m) for i in range(n_gy)])]
    ppermute x8, waiting for transfers between devices: 14.4 us -> 20.5 us  [to_first(): return lax.ppermute(x, both, first_pairs)]
    unnamed x36 -> x44, local copies, waits for them, and re-layouts: 9.59 us -> 3.61 us
    pallas_call x7 -> x8, Pallas kernels: 29.1 us -> 31.6 us  [the longest x4 14.7 us: load_and_multiply(): call(kernel, name, out_shape, [IN_SMEM] + [IN_VMEM] * len(xs) + [IN_HBM],...]
    ppermute x4, waiting for transfers between devices: 4.81 us -> 2.66 us  [along_gx(): return lax.ppermute(x, 'gx', [(i, i ^ m) for i in range(n_gx)])]
    ppermute x25 -> x23, starting transfers between devices: 22.2 us -> 23.1 us  [along_gy(): return lax.ppermute(x, 'gy', [(i, i ^ m) for i in range(n_gy)])]
  transfers between devices with their start and end apart: 45 -> 43, of which waited for: 19 -> 21; matrix products, arithmetic and copies ran while one was open for 8% -> 8% of each run, Pallas kernels for 26% -> 30%
where the time goes in v3:
time: 176 us; the launch traced here: 175 us
  waiting for transfers between devices  55.4 us (31%)
  Pallas kernels  52.8 us (30%)
  starting transfers between devices  47.6 us (27%)
  other arithmetic  13.6 us (8%)
  local copies, waits for them, and re-layouts  4.65 us (3%)
    ppermute x23, starting transfers between devices, along_gy(): return lax.ppermute(x, 'gy', [(i, i ^ m) for i in range(n_gy)])  23.1 us
    ppermute x8, waiting for transfers between devices, to_first(): return lax.ppermute(x, both, first_pairs)  20.5 us
    ppermute x23, waiting for transfers between devices, along_gy(): return lax.ppermute(x, 'gy', [(i, i ^ m) for i in range(n_gy)])  16.8 us
    ppermute x8, waiting for transfers between devices, to_second(): return lax.ppermute(x, both, second_pairs)  15.4 us
    pallas_call x4, Pallas kernels, load_and_multiply(): call(kernel, name, out_shape, [IN_SMEM] + [IN_VMEM] * len(xs) + [IN_HBM],...  14.7 us
    pallas_call x2, Pallas kernels, weight_grad_up(): call(kernel, name, out_shape, [IN_SMEM] + [IN_VMEM] * 6 + ([] if sums els...  11.7 us
    pallas_call x2, Pallas kernels, weight_grad_down(): call(kernel, name, jax.ShapeDtypeStruct((units, out), f32), [IN_SMEM] + [...  10.7 us
    ppermute x8, starting transfers between devices, to_first(): return lax.ppermute(x, both, first_pairs)  9.72 us
  transfers between devices with their start and end apart: 43, of which 21 were waited for; matrix products, arithmetic and copies ran while one was open for 8% of the time, Pallas kernels for 30%

profile of v3, /device:TPU:0, one launch (start us, length us, event | category | flops | bytes accessed | tf_op | source)
XLA Modules:
  0.0 175.3 jit_solution(6959211634879148412)
XLA Ops:
  0.6 3.1 %collective-permute-start.1 = (bf16[64,1536]{1,0:T(8,128)(2,1)}, bf16[64,1536]{1,0:T(8,128)(2,1)S(1)}, u32[]{:S(2)}, u32[]{:S(2)}) collective-permute-start(bf16[64,1536]{1,0:T(8,128)(2,1)} %refs_0_.1), channel_id=1, source_target_pairs={{0,2},{1,3},{2,0},{3,1},{4,6},{5,7},{6,4},{7,5},{8,10},{9,11},{10,... | collective-permute-start | bytes 589832 | tf_op jit(solution)/shard_map/ppermute | solution.py:320
  3.7 2.6 %collective-permute-start.5 = (bf16[64,1536]{1,0:T(8,128)(2,1)}, bf16[64,1536]{1,0:T(8,128)(2,1)S(1)}, u32[]{:S(2)}, u32[]{:S(2)}) collective-permute-start(bf16[64,1536]{1,0:T(8,128)(2,1)} %refs_0_.1), channel_id=1, source_target_pairs={{0,4},{1,5},{2,6},{3,7},{4,0},{5,1},{6,2},{7,3},{8,12},{9,13},{10,... | collective-permute-start | bytes 589832 | tf_op jit(solution)/shard_map/ppermute | solution.py:320
  6.3 1.1 convert_reduce_fusion.2
  7.4 1.6 collective-permute-start
  9.0 2.6 %collective-permute-done.1.refs_1_ = bf16[64,1536]{1,0:T(8,128)(2,1)S(1)} collective-permute-done((bf16[64,1536]{1,0:T(8,128)(2,1)}, bf16[64,1536]{1,0:T(8,128)(2,1)S(1)}, u32[]{:S(2)}, u32[]{:S(2)}) %collective-permute-start.1) | collective-permute-done | bytes 196640 | tf_op jit(solution)/shard_map/ppermute | solution.py:320
  11.6 1.4 collective-permute-done.3.refs_3_
  13.0 0.9 copy-done.7
  14.0 3.7 %grad_act_w_go.1 = (bf16[256,1536]{1,0:T(8,128)(2,1)S(1)}, bf16[1536,1536]{1,0:T(8,128)(2,1)S(1)}, bf16[256,1536]{1,0:T(8,128)(2,1)S(1)}) custom-call(s32[1]{0:T(128)} %bitcast.me_ref, bf16[64,1536]{1,0:T(8,128)(2,1)S(1)} %copy-done.7, bf16[64,1536]{1,0:T(8,128)(2,1)S(1)} %collective-permute-done.1.refs_1_, ...), custom_call_target="tpu_custom_call" | custom-call | tf_op jit(solution)/shard_map/grad_act_w_go/pallas_call | solution.py:94
  17.7 1.9 %collective-permute-start.9 = (bf16[256,1536]{1,0:T(8,128)(2,1)S(1)}, bf16[256,1536]{1,0:T(8,128)(2,1)S(1)}, u32[]{:S(2)}, u32[]{:S(2)}) collective-permute-start(bf16[256,1536]{1,0:T(8,128)(2,1)S(1)} %get-tuple-element.60), channel_id=1, source_target_pairs={{0,8},{1,17},{2,10},{3,19},{4,12},{5,21},{6,14},{7,23},{8,0},{9,25... | collective-permute-start | bytes 2359304 | tf_op jit(solution)/shard_map/ppermute | solution.py:314
  19.6 1.5 collective-permute-start.4
  21.2 2.0 %collective-permute-done.4 = f32[2,64]{1,0:T(2,128)S(1)} collective-permute-done((f32[2,64]{1,0:T(2,128)S(1)}, f32[2,64]{1,0:T(2,128)S(1)}, u32[]{:S(2)}, u32[]{:S(2)}) %collective-permute-start.4) | collective-permute-done | bytes 544 | tf_op jit(solution)/shard_map/ppermute | solution.py:323
  23.4 1.3 collective-permute-start.14
  24.7 2.1 %collective-permute-done.6 = bf16[64,1536]{1,0:T(8,128)(2,1)S(1)} collective-permute-done((bf16[64,1536]{1,0:T(8,128)(2,1)S(1)}, bf16[64,1536]{1,0:T(8,128)(2,1)S(1)}, u32[]{:S(2)}, u32[]{:S(2)}) %collective-permute-start.6) | collective-permute-done | bytes 196640 | tf_op jit(solution)/shard_map/ppermute | solution.py:320
  26.9 3.5 %collective-permute-start.7 = (bf16[128,1536]{1,0:T(8,128)(2,1)S(1)}, bf16[128,1536]{1,0:T(8,128)(2,1)S(1)}, u32[]{:S(2)}, u32[]{:S(2)}) collective-permute-start(bf16[128,1536]{1,0:T(8,128)(2,1)S(1)} %constant_dynamic-update-slice_fusion.refs_0_), channel_id=1, source_target_pairs={{0,1},{1,0},{2,3},{3,2},{4,5},{5,4},{6,7},{7,6},{8,9},{9,8},{10,11... | collective-permute-start | bytes 1179656 | tf_op jit(solution)/shard_map/ppermute | solution.py:320
  30.3 3.7 %grad_act_w_keep.1 = (f32[256,1536]{1,0:T(8,128)S(1)}, bf16[1536,1536]{1,0:T(8,128)(2,1)S(1)}) custom-call(s32[1]{0:T(128)} %bitcast.me_ref, bf16[256,1536]{1,0:T(8,128)(2,1)S(1)} %get-tuple-element.64.refs_0_.c0, bf16[3072,1536]{1,0:T(8,128)(2,1)} %w_ref.7), custom_call_target="tpu_custom_call" | custom-call | tf_op jit(solution)/shard_map/grad_act_w_keep/pallas_call | solution.py:94
  34.0 2.4 %collective-permute-start.8 = (bf16[64,1536]{1,0:T(8,128)(2,1)S(1)}, bf16[64,1536]{1,0:T(8,128)(2,1)S(1)}, u32[]{:S(2)}, u32[]{:S(2)}) collective-permute-start(bf16[64,1536]{1,0:T(8,128)(2,1)S(1)} %fusion.17.refs_0_), channel_id=1, source_target_pairs={{0,2},{1,3},{2,0},{3,1},{4,6},{5,7},{6,4},{7,5},{8,10},{9,11},{10,... | collective-permute-start | bytes 589832 | tf_op jit(solution)/shard_map/ppermute | solution.py:320
  36.7 2.6 %grad_act_x.1 = (bf16[256,1536]{1,0:T(8,128)(2,1)S(1)}, f32[256,1536]{1,0:T(8,128)S(1)}, bf16[256,1536]{1,0:T(8,128)(2,1)S(1)}) custom-call(bf16[128,1536]{1,0:T(8,128)(2,1)S(1)} %constant_dynamic-update-slice_fusion.refs_0_, bf16[128,1536]{1,0:T(8,128)(2,1)S(1)} %collective-permute-done.7.refs_1_, bf16[1536,1536]{1,0:T(8,128)(2,1)S(1)} %get-tuple-element.63.refs_2_, ...), custom_call_target="tpu_custom_call" | custom-call | tf_op jit(solution)/shard_map/grad_act_x/pallas_call | solution.py:117
  39.3 1.6 collective-permute-start.13
  40.9 1.0 add_convert_fusion.3
  42.2 3.6 %collective-permute-done.15 = bf16[64,1536]{1,0:T(8,128)(2,1)S(1)} collective-permute-done((bf16[64,1536]{1,0:T(8,128)(2,1)S(1)}, bf16[64,1536]{1,0:T(8,128)(2,1)S(1)}, u32[]{:S(2)}, u32[]{:S(2)}) %collective-permute-start.15) | collective-permute-done | bytes 196640 | tf_op jit(solution)/shard_map/ppermute | solution.py:320
  45.9 3.6 %hidden_w_go.1 = (bf16[256,1536]{1,0:T(8,128)(2,1)S(1)}, bf16[1536,1536]{1,0:T(8,128)(2,1)S(1)}, bf16[256,1536]{1,0:T(8,128)(2,1)S(1)}) custom-call(s32[1]{0:T(128)} %bitcast.me_ref, bf16[64,1536]{1,0:T(8,128)(2,1)S(1)} %fusion.17.refs_0_, bf16[64,1536]{1,0:T(8,128)(2,1)S(1)} %collective-permute-done.8.refs_1_, ...), custom_call_target="tpu_custom_call" | custom-call | tf_op jit(solution)/shard_map/hidden_w_go/pallas_call | solution.py:94
  49.6 1.6 collective-permute-start.12
  51.1 3.6 %hidden_w_keep.1 = (f32[256,1536]{1,0:T(8,128)S(1)}, bf16[1536,1536]{1,0:T(8,128)(2,1)S(1)}) custom-call(s32[1]{0:T(128)} %bitcast.me_ref, bf16[256,1536]{1,0:T(8,128)(2,1)S(1)} %get-tuple-element.108.refs_0_.n_ref.n0, bf16[1536,3072]{1,0:T(8,128)(2,1)} %w_ref.6), custom_call_target="tpu_custom_call" | custom-call | tf_op jit(solution)/shard_map/hidden_w_keep/pallas_call | solution.py:94
  54.8 2.6 %hidden_x.1 = (bf16[256,1536]{1,0:T(8,128)(2,1)}, f32[256,1536]{1,0:T(8,128)S(1)}, bf16[256,1536]{1,0:T(8,128)(2,1)S(1)}) custom-call(bf16[128,1536]{1,0:T(8,128)(2,1)S(1)} %constant_dynamic-update-slice_fusion.2.refs_0_, bf16[128,1536]{1,0:T(8,128)(2,1)S(1)} %collective-permute-done.16.refs_1_, bf16[1536,1536]{1,0:T(8,128)(2,1)S(1)} %get-tuple-element.74.refs_2_, ...), custom_call_target="tpu_custom_call" | custom-call | tf_op jit(solution)/shard_map/hidden_x/pallas_call | solution.py:117
  57.4 1.1 copy-done.4
  59.1 0.9 add_convert_fusion.2
  60.0 1.5 collective-permute-start.22
  61.6 1.0 add_convert_fusion.1
  62.6 1.5 collective-permute-start.17
  65.5 6.9 %collective-permute-done.22 = bf16[256,768]{1,0:T(8,128)(2,1)} collective-permute-done((bf16[256,768]{1,0:T(8,128)(2,1)}, bf16[256,768]{1,0:T(8,128)(2,1)}, u32[]{:S(2)}, u32[]{:S(2)}) %collective-permute-start.22) | collective-permute-done | bytes 393248 | tf_op jit(solution)/shard_map/ppermute | solution.py:317
  72.4 6.5 %collective-permute-done.18 = bf16[256,1536]{1,0:T(8,128)(2,1)} collective-permute-done((bf16[256,1536]{1,0:T(8,128)(2,1)}, bf16[256,1536]{1,0:T(8,128)(2,1)}, u32[]{:S(2)}, u32[]{:S(2)}) %collective-permute-start.18) | collective-permute-done | bytes 786464 | tf_op jit(solution)/shard_map/ppermute | solution.py:314
  78.9 1.3 add_convert_fusion
  80.2 1.6 collective-permute-start.20
  81.8 0.9 collective-permute-done.23
  82.8 2.2 %fusion.5 = (bf16[256,768]{1,0:T(8,128)(2,1)S(1)}, bf16[256,768]{1,0:T(8,128)(2,1)S(1)}) fusion(bf16[256,768]{1,0:T(8,128)(2,1)} %collective-permute-done.23, f32[256,1536]{1,0:T(8,128)S(1)} %copy-done.1, bf16[256,1536]{1,0:T(8,128)(2,1)} %copy-done.9, f32[768]{0:T(1024)S(1)} %dynamic_slice.3, bf16[256,768]{1,0:T(8,128)(2,1)} %collective-permute-done.17, ...), kind=kLoop, calls=%fused_computation.9 | loop fusion | flops 4128768 | bytes 3935232 | tf_op jit(solution)/shard_map/convert_element_type | solution.py:405
  85.0 1.6 collective-permute-start.25
  87.1 1.0 collective-permute-done.20
  88.1 1.7 fusion.11
  90.4 1.6 collective-permute-start.21
  92.9 4.2 %collective-permute-done.19 = bf16[256,768]{1,0:T(8,128)(2,1)S(1)} collective-permute-done((bf16[256,768]{1,0:T(8,128)(2,1)S(1)}, bf16[256,768]{1,0:T(8,128)(2,1)S(1)}, u32[]{:S(2)}, u32[]{:S(2)}) %collective-permute-start.19) | collective-permute-done | bytes 393248 | tf_op jit(solution)/shard_map/ppermute | solution.py:314
  97.1 4.2 %collective-permute-done.24 = bf16[256,768]{1,0:T(8,128)(2,1)S(1)} collective-permute-done((bf16[256,768]{1,0:T(8,128)(2,1)S(1)}, bf16[256,768]{1,0:T(8,128)(2,1)S(1)}, u32[]{:S(2)}, u32[]{:S(2)}) %collective-permute-start.24) | collective-permute-done | bytes 393248 | tf_op jit(solution)/shard_map/ppermute | solution.py:314
  101.3 1.1 collective-permute-start.29
  102.4 4.7 %collective-permute-done.21 = bf16[256,768]{1,0:T(8,128)(2,1)S(1)} collective-permute-done((bf16[256,768]{1,0:T(8,128)(2,1)S(1)}, bf16[256,768]{1,0:T(8,128)(2,1)S(1)}, u32[]{:S(2)}, u32[]{:S(2)}) %collective-permute-start.21) | collective-permute-done | bytes 393248 | tf_op jit(solution)/shard_map/ppermute | solution.py:314
  107.9 1.4 collective-permute-start.27
  109.4 5.5 %wgrad_near.1.refs_0_ = f32[3072,1536]{1,0:T(8,128)} custom-call(s32[1]{0:T(128)} %bitcast.me_ref, bf16[256,1536]{1,0:T(8,128)(2,1)S(1)} %pad_maximum_fusion.p0.near_ref, bf16[256,1536]{1,0:T(8,128)(2,1)S(1)} %pad_maximum_fusion.3.p1.near_ref, bf16[256,1536]{1,0:T(8,128)(2,1)S(1)} %get-tuple-element.64.refs_0_.c0, bf16[256,1536]{1,0:T(8,128)(2,1)S(1)} %get-tuple-element.86.c1), custom_call_target="tpu_custom_call" | custom-call | tf_op jit(solution)/shard_map/wgrad_near/pallas_call | solution.py:235
  114.8 1.2 slice-done.1
  116.3 2.7 %normed_grad_x.1 = (f32[128,1536]{1,0:T(8,128)S(1)}, bf16[128,1536]{1,0:T(8,128)(2,1)S(1)}, f32[1,1536]{1,0:T(1,128)S(1)}) custom-call(s32[1]{0:T(128)} %bitcast.me_ref, bf16[256,1536]{1,0:T(8,128)(2,1)S(1)} %pad_maximum_fusion.2.near_ref.near1, bf16[256,1536]{1,0:T(8,128)(2,1)S(1)} %collective-permute-done.29.far_ref.far1, bf16[1536,3072]{1,0:T(8,128)(2,1)S(1)} %bitcast.21, ...), custom_call_target="tpu_custom_call" | custom-call | tf_op jit(solution)/shard_map/normed_grad_x/pallas_call | solution.py:188
  120.6 1.3 collective-permute-done.28.far_ref.p1
  121.9 2.6 %mlp_x.1 = (f32[128,1536]{1,0:T(8,128)S(1)}, bf16[128,1536]{1,0:T(8,128)(2,1)S(1)}) custom-call(s32[1]{0:T(128)} %bitcast.me_ref, bf16[256,1536]{1,0:T(8,128)(2,1)S(1)} %pad_maximum_fusion.3.p1.near_ref, bf16[256,1536]{1,0:T(8,128)(2,1)S(1)} %collective-permute-done.28.far_ref.p1, bf16[3072,1536]{1,0:T(8,128)(2,1)S(1)} %bitcast.23), custom_call_target="tpu_custom_call" | custom-call | tf_op jit(solution)/shard_map/mlp_x/pallas_call | solution.py:154
  125.1 5.2 %collective-permute-done.27.far_ref.far0 = bf16[256,1536]{1,0:T(8,128)(2,1)S(1)} collective-permute-done((bf16[256,1536]{1,0:T(8,128)(2,1)S(1)}, bf16[256,1536]{1,0:T(8,128)(2,1)S(1)}, u32[]{:S(2)}, u32[]{:S(2)}) %collective-permute-start.27) | collective-permute-done | bytes 786464 | tf_op jit(solution)/shard_map/ppermute | solution.py:317
  130.3 2.7 %normed_grad_w.1 = (f32[128,1536]{1,0:T(8,128)S(1)}, bf16[144,1536]{1,0:T(8,128)(2,1)S(1)}, f32[1,1536]{1,0:T(1,128)S(1)}) custom-call(s32[1]{0:T(128)} %bitcast.me_ref, bf16[256,1536]{1,0:T(8,128)(2,1)S(1)} %pad_maximum_fusion.1.near_ref.near0, bf16[256,1536]{1,0:T(8,128)(2,1)S(1)} %collective-permute-done.27.far_ref.far0, bf16[1536,3072]{1,0:T(8,128)(2,1)S(1)} %bitcast.21, ...), custom_call_target="tpu_custom_call" | custom-call | tf_op jit(solution)/shard_map/normed_grad_w/pallas_call | solution.py:188
  133.8 1.8 %collective-permute-start.33 = (bf16[64,1536]{1,0:T(8,128)(2,1)S(1)}, bf16[64,1536]{1,0:T(8,128)(2,1)S(1)}, u32[]{:S(2)}, u32[]{:S(2)}) collective-permute-start(bf16[64,1536]{1,0:T(8,128)(2,1)S(1)} %slice.227), channel_id=1, source_target_pairs={{0,2},{1,3},{2,0},{3,1},{4,6},{5,7},{6,4},{7,5},{8,10},{9,11},{10,... | collective-permute-start | bytes 589832 | tf_op jit(solution)/shard_map/ppermute | solution.py:320
  135.9 6.3 %wgrad_up_1.1 = (f32[1536,3072]{1,0:T(8,128)}, f32[1,3072]{1,0:T(1,128)}) custom-call(s32[1]{0:T(128)} %bitcast.me_ref, bf16[256,1536]{1,0:T(8,128)(2,1)S(1)} %get-tuple-element.108.refs_0_.n_ref.n0, bf16[256,1536]{1,0:T(8,128)(2,1)S(1)} %get-tuple-element.88.n_ref.n1, bf16[256,1536]{1,0:T(8,128)(2,1)S(1)} %pad_maximum_fusion.1.near_ref.near0, ...), custom_call_target="tpu_custom_call" | custom-call | tf_op jit(solution)/shard_map/wgrad_up_1/pallas_call | solution.py:284
  142.6 1.8 %collective-permute-start.37 = (bf16[80,1536]{1,0:T(8,128)(2,1)S(1)}, bf16[80,1536]{1,0:T(8,128)(2,1)S(1)}, u32[]{:S(2)}, u32[]{:S(2)}) collective-permute-start(bf16[80,1536]{1,0:T(8,128)(2,1)S(1)} %pad_maximum_fusion.4), channel_id=1, source_target_pairs={{0,2},{1,3},{2,0},{3,1},{4,6},{5,7},{6,4},{7,5},{8,10},{9,11},{10,... | collective-permute-start | bytes 737288 | tf_op jit(solution)/shard_map/ppermute | solution.py:320
  145.1 1.5 collective-permute-start.38
  146.6 2.6 %mlp_w.1 = (f32[128,1536]{1,0:T(8,128)S(1)}, bf16[128,1536]{1,0:T(8,128)(2,1)S(1)}) custom-call(s32[1]{0:T(128)} %bitcast.me_ref, bf16[256,1536]{1,0:T(8,128)(2,1)S(1)} %pad_maximum_fusion.p0.near_ref, bf16[256,1536]{1,0:T(8,128)(2,1)S(1)} %collective-permute-done.26.far_ref.p0, bf16[3072,1536]{1,0:T(8,128)(2,1)S(1)} %bitcast.23), custom_call_target="tpu_custom_call" | custom-call | tf_op jit(solution)/shard_map/mlp_w/pallas_call | solution.py:154
  149.3 5.2 %wgrad_far.1 = f32[3072,1536]{1,0:T(8,128)} custom-call(s32[1]{0:T(128)} %bitcast.me_ref, bf16[256,1536]{1,0:T(8,128)(2,1)S(1)} %collective-permute-done.26.far_ref.p0, bf16[256,1536]{1,0:T(8,128)(2,1)S(1)} %collective-permute-done.28.far_ref.p1, bf16[256,1536]{1,0:T(8,128)(2,1)S(1)} %get-tuple-element.64.refs_0_.c0, ...), custom_call_target="tpu_custom_call", output_to_operand_aliasing={{}: (5, {})} | custom-call | tf_op jit(solution)/shard_map/wgrad_far/pallas_call | solution.py:235
  154.6 1.5 collective-permute-start.39
  156.2 1.5 collective-permute-start.42
  158.0 1.6 collective-permute-start.40
  159.6 5.4 %wgrad_up_2.1 = f32[1536,3072]{1,0:T(8,128)} custom-call(s32[1]{0:T(128)} %bitcast.me_ref, bf16[256,1536]{1,0:T(8,128)(2,1)S(1)} %get-tuple-element.108.refs_0_.n_ref.n0, bf16[256,1536]{1,0:T(8,128)(2,1)S(1)} %get-tuple-element.88.n_ref.n1, bf16[256,1536]{1,0:T(8,128)(2,1)S(1)} %pad_maximum_fusion.1.near_ref.near0, ...), custom_call_target="tpu_custom_call", output_to_operand_aliasing={{}: (7, {})} | custom-call | tf_op jit(solution)/shard_map/wgrad_up_2/pallas_call | solution.py:284
  165.0 1.1 collective-permute-start.41
  166.2 1.1 collective-permute-done.42
  169.6 5.0 %collective-permute-done.36 = bf16[64,1536]{1,0:T(8,128)(2,1)S(1)} collective-permute-done((bf16[64,1536]{1,0:T(8,128)(2,1)S(1)}, bf16[64,1536]{1,0:T(8,128)(2,1)S(1)}, u32[]{:S(2)}, u32[]{:S(2)}) %collective-permute-start.36) | collective-permute-done | bytes 196640 | tf_op jit(solution)/shard_map/ppermute | solution.py:320
  (133 shorter events, 13.8 us)
Async XLA Ops:
  0.6 11.0 %collective-permute-start.1 = (bf16[64,1536]{1,0:T(8,128)(2,1)}, bf16[64,1536]{1,0:T(8,128)(2,1)S(1)}, u32[]{:S(2)}, u32[]{:S(2)}) collective-permute-start(bf16[64,1536]{1,0:T(8,128)(2,1)} %refs_0_.1), channel_id=1, source_target_pairs={{0,2},{1,3},{2,0},{3,1},{4,6},{5,7},{6,4},{7,5},{8,10},{9,11},{10,... | collective-permute-start | bytes 589832 | tf_op jit(solution)/shard_map/ppermute | solution.py:320
  3.7 7.9 %collective-permute-start.2 = (bf16[64,1536]{1,0:T(8,128)(2,1)}, bf16[64,1536]{1,0:T(8,128)(2,1)S(1)}, u32[]{:S(2)}, u32[]{:S(2)}) collective-permute-start(bf16[64,1536]{1,0:T(8,128)(2,1)} %refs_0_.1), channel_id=1, source_target_pairs={{0,1},{1,0},{2,3},{3,2},{4,5},{5,4},{6,7},{7,6},{8,9},{9,8},{10,11... | collective-permute-start | bytes 589832 | tf_op jit(solution)/shard_map/ppermute | solution.py:320
  3.7 17.4 %collective-permute-start.5 = (bf16[64,1536]{1,0:T(8,128)(2,1)}, bf16[64,1536]{1,0:T(8,128)(2,1)S(1)}, u32[]{:S(2)}, u32[]{:S(2)}) collective-permute-start(bf16[64,1536]{1,0:T(8,128)(2,1)} %refs_0_.1), channel_id=1, source_target_pairs={{0,4},{1,5},{2,6},{3,7},{4,0},{5,1},{6,2},{7,3},{8,12},{9,13},{10,... | collective-permute-start | bytes 589832 | tf_op jit(solution)/shard_map/ppermute | solution.py:320
  7.4 4.2 %collective-permute-start = (f32[2,64]{1,0:T(2,128)S(1)}, f32[2,64]{1,0:T(2,128)S(1)}, u32[]{:S(2)}, u32[]{:S(2)}) collective-permute-start(f32[2,64]{1,0:T(2,128)S(1)} %pad_maximum_fusion.5), channel_id=1, source_target_pairs={{0,8},{8,0},{16,24},{24,16},{1,9},{9,1},{17,25},{25,17},{2,10},{10... | collective-permute-start | bytes 1544 | tf_op jit(solution)/shard_map/ppermute | solution.py:323
  11.6 1.4 collective-permute-start.3
  13.0 0.9 copy-start.7
  14.0 9.3 %copy-start.8 = (bf16[64,1536]{1,0:T(8,128)(2,1)S(1)}, bf16[64,1536]{1,0:T(8,128)(2,1)}, u32[]{:S(2)}) copy-start(bf16[64,1536]{1,0:T(8,128)(2,1)} %param.7) | copy-start | bytes 589828
  14.0 9.3 %copy-start.13 = (f32[1536]{0:T(1024)S(1)}, f32[1536]{0:T(1024)}, u32[]{:S(2)}) copy-start(f32[1536]{0:T(1024)} %param.8) | copy-start | bytes 18436
  17.7 23.2 %collective-permute-start.9 = (bf16[256,1536]{1,0:T(8,128)(2,1)S(1)}, bf16[256,1536]{1,0:T(8,128)(2,1)S(1)}, u32[]{:S(2)}, u32[]{:S(2)}) collective-permute-start(bf16[256,1536]{1,0:T(8,128)(2,1)S(1)} %get-tuple-element.60), channel_id=1, source_target_pairs={{0,8},{1,17},{2,10},{3,19},{4,12},{5,21},{6,14},{7,23},{8,0},{9,25... | collective-permute-start | bytes 2359304 | tf_op jit(solution)/shard_map/ppermute | solution.py:314
  19.6 3.6 %collective-permute-start.4 = (f32[2,64]{1,0:T(2,128)S(1)}, f32[2,64]{1,0:T(2,128)S(1)}, u32[]{:S(2)}, u32[]{:S(2)}) collective-permute-start(f32[2,64]{1,0:T(2,128)S(1)} %fusion.32), channel_id=1, source_target_pairs={{0,16},{8,24},{16,0},{24,8},{1,17},{9,25},{17,1},{25,9},{2,18},{10... | collective-permute-start | bytes 1544 | tf_op jit(solution)/shard_map/ppermute | solution.py:323
  21.1 5.7 %collective-permute-start.6 = (bf16[64,1536]{1,0:T(8,128)(2,1)S(1)}, bf16[64,1536]{1,0:T(8,128)(2,1)S(1)}, u32[]{:S(2)}, u32[]{:S(2)}) collective-permute-start(bf16[64,1536]{1,0:T(8,128)(2,1)S(1)} %collective-permute-done.5), channel_id=1, source_target_pairs={{0,2},{1,3},{2,0},{3,1},{4,6},{5,7},{6,4},{7,5},{8,10},{9,11},{10,... | collective-permute-start | bytes 589832 | tf_op jit(solution)/shard_map/ppermute | solution.py:320
  23.4 13.1 %collective-permute-start.14 = (bf16[64,1536]{1,0:T(8,128)(2,1)S(1)}, bf16[64,1536]{1,0:T(8,128)(2,1)S(1)}, u32[]{:S(2)}, u32[]{:S(2)}) collective-permute-start(bf16[64,1536]{1,0:T(8,128)(2,1)S(1)} %fusion.17.refs_0_), channel_id=1, source_target_pairs={{0,4},{1,5},{2,6},{3,7},{4,0},{5,1},{6,2},{7,3},{8,12},{9,13},{10,... | collective-permute-start | bytes 589832 | tf_op jit(solution)/shard_map/ppermute | solution.py:320
  26.9 9.8 %collective-permute-start.7 = (bf16[128,1536]{1,0:T(8,128)(2,1)S(1)}, bf16[128,1536]{1,0:T(8,128)(2,1)S(1)}, u32[]{:S(2)}, u32[]{:S(2)}) collective-permute-start(bf16[128,1536]{1,0:T(8,128)(2,1)S(1)} %constant_dynamic-update-slice_fusion.refs_0_), channel_id=1, source_target_pairs={{0,1},{1,0},{2,3},{3,2},{4,5},{5,4},{6,7},{7,6},{8,9},{9,8},{10,11... | collective-permute-start | bytes 1179656 | tf_op jit(solution)/shard_map/ppermute | solution.py:320
  34.0 6.9 %copy-start = (f32[256,1536]{1,0:T(8,128)}, f32[256,1536]{1,0:T(8,128)S(1)}, u32[]{:S(2)}) copy-start(f32[256,1536]{1,0:T(8,128)S(1)} %get-tuple-element.68) | copy-start | bytes 4718596
  34.0 8.1 %collective-permute-start.8 = (bf16[64,1536]{1,0:T(8,128)(2,1)S(1)}, bf16[64,1536]{1,0:T(8,128)(2,1)S(1)}, u32[]{:S(2)}, u32[]{:S(2)}) collective-permute-start(bf16[64,1536]{1,0:T(8,128)(2,1)S(1)} %fusion.17.refs_0_), channel_id=1, source_target_pairs={{0,2},{1,3},{2,0},{3,1},{4,6},{5,7},{6,4},{7,5},{8,10},{9,11},{10,... | collective-permute-start | bytes 589832 | tf_op jit(solution)/shard_map/ppermute | solution.py:320
  36.5 9.4 %collective-permute-start.10 = (bf16[64,1536]{1,0:T(8,128)(2,1)S(1)}, bf16[64,1536]{1,0:T(8,128)(2,1)S(1)}, u32[]{:S(2)}, u32[]{:S(2)}) collective-permute-start(bf16[64,1536]{1,0:T(8,128)(2,1)S(1)} %fusion.17.refs_0_), channel_id=1, source_target_pairs={{0,1},{1,0},{2,3},{3,2},{4,5},{5,4},{6,7},{7,6},{8,9},{9,8},{10,11... | collective-permute-start | bytes 589832 | tf_op jit(solution)/shard_map/ppermute | solution.py:320
  36.5 9.3 %collective-permute-start.15 = (bf16[64,1536]{1,0:T(8,128)(2,1)S(1)}, bf16[64,1536]{1,0:T(8,128)(2,1)S(1)}, u32[]{:S(2)}, u32[]{:S(2)}) collective-permute-start(bf16[64,1536]{1,0:T(8,128)(2,1)S(1)} %collective-permute-done.14), channel_id=1, source_target_pairs={{0,2},{1,3},{2,0},{3,1},{4,6},{5,7},{6,4},{7,5},{8,10},{9,11},{10,... | collective-permute-start | bytes 589832 | tf_op jit(solution)/shard_map/ppermute | solution.py:320
  39.3 19.8 %copy-start.2 = (f32[256,1536]{1,0:T(8,128)}, f32[256,1536]{1,0:T(8,128)S(1)}, u32[]{:S(2)}) copy-start(f32[256,1536]{1,0:T(8,128)S(1)} %get-tuple-element.73) | copy-start | bytes 4718596
  39.3 19.8 %collective-permute-start.13 = (bf16[256,1536]{1,0:T(8,128)(2,1)S(1)}, bf16[256,1536]{1,0:T(8,128)(2,1)S(1)}, u32[]{:S(2)}, u32[]{:S(2)}) collective-permute-start(bf16[256,1536]{1,0:T(8,128)(2,1)S(1)} %get-tuple-element.66), channel_id=1, source_target_pairs={{0,8},{1,17},{2,10},{3,19},{4,12},{5,21},{6,14},{7,23},{8,0},{9,25... | collective-permute-start | bytes 2359304 | tf_op jit(solution)/shard_map/ppermute | solution.py:314
  40.9 8.7 %copy-start.9 = (bf16[256,1536]{1,0:T(8,128)(2,1)}, bf16[256,1536]{1,0:T(8,128)(2,1)S(1)}, u32[]{:S(2)}) copy-start(bf16[256,1536]{1,0:T(8,128)(2,1)S(1)} %collective-permute-done.9) | copy-start | bytes 2359300
  42.2 3.7 %collective-permute-start.11 = (bf16[64,1536]{1,0:T(8,128)(2,1)S(1)}, bf16[64,1536]{1,0:T(8,128)(2,1)S(1)}, u32[]{:S(2)}, u32[]{:S(2)}) collective-permute-start(bf16[64,1536]{1,0:T(8,128)(2,1)S(1)} %collective-permute-done.8.refs_1_), channel_id=1, source_target_pairs={{0,1},{1,0},{2,3},{3,2},{4,5},{5,4},{6,7},{7,6},{8,9},{9,8},{10,11... | collective-permute-start | bytes 589832 | tf_op jit(solution)/shard_map/ppermute | solution.py:320
  45.8 9.0 %collective-permute-start.16 = (bf16[128,1536]{1,0:T(8,128)(2,1)S(1)}, bf16[128,1536]{1,0:T(8,128)(2,1)S(1)}, u32[]{:S(2)}, u32[]{:S(2)}) collective-permute-start(bf16[128,1536]{1,0:T(8,128)(2,1)S(1)} %constant_dynamic-update-slice_fusion.2.refs_0_), channel_id=1, source_target_pairs={{0,1},{1,0},{2,3},{3,2},{4,5},{5,4},{6,7},{7,6},{8,9},{9,8},{10,11... | collective-permute-start | bytes 1179656 | tf_op jit(solution)/shard_map/ppermute | solution.py:320
  49.6 12.1 %collective-permute-start.12 = (bf16[256,1536]{1,0:T(8,128)(2,1)S(1)}, bf16[256,1536]{1,0:T(8,128)(2,1)S(1)}, u32[]{:S(2)}, u32[]{:S(2)}) collective-permute-start(bf16[256,1536]{1,0:T(8,128)(2,1)S(1)} %get-tuple-element.72), channel_id=1, source_target_pairs={{0,8},{1,17},{2,10},{3,19},{4,12},{5,21},{6,14},{7,23},{8,0},{9,25... | collective-permute-start | bytes 2359304 | tf_op jit(solution)/shard_map/ppermute | solution.py:314
  54.8 6.9 %copy-start.6 = (f32[256,1536]{1,0:T(8,128)}, f32[256,1536]{1,0:T(8,128)S(1)}, u32[]{:S(2)}) copy-start(f32[256,1536]{1,0:T(8,128)S(1)} %get-tuple-element.71) | copy-start | bytes 4718596
  57.4 1.1 copy-start.4
  58.5 20.4 %collective-permute-start.18 = (bf16[256,1536]{1,0:T(8,128)(2,1)}, bf16[256,1536]{1,0:T(8,128)(2,1)}, u32[]{:S(2)}, u32[]{:S(2)}) collective-permute-start(bf16[256,1536]{1,0:T(8,128)(2,1)} %get-tuple-element.76), channel_id=1, source_target_pairs={{0,8},{1,17},{2,10},{3,19},{4,12},{5,21},{6,14},{7,23},{8,0},{9,25... | collective-permute-start | bytes 2359304 | tf_op jit(solution)/shard_map/ppermute | solution.py:314
  59.1 3.5 %copy-start.10 = (bf16[256,1536]{1,0:T(8,128)(2,1)}, bf16[256,1536]{1,0:T(8,128)(2,1)S(1)}, u32[]{:S(2)}) copy-start(bf16[256,1536]{1,0:T(8,128)(2,1)S(1)} %collective-permute-done.13) | copy-start | bytes 2359300
  60.0 12.4 %collective-permute-start.22 = (bf16[256,768]{1,0:T(8,128)(2,1)}, bf16[256,768]{1,0:T(8,128)(2,1)}, u32[]{:S(2)}, u32[]{:S(2)}) collective-permute-start(bf16[256,768]{1,0:T(8,128)(2,1)} %add_convert_fusion.2), channel_id=1, source_target_pairs={{0,16},{1,9},{2,18},{3,11},{4,20},{5,13},{6,22},{7,15},{8,24},{9,1... | collective-permute-start | bytes 1179656 | tf_op jit(solution)/shard_map/ppermute | solution.py:317
  61.6 2.5 %copy-start.12 = (bf16[256,1536]{1,0:T(8,128)(2,1)}, bf16[256,1536]{1,0:T(8,128)(2,1)S(1)}, u32[]{:S(2)}) copy-start(bf16[256,1536]{1,0:T(8,128)(2,1)S(1)} %collective-permute-done.12) | copy-start | bytes 2359300
  62.6 19.2 %collective-permute-start.17 = (bf16[256,768]{1,0:T(8,128)(2,1)}, bf16[256,768]{1,0:T(8,128)(2,1)}, u32[]{:S(2)}, u32[]{:S(2)}) collective-permute-start(bf16[256,768]{1,0:T(8,128)(2,1)} %add_convert_fusion.1), channel_id=1, source_target_pairs={{0,16},{1,9},{2,18},{3,11},{4,20},{5,13},{6,22},{7,15},{8,24},{9,1... | collective-permute-start | bytes 1179656 | tf_op jit(solution)/shard_map/ppermute | solution.py:317
  64.1 18.6 %collective-permute-start.23 = (bf16[256,768]{1,0:T(8,128)(2,1)}, bf16[256,768]{1,0:T(8,128)(2,1)}, u32[]{:S(2)}, u32[]{:S(2)}) collective-permute-start(bf16[256,768]{1,0:T(8,128)(2,1)} %add_convert_fusion.3), channel_id=1, source_target_pairs={{0,16},{1,9},{2,18},{3,11},{4,20},{5,13},{6,22},{7,15},{8,24},{9,1... | collective-permute-start | bytes 1179656 | tf_op jit(solution)/shard_map/ppermute | solution.py:317
  64.6 18.1 %copy-start.1 = (f32[256,1536]{1,0:T(8,128)S(1)}, f32[256,1536]{1,0:T(8,128)}, u32[]{:S(2)}) copy-start(f32[256,1536]{1,0:T(8,128)} %copy-done) | copy-start | bytes 4718596
  80.2 7.9 %copy-start.3 = (f32[256,1536]{1,0:T(8,128)S(1)}, f32[256,1536]{1,0:T(8,128)}, u32[]{:S(2)}) copy-start(f32[256,1536]{1,0:T(8,128)} %copy-done.2) | copy-start | bytes 4718596
  80.2 7.9 %copy-start.5 = (f32[256,1536]{1,0:T(8,128)S(1)}, f32[256,1536]{1,0:T(8,128)}, u32[]{:S(2)}) copy-start(f32[256,1536]{1,0:T(8,128)} %copy-done.4) | copy-start | bytes 4718596
  80.2 7.9 %copy-start.11 = (bf16[256,1536]{1,0:T(8,128)(2,1)S(1)}, bf16[256,1536]{1,0:T(8,128)(2,1)}, u32[]{:S(2)}) copy-start(bf16[256,1536]{1,0:T(8,128)(2,1)} %copy-done.10) | copy-start | bytes 2359300
  80.2 7.8 %collective-permute-start.20 = (bf16[256,768]{1,0:T(8,128)(2,1)S(1)}, bf16[256,768]{1,0:T(8,128)(2,1)S(1)}, u32[]{:S(2)}, u32[]{:S(2)}) collective-permute-start(bf16[256,768]{1,0:T(8,128)(2,1)S(1)} %add_convert_fusion), channel_id=1, source_target_pairs={{0,16},{1,9},{2,18},{3,11},{4,20},{5,13},{6,22},{7,15},{8,24},{9,1... | collective-permute-start | bytes 1179656 | tf_op jit(solution)/shard_map/ppermute | solution.py:317
  85.0 7.8 %collective-permute-start.25 = (bf16[256,768]{1,0:T(8,128)(2,1)S(1)}, bf16[256,768]{1,0:T(8,128)(2,1)S(1)}, u32[]{:S(2)}, u32[]{:S(2)}) collective-permute-start(bf16[256,768]{1,0:T(8,128)(2,1)S(1)} %get-tuple-element.123), channel_id=1, source_target_pairs={{0,8},{1,17},{2,10},{3,19},{4,12},{5,21},{6,14},{7,23},{8,0},{9,25... | collective-permute-start | bytes 1179656 | tf_op jit(solution)/shard_map/ppermute | solution.py:314
  86.5 10.5 %collective-permute-start.19 = (bf16[256,768]{1,0:T(8,128)(2,1)S(1)}, bf16[256,768]{1,0:T(8,128)(2,1)S(1)}, u32[]{:S(2)}, u32[]{:S(2)}) collective-permute-start(bf16[256,768]{1,0:T(8,128)(2,1)S(1)} %get-tuple-element.124), channel_id=1, source_target_pairs={{0,8},{1,17},{2,10},{3,19},{4,12},{5,21},{6,14},{7,23},{8,0},{9,25... | collective-permute-start | bytes 1179656 | tf_op jit(solution)/shard_map/ppermute | solution.py:314
  89.8 11.4 %collective-permute-start.24 = (bf16[256,768]{1,0:T(8,128)(2,1)S(1)}, bf16[256,768]{1,0:T(8,128)(2,1)S(1)}, u32[]{:S(2)}, u32[]{:S(2)}) collective-permute-start(bf16[256,768]{1,0:T(8,128)(2,1)S(1)} %get-tuple-element.121), channel_id=1, source_target_pairs={{0,8},{1,17},{2,10},{3,19},{4,12},{5,21},{6,14},{7,23},{8,0},{9,25... | collective-permute-start | bytes 1179656 | tf_op jit(solution)/shard_map/ppermute | solution.py:314
  90.4 16.8 %collective-permute-start.21 = (bf16[256,768]{1,0:T(8,128)(2,1)S(1)}, bf16[256,768]{1,0:T(8,128)(2,1)S(1)}, u32[]{:S(2)}, u32[]{:S(2)}) collective-permute-start(bf16[256,768]{1,0:T(8,128)(2,1)S(1)} %get-tuple-element.122), channel_id=1, source_target_pairs={{0,8},{1,17},{2,10},{3,19},{4,12},{5,21},{6,14},{7,23},{8,0},{9,25... | collective-permute-start | bytes 1179656 | tf_op jit(solution)/shard_map/ppermute | solution.py:314
  101.3 13.5 %collective-permute-start.29 = (bf16[256,1536]{1,0:T(8,128)(2,1)S(1)}, bf16[256,1536]{1,0:T(8,128)(2,1)S(1)}, u32[]{:S(2)}, u32[]{:S(2)}) collective-permute-start(bf16[256,1536]{1,0:T(8,128)(2,1)S(1)} %pad_maximum_fusion.2.near_ref.near1), channel_id=1, source_target_pairs={{0,16},{1,9},{2,18},{3,11},{4,20},{5,13},{6,22},{7,15},{8,24},{9,1... | collective-permute-start | bytes 2359304 | tf_op jit(solution)/shard_map/ppermute | solution.py:317
  107.2 14.6 %collective-permute-start.28 = (bf16[256,1536]{1,0:T(8,128)(2,1)S(1)}, bf16[256,1536]{1,0:T(8,128)(2,1)S(1)}, u32[]{:S(2)}, u32[]{:S(2)}) collective-permute-start(bf16[256,1536]{1,0:T(8,128)(2,1)S(1)} %pad_maximum_fusion.3.p1.near_ref), channel_id=1, source_target_pairs={{0,16},{1,9},{2,18},{3,11},{4,20},{5,13},{6,22},{7,15},{8,24},{9,1... | collective-permute-start | bytes 2359304 | tf_op jit(solution)/shard_map/ppermute | solution.py:317
  107.9 22.4 %collective-permute-start.27 = (bf16[256,1536]{1,0:T(8,128)(2,1)S(1)}, bf16[256,1536]{1,0:T(8,128)(2,1)S(1)}, u32[]{:S(2)}, u32[]{:S(2)}) collective-permute-start(bf16[256,1536]{1,0:T(8,128)(2,1)S(1)} %pad_maximum_fusion.1.near_ref.near0), channel_id=1, source_target_pairs={{0,16},{1,9},{2,18},{3,11},{4,20},{5,13},{6,22},{7,15},{8,24},{9,1... | collective-permute-start | bytes 2359304 | tf_op jit(solution)/shard_map/ppermute | solution.py:317
  109.3 5.5 %slice-start = ((s8[9437184]{0:T(1024)(128)(4,1)}), s8[4194304]{0:T(1024)(128)(4,1)S(1)}, s32[]{:S(2)}) async-start(s8[9437184]{0:T(1024)(128)(4,1)} %bitcast.20), calls=%async_computation | async-start | bytes 8388608
  109.3 6.7 %slice-start.1 = ((s8[9437184]{0:T(1024)(128)(4,1)}), s8[4194304]{0:T(1024)(128)(4,1)S(1)}, s32[]{:S(2)}) async-start(s8[9437184]{0:T(1024)(128)(4,1)} %bitcast.20), calls=%async_computation.1 | async-start | bytes 8388608
  109.3 6.9 %slice-start.2 = ((s8[9437184]{0:T(1024)(128)(4,1)}), s8[1048576]{0:T(1024)(128)(4,1)S(1)}, s32[]{:S(2)}) async-start(s8[9437184]{0:T(1024)(128)(4,1)} %bitcast.20), calls=%async_computation.2 | async-start | bytes 2097152
  109.3 12.5 %slice-start.3 = ((s8[9437184]{0:T(1024)(128)(4,1)}), s8[4194304]{0:T(1024)(128)(4,1)S(1)}, s32[]{:S(2)}) async-start(s8[9437184]{0:T(1024)(128)(4,1)} %bitcast.22), calls=%async_computation.3 | async-start | bytes 8388608
  109.3 12.5 %slice-start.4 = ((s8[9437184]{0:T(1024)(128)(4,1)}), s8[4194304]{0:T(1024)(128)(4,1)S(1)}, s32[]{:S(2)}) async-start(s8[9437184]{0:T(1024)(128)(4,1)} %bitcast.22), calls=%async_computation.4 | async-start | bytes 8388608
  116.3 5.6 %slice-start.5 = ((s8[9437184]{0:T(1024)(128)(4,1)}), s8[1048576]{0:T(1024)(128)(4,1)S(1)}, s32[]{:S(2)}) async-start(s8[9437184]{0:T(1024)(128)(4,1)} %bitcast.22), calls=%async_computation.5 | async-start | bytes 2097152
  119.0 14.6 %collective-permute-start.31 = (bf16[128,1536]{1,0:T(8,128)(2,1)S(1)}, bf16[128,1536]{1,0:T(8,128)(2,1)S(1)}, u32[]{:S(2)}, u32[]{:S(2)}) collective-permute-start(bf16[128,1536]{1,0:T(8,128)(2,1)S(1)} %get-tuple-element.89), channel_id=1, source_target_pairs={{0,1},{1,0},{2,3},{3,2},{4,5},{5,4},{6,7},{7,6},{8,9},{9,8},{10,11... | collective-permute-start | bytes 1179656 | tf_op jit(solution)/shard_map/ppermute | solution.py:320
  119.9 26.7 %collective-permute-start.26 = (bf16[256,1536]{1,0:T(8,128)(2,1)S(1)}, bf16[256,1536]{1,0:T(8,128)(2,1)S(1)}, u32[]{:S(2)}, u32[]{:S(2)}) collective-permute-start(bf16[256,1536]{1,0:T(8,128)(2,1)S(1)} %pad_maximum_fusion.p0.near_ref), channel_id=1, source_target_pairs={{0,16},{1,9},{2,18},{3,11},{4,20},{5,13},{6,22},{7,15},{8,24},{9,1... | collective-permute-start | bytes 2359304 | tf_op jit(solution)/shard_map/ppermute | solution.py:317
  124.5 9.2 %collective-permute-start.30 = (bf16[128,1536]{1,0:T(8,128)(2,1)S(1)}, bf16[128,1536]{1,0:T(8,128)(2,1)S(1)}, u32[]{:S(2)}, u32[]{:S(2)}) collective-permute-start(bf16[128,1536]{1,0:T(8,128)(2,1)S(1)} %get-tuple-element.91), channel_id=1, source_target_pairs={{0,1},{1,0},{2,3},{3,2},{4,5},{5,4},{6,7},{7,6},{8,9},{9,8},{10,11... | collective-permute-start | bytes 1179656 | tf_op jit(solution)/shard_map/ppermute | solution.py:320
  133.0 9.3 %collective-permute-start.32 = (bf16[144,1536]{1,0:T(8,128)(2,1)S(1)}, bf16[144,1536]{1,0:T(8,128)(2,1)S(1)}, u32[]{:S(2)}, u32[]{:S(2)}) collective-permute-start(bf16[144,1536]{1,0:T(8,128)(2,1)S(1)} %get-tuple-element.94), channel_id=1, source_target_pairs={{0,1},{1,0},{2,3},{3,2},{4,5},{5,4},{6,7},{7,6},{8,9},{9,8},{10,11... | collective-permute-start | bytes 1327112 | tf_op jit(solution)/shard_map/ppermute | solution.py:320
  133.8 10.6 %collective-permute-start.33 = (bf16[64,1536]{1,0:T(8,128)(2,1)S(1)}, bf16[64,1536]{1,0:T(8,128)(2,1)S(1)}, u32[]{:S(2)}, u32[]{:S(2)}) collective-permute-start(bf16[64,1536]{1,0:T(8,128)(2,1)S(1)} %slice.227), channel_id=1, source_target_pairs={{0,2},{1,3},{2,0},{3,1},{4,6},{5,7},{6,4},{7,5},{8,10},{9,11},{10,... | collective-permute-start | bytes 589832 | tf_op jit(solution)/shard_map/ppermute | solution.py:320
  135.6 9.4 %collective-permute-start.34 = (bf16[64,1536]{1,0:T(8,128)(2,1)S(1)}, bf16[64,1536]{1,0:T(8,128)(2,1)S(1)}, u32[]{:S(2)}, u32[]{:S(2)}) collective-permute-start(bf16[64,1536]{1,0:T(8,128)(2,1)S(1)} %slice.226), channel_id=1, source_target_pairs={{0,2},{1,3},{2,0},{3,1},{4,6},{5,7},{6,4},{7,5},{8,10},{9,11},{10,... | collective-permute-start | bytes 589832 | tf_op jit(solution)/shard_map/ppermute | solution.py:320
  142.6 13.5 %collective-permute-start.37 = (bf16[80,1536]{1,0:T(8,128)(2,1)S(1)}, bf16[80,1536]{1,0:T(8,128)(2,1)S(1)}, u32[]{:S(2)}, u32[]{:S(2)}) collective-permute-start(bf16[80,1536]{1,0:T(8,128)(2,1)S(1)} %pad_maximum_fusion.4), channel_id=1, source_target_pairs={{0,2},{1,3},{2,0},{3,1},{4,6},{5,7},{6,4},{7,5},{8,10},{9,11},{10,... | collective-permute-start | bytes 737288 | tf_op jit(solution)/shard_map/ppermute | solution.py:320
  145.1 12.6 %collective-permute-start.38 = (bf16[64,1536]{1,0:T(8,128)(2,1)S(1)}, bf16[64,1536]{1,0:T(8,128)(2,1)S(1)}, u32[]{:S(2)}, u32[]{:S(2)}) collective-permute-start(bf16[64,1536]{1,0:T(8,128)(2,1)S(1)} %get-tuple-element.128), channel_id=1, source_target_pairs={{0,4},{1,5},{2,6},{3,7},{4,0},{5,1},{6,2},{7,3},{8,12},{9,13},{10,... | collective-permute-start | bytes 589832 | tf_op jit(solution)/shard_map/ppermute | solution.py:320
  149.2 10.3 %collective-permute-start.35 = (bf16[128,1536]{1,0:T(8,128)(2,1)S(1)}, bf16[128,1536]{1,0:T(8,128)(2,1)S(1)}, u32[]{:S(2)}, u32[]{:S(2)}) collective-permute-start(bf16[128,1536]{1,0:T(8,128)(2,1)S(1)} %get-tuple-element.104), channel_id=1, source_target_pairs={{0,1},{1,0},{2,3},{3,2},{4,5},{5,4},{6,7},{7,6},{8,9},{9,8},{10,11... | collective-permute-start | bytes 1179656 | tf_op jit(solution)/shard_map/ppermute | solution.py:320
  154.6 20.0 %collective-permute-start.39 = (bf16[64,1536]{1,0:T(8,128)(2,1)S(1)}, bf16[64,1536]{1,0:T(8,128)(2,1)S(1)}, u32[]{:S(2)}, u32[]{:S(2)}) collective-permute-start(bf16[64,1536]{1,0:T(8,128)(2,1)S(1)} %get-tuple-element.111), channel_id=1, source_target_pairs={{0,4},{1,5},{2,6},{3,7},{4,0},{5,1},{6,2},{7,3},{8,12},{9,13},{10,... | collective-permute-start | bytes 589832 | tf_op jit(solution)/shard_map/ppermute | solution.py:320
  156.2 11.1 %collective-permute-start.42 = (f32[1,1536]{1,0:T(1,128)S(1)}, f32[1,1536]{1,0:T(1,128)S(1)}, u32[]{:S(2)}, u32[]{:S(2)}) collective-permute-start(f32[1,1536]{1,0:T(1,128)S(1)} %fusion.27), channel_id=1, source_target_pairs={{0,4},{1,5},{2,6},{3,7},{4,0},{5,1},{6,2},{7,3},{8,12},{9,13},{10,... | collective-permute-start | bytes 18440 | tf_op jit(solution)/shard_map/ppermute | solution.py:320
  158.0 7.0 %collective-permute-start.40 = (f32[2,64]{1,0:T(2,128)S(1)}, f32[2,64]{1,0:T(2,128)S(1)}, u32[]{:S(2)}, u32[]{:S(2)}) collective-permute-start(f32[2,64]{1,0:T(2,128)S(1)} %pad_maximum_fusion.6), channel_id=1, source_target_pairs={{0,8},{8,0},{16,24},{24,16},{1,9},{9,1},{17,25},{25,17},{2,10},{10... | collective-permute-start | bytes 1544 | tf_op jit(solution)/shard_map/ppermute | solution.py:323
  159.6 14.9 %copy-start.14 = (f32[1536]{0:T(1024)S(1)}, f32[1536]{0:T(1024)}, u32[]{:S(2)}) copy-start(f32[1536]{0:T(1024)} %param.12) | copy-start | bytes 18436
  165.0 3.6 %collective-permute-start.41 = (f32[2,64]{1,0:T(2,128)S(1)}, f32[2,64]{1,0:T(2,128)S(1)}, u32[]{:S(2)}, u32[]{:S(2)}) collective-permute-start(f32[2,64]{1,0:T(2,128)S(1)} %fusion.31), channel_id=1, source_target_pairs={{0,16},{8,24},{16,0},{24,8},{1,17},{9,25},{17,1},{25,9},{2,18},{10... | collective-permute-start | bytes 1544 | tf_op jit(solution)/shard_map/ppermute | solution.py:323
  168.0 6.6 %collective-permute-start.36 = (bf16[64,1536]{1,0:T(8,128)(2,1)S(1)}, bf16[64,1536]{1,0:T(8,128)(2,1)S(1)}, u32[]{:S(2)}, u32[]{:S(2)}) collective-permute-start(bf16[64,1536]{1,0:T(8,128)(2,1)S(1)} %slice.225), channel_id=1, source_target_pairs={{0,2},{1,3},{2,0},{3,1},{4,6},{5,7},{6,4},{7,5},{8,10},{9,11},{10,... | collective-permute-start | bytes 589832 | tf_op jit(solution)/shard_map/ppermute | solution.py:320

commit v4 on v3

--- a/solution.py
+++ b/solution.py
@@ -59,38 +59,38 @@
     return jnp.concatenate([x[...] for x in x_refs], axis=0)
 
 
-def load_and_multiply(name, xs, w, me, shard, rels, dtype, by_rows):
+def load_and_multiply(name, xs, w, me, shard, rels, dtype, joined):
     rows, depth = sum(x.shape[0] for x in xs), xs[0].shape[1]
-    n, parts, whole = len(rels), 4, len(xs) > 1
+    n, parts = len(rels), 4
 
     def kernel(me_ref, *refs):
-        x_refs, (w_ref, o_ref, held_ref), sem = refs[: len(xs)], refs[len(xs) : len(xs) + 3], refs[-1]
+        x_refs, w_ref, out_refs, sem = refs[: len(xs)], refs[len(xs)], refs[len(xs) + 1 : -1], refs[-1]
+        held_ref = out_refs[len(out_refs) - 2 if joined else -1]
         copies = {}
         for i, r in enumerate(rels):
-            at, to = block_at(me_ref[0], r, shard), slice(i * shard, (i + 1) * shard)
-            source, target = (w_ref.at[at, :], held_ref.at[to, :]) if by_rows else (w_ref.at[:, at], held_ref.at[:, to])
-            size = source.shape[0] // parts
+            source, target = w_ref.at[block_at(me_ref[0], r, shard), :], held_ref.at[pl.ds(i * shard, shard), :]
+            size = shard // parts
             for p in range(parts):
                 span = pl.ds(p * size, size)
                 copies[i, p] = pltpu.make_async_copy(source.at[span, :], target.at[span, :], sem.at[i, p])
                 copies[i, p].start()
-        x_ref = x_refs[0]
-        if whole:
-            x_ref = refs[len(xs) + 3]
-            x_ref[...] = pieces_of(x_refs)
+        if joined:
+            out_refs[2][...] = pieces_of(x_refs)
+            x_refs = out_refs[2:3]
         for i in range(n):
             for p in range(parts):
                 copies[i, p].wait()
             to = slice(i * shard, (i + 1) * shard)
-            block = held_ref[to, :] if by_rows else held_ref[:, to]
-            o_ref[:, to] = mm(x_ref[...], block, NT if by_rows else NN).astype(dtype)
-
-    out_shape = [
-        jax.ShapeDtypeStruct((rows, n * shard), dtype),
-        pltpu.VMEM((n * shard, depth) if by_rows else (depth, n * shard), w.dtype),
-    ]
-    if whole:
-        out_shape.append(jax.ShapeDtypeStruct((rows, depth), bf16))
+            for x_ref, o_ref in zip(x_refs, out_refs):
+                o_ref[:, to] = mm(x_ref[...], held_ref[to, :], NT).astype(dtype)
+
+    held = pltpu.VMEM((n * shard, depth), w.dtype)
+    if joined:
+        out_shape = [jax.ShapeDtypeStruct((rows, n * shard), dtype), held, jax.ShapeDtypeStruct((rows, depth), bf16)]
+        scratch = []
+    else:
+        out_shape = [jax.ShapeDtypeStruct((x.shape[0], n * shard), dtype) for x in xs]
+        scratch = [held]
     return call(
         kernel,
         name,
@@ -99,34 +99,40 @@
         [IN_VMEM] * len(out_shape),
         2 * rows * depth * shard * n,
         2 * depth * shard * n,
-        scratch=[pltpu.SemaphoreType.DMA((n, parts))],
+        scratch=scratch + [pltpu.SemaphoreType.DMA((n, parts))],
+        limit=8 if joined else 14,
     )(me, *xs, pltpu.with_memory_space_constraint(w, pltpu.HBM))
 
 
-def multiply(name, xs, w_go, w_keep, shard, by_rows):
+def multiply(name, xs, w, shard, by_rows, me=None):
     rows, depth = sum(x.shape[0] for x in xs), xs[0].shape[1]
+    whole = me is not None
+    more = (me,) if whole else ()
 
     def kernel(*refs):
-        x_refs, (go_w, keep_w, go_ref, keep_ref, all_ref) = refs[: len(xs)], refs[len(xs) :]
+        x_refs, w_ref, out_refs = refs[: len(xs)], refs[len(xs) + len(more)], refs[len(xs) + len(more) + 1 :]
+        all_ref = out_refs[-1]
         all_ref[...] = pieces_of(x_refs)
-        for w_ref, o_ref in ((go_w, go_ref), (keep_w, keep_ref)):
-            for c in (slice(0, shard), slice(shard, 2 * shard)):
-                block = w_ref[c, :] if by_rows else w_ref[:, c]
-                o_ref[:, c] = mm(all_ref[...], block, NT if by_rows else NN).astype(o_ref.dtype)
-
+        for i in range(4 if whole else 2):
+            c = slice((i % 2) * shard, (i % 2 + 1) * shard)
+            at = block_at(refs[len(xs)][0], (2, 3, 0, 1)[i], shard) if whole else c
+            block = w_ref[at, :] if by_rows else w_ref[:, at]
+            o_ref = out_refs[i // 2]
+            o_ref[:, c] = mm(all_ref[...], block, NT if by_rows else NN).astype(o_ref.dtype)
+
+    out_shape = [jax.ShapeDtypeStruct((rows, 2 * shard), bf16)]
+    if whole:
+        out_shape.append(jax.ShapeDtypeStruct((rows, 2 * shard), f32))
+    out_shape.append(jax.ShapeDtypeStruct((rows, depth), bf16))
     return call(
         kernel,
         name,
-        (
-            jax.ShapeDtypeStruct((rows, 2 * shard), bf16),
-            jax.ShapeDtypeStruct((rows, 2 * shard), f32),
-            jax.ShapeDtypeStruct((rows, depth), bf16),
-        ),
-        [IN_VMEM] * (len(xs) + 2),
-        [IN_VMEM] * 3,
+        out_shape,
+        [IN_VMEM] * len(xs) + [IN_SMEM] * len(more) + [IN_VMEM],
+        [IN_VMEM] * len(out_shape),
         8 * rows * depth * shard,
         12 * rows * shard,
-    )(*xs, w_go, w_keep)
+    )(*xs, *more, w)
 
 
 def summed(near, far, w_ref, me, shard, cols, by_rows):
@@ -363,7 +369,10 @@
             even = even[1:]
             if first:
                 even[0] = after(even[0], *first)
-            even += [along_gy(e, 2) for e in even]
+            return even + [along_gy(e, 2) for e in even]
+
+        def swapped(even, first):
+            even = even[:-1] + [after(even[-1], *first)]
             even = jnp.concatenate(even)
             return [even, along_gy(even, 1)]
 
@@ -375,8 +384,7 @@
         late_up = pltpu.with_memory_space_constraint(w_up, pltpu.VMEM)
         go, down_go, cot_w = load_and_multiply("grad_act_w_go", cot_w, w_down, me, shard, (2, 3), bf16, True)
         came_gw = to_first(go)
-        cot_x = gather_far(cotangent, [go])
-        keep_gw, down_keep = load_and_multiply("grad_act_w_keep", [cot_w], w_down, me, shard, (0, 1), f32, True)
+        cot_x = swapped(gather_far(cotangent, [go]), [go])
         totals = plane_sum(after(totals, go), 2)
 
         row_mean = (totals[0] / D)[:, None]
@@ -384,18 +392,19 @@
         inv_std = lax.rsqrt(variance + epsilon)
         standard = (values - row_mean) * inv_std
         own = (standard * norm_gain).astype(bf16)
+        go, cot_x = multiply("grad_act_x_go", cot_x, down_go, shard, True)
+        came_gx = to_first(go)
+        keep_gw, keep_gx = load_and_multiply("grad_act_keep", [cot_w, cot_x], w_down, me, shard, (0, 1), f32, False)
         second_gw = for_second(keep_gw, came_gw, shard)
         back_gw = to_second(second_gw)
-        normed_w = gather(own, [second_gw])
-        normed_x = gather_far(own)
-        go, keep_gx, cot_x = multiply("grad_act_x", cot_x, down_go, down_keep, shard, True)
-        came_gx = to_first(go)
-        normed_w[0] = after(normed_w[0], go)
-        go, up_go, normed_w = load_and_multiply("hidden_w_go", normed_w, w_up, me, shard, (2, 3), bf16, False)
-        came_hw = to_first(go)
-        keep_hw, up_keep = load_and_multiply("hidden_w_keep", [normed_w], w_up, me, shard, (0, 1), f32, False)
+        normed_w = gather(own, [go])
+        normed_even = gather_far(own, [keep_gw])
         second_gx = for_second(keep_gx, came_gx, shard)
         back_gx = to_second(second_gx)
+        normed_w[0] = after(normed_w[0], second_gw, second_gx)
+        go, keep_hw, normed_w = multiply("hidden_w", normed_w, late_up, shard, False, me)
+        came_hw = to_first(go)
+        normed_x = swapped(normed_even, [go])
 
         def middle(grad_act, hidden):
             hidden = hidden + bias
@@ -404,14 +413,15 @@
             slope = upper + hidden * jnp.exp(-0.5 * hidden * hidden) * inv_root_two_pi
             return act, (grad_act * slope).astype(bf16)
 
-        go, keep_hx, normed_x = multiply("hidden_x", normed_x, up_go, up_keep, shard, False)
+        normed_x[0] = after(normed_x[0], back_gw)
+        go, keep_hx, normed_x = multiply("hidden_x", normed_x, late_up, shard, False, me)
         came_hx = to_first(go)
-        second_hw = for_second(keep_hw, after(came_hw, second_gx, go), shard)
+        second_hw = for_second(keep_hw, after(came_hw, back_gx, go), shard)
         back_hw = to_second(second_hw)
         second_hx = for_second(keep_hx, came_hx, shard)
         back_hx = to_second(second_hx)
         act_w, grad_w = middle(
-            plane_total(keep_gw, after(came_gw, back_gx), back_gw, shard),
+            plane_total(keep_gw, came_gw, back_gw, shard),
             plane_total(keep_hw, came_hw, after(back_hw, second_hx), shard),
         )
         grad_near_w = jnp.concatenate([grad_w, to_first(grad_w)], axis=1)
@@ -424,7 +434,7 @@
         near_x = jnp.concatenate([act_x, after(to_first(act_x), grad_near_x)], axis=1)
         grad_far_x = to_second(grad_near_x)
         far_x = to_second(near_x)
-        grad_far_w = to_second(after(grad_near_w, near_x))
+        grad_far_w = to_second(after(grad_near_w, grad_near_x))
         far_w = to_second(after(near_w, near_x))
 
         def pair_sum(keep, go):
@@ -462,36 +472,36 @@
         down = weight_grad_down("wgrad_near", (near_w, near_x), (cot_w, cot_x), me, (0, 2), shard, units, None)
         keep, go, gain_x = normed_grad("normed_grad_x", grad_near_x, after(grad_far_x, down), late_up, normed_x, me)
         grad_sums_x = pair_sum(keep, go)
-        keep, go = down_product("mlp_x", near_x, after(far_x, go), late_down, me)
-        sums_x = pair_sum(keep, go)
         keep, go, gain = normed_grad(
             "normed_grad_w", grad_near_w, after(grad_far_w, go), late_up, normed_w, me, gain_x
         )
         n = keep.shape[0]
-        normed = (after(normed_w, go, sums_x, grad_sums_x), normed_x)
+        nears, fars = (grad_near_w, grad_near_x), (grad_far_w, grad_far_x)
+        steps = range(0, patches.shape[1], 256)
+        some, others = steps[: len(steps) // 2], steps[len(steps) // 2 :]
+        normed = (after(normed_w, go), normed_x)
+        grad_w_up, grad_bias_up = weight_grad_up("wgrad_up_1", normed, nears, fars, me, units, some, None)
         came = along_gy(go, 1).astype(f32)
         grad_sums_w = keep + came[:n]
         gain = gain + (came[n : n + 1] + came[n + 8 : n + 9])
-        nears, fars = (grad_near_w, grad_near_x), (grad_far_w, grad_far_x)
-        steps = range(0, patches.shape[1], 256)
-        some, others = steps[: len(steps) // 2], steps[len(steps) // 2 :]
-        grad_w_up, grad_bias_up = weight_grad_up("wgrad_up_1", normed, nears, fars, me, units, some, None)
-        grad_held, _ = from_neighbour(grad_sums_x, None, grad_bias_up)
-        held, _ = from_neighbour(sums_x, None, grad_bias_up)
-        keep, go = down_product("mlp_w", near_w, after(far_w, grad_bias_up, grad_sums_w, *grad_held, *held), late_down, me)
+        keep, go = down_product("mlp_x", near_x, after(far_x, grad_bias_up), late_down, me)
+        sums_x = pair_sum(keep, go)
+        grad_held, _ = from_neighbour(grad_sums_x)
+        normed = (after(normed_w, go, grad_sums_w, sums_x, *grad_held), normed_x)
+        grad_w_up = weight_grad_up("wgrad_up_2", normed, nears, fars, me, units, others, grad_w_up)[0]
+        held, _ = from_neighbour(sums_x, None, grad_w_up)
+        keep, go = down_product("mlp_w", near_w, after(far_w, grad_w_up), late_down, me)
         sums_w = pair_sum(keep, go)
-        far_w = after(far_w, go, *held)
+        far_w = after(far_w, go, sums_w)
         grad_w_down = weight_grad_down("wgrad_far", (far_w, far_x), (cot_w, cot_x), me, (1, 3), shard, units, down)
         grad_far, _ = from_far(grad_held)
         came, gain = swap(grad_sums_w[rows:], 2, gain)
-        grad_normed = grad_sums_w[:rows] + after(came, grad_w_down) + grad_far
+        grad_normed = grad_sums_w[:rows] + after(came, go) + grad_far
         scaled = grad_normed * norm_gain
         sums = jnp.stack([jnp.sum(scaled, axis=1), jnp.sum(scaled * standard, axis=1)])
-        normed = (after(normed_w, grad_w_down, sums_w, sums), normed_x)
-        grad_w_up = weight_grad_up("wgrad_up_2", normed, nears, fars, me, units, others, grad_w_up)[0]
-        sums = sums + after(along_gx(sums, 1), grad_w_up)
-        mlp_home = sums_w[:rows] + after(along_gy(sums_w[rows:].astype(bf16), 2), grad_w_up).astype(f32)
-        held = [after(h, grad_w_down) for h in held]
+        sums = sums + after(along_gx(sums, 1), grad_w_down)
+        mlp_home = sums_w[:rows] + after(along_gy(sums_w[rows:].astype(bf16), 2), grad_w_down).astype(f32)
+        held = [after(h, grad_w_up) for h in held]
         mlp_out = (mlp_home + from_far(held)[0] + bias_down).astype(bf16)
         for step in bits(chips)[1:]:
             gain = gain + along_gy(gain, 2 * step)

time: 176 us -> 173 us (0.983)
  waiting for transfers between devices: 55.4 us -> 60.9 us
  Pallas kernels: 52.8 us -> 47.6 us
    ppermute x23, waiting for transfers between devices: 16.8 us -> 25.2 us  [along_gy(): return lax.ppermute(x, 'gy', [(i, i ^ m) for i in range(n_gy)])]
    pallas_call x4 -> x2, Pallas kernels: 14.7 us -> 8.44 us  [load_and_multiply(): call(kernel, name, out_shape, [IN_SMEM] + [IN_VMEM] * len(xs) + [IN_HBM],...]
    ppermute x23, starting transfers between devices: 23.1 us -> 19.8 us  [along_gy(): return lax.ppermute(x, 'gy', [(i, i ^ m) for i in range(n_gy)])]
    ppermute x4, waiting for transfers between devices: 2.66 us -> 0.16 us  [along_gx(): return lax.ppermute(x, 'gx', [(i, i ^ m) for i in range(n_gx)])]
    ppermute x8, waiting for transfers between devices: 15.4 us -> 13 us  [to_second(): return lax.ppermute(x, both, second_pairs)]
    ppermute x8, waiting for transfers between devices: 20.5 us -> 22.6 us  [to_first(): return lax.ppermute(x, both, first_pairs)]
    convert_element_type x4, other arithmetic: 4.21 us -> 2.44 us  [for_second(): return (keep[:, shard:] + came[:, shard:].astype(f32)).astype(bf16)]
    pallas_call x2 -> x3, Pallas kernels: 5.23 us -> 6.77 us  [multiply(): call(kernel, name, out_shape, [IN_VMEM] * len(xs) + [IN_SMEM] * len(more)...]
  transfers between devices with their start and end apart: 43 -> 43, of which waited for: 21 -> 19; matrix products, arithmetic and copies ran while one was open for 8% -> 7% of each run, Pallas kernels for 30% -> 28%
where the time goes in v4:
time: 173 us; the launch traced here: 172 us
  waiting for transfers between devices  60.9 us (35%)
  Pallas kernels  47.6 us (28%)
  starting transfers between devices  47.1 us (27%)
  other arithmetic  12.1 us (7%)
  local copies, waits for them, and re-layouts  3.34 us (2%)
    ppermute x23, waiting for transfers between devices, along_gy(): return lax.ppermute(x, 'gy', [(i, i ^ m) for i in range(n_gy)])  25.2 us
    ppermute x8, waiting for transfers between devices, to_first(): return lax.ppermute(x, both, first_pairs)  22.6 us
    ppermute x23, starting transfers between devices, along_gy(): return lax.ppermute(x, 'gy', [(i, i ^ m) for i in range(n_gy)])  19.8 us
    ppermute x8, waiting for transfers between devices, to_second(): return lax.ppermute(x, both, second_pairs)  13 us
    pallas_call x2, Pallas kernels, weight_grad_up(): call(kernel, name, out_shape, [IN_SMEM] + [IN_VMEM] * 6 + ([] if sums els...  11.5 us
    ppermute x8, starting transfers between devices, to_first(): return lax.ppermute(x, both, first_pairs)  10.7 us
    pallas_call x2, Pallas kernels, weight_grad_down(): call(kernel, name, jax.ShapeDtypeStruct((units, out), f32), [IN_SMEM] + [...  10.4 us
    ppermute x8, starting transfers between devices, to_second(): return lax.ppermute(x, both, second_pairs)  10.1 us
  transfers between devices with their start and end apart: 43, of which 19 were waited for; matrix products, arithmetic and copies ran while one was open for 7% of the time, Pallas kernels for 28%

profile of v4, /device:TPU:0, one launch (start us, length us, event | category | flops | bytes accessed | tf_op | source)
XLA Modules:
  0.0 172.5 jit_solution(6307765487482811775)
XLA Ops:
  0.6 3.1 %collective-permute-start.1 = (bf16[64,1536]{1,0:T(8,128)(2,1)}, bf16[64,1536]{1,0:T(8,128)(2,1)S(1)}, u32[]{:S(2)}, u32[]{:S(2)}) collective-permute-start(bf16[64,1536]{1,0:T(8,128)(2,1)} %refs_0_.1), channel_id=1, source_target_pairs={{0,2},{1,3},{2,0},{3,1},{4,6},{5,7},{6,4},{7,5},{8,10},{9,11},{10,... | collective-permute-start | bytes 589832 | tf_op jit(solution)/shard_map/ppermute | solution.py:326
  3.7 2.6 %collective-permute-start.5 = (bf16[64,1536]{1,0:T(8,128)(2,1)}, bf16[64,1536]{1,0:T(8,128)(2,1)S(1)}, u32[]{:S(2)}, u32[]{:S(2)}) collective-permute-start(bf16[64,1536]{1,0:T(8,128)(2,1)} %refs_0_.1), channel_id=1, source_target_pairs={{0,4},{1,5},{2,6},{3,7},{4,0},{5,1},{6,2},{7,3},{8,12},{9,13},{10,... | collective-permute-start | bytes 589832 | tf_op jit(solution)/shard_map/ppermute | solution.py:326
  6.3 1.1 convert_reduce_fusion.2
  7.4 1.6 collective-permute-start
  9.0 2.6 %collective-permute-done.1.refs_1_ = bf16[64,1536]{1,0:T(8,128)(2,1)S(1)} collective-permute-done((bf16[64,1536]{1,0:T(8,128)(2,1)}, bf16[64,1536]{1,0:T(8,128)(2,1)S(1)}, u32[]{:S(2)}, u32[]{:S(2)}) %collective-permute-start.1) | collective-permute-done | bytes 196640 | tf_op jit(solution)/shard_map/ppermute | solution.py:326
  11.6 1.4 collective-permute-done.3.refs_3_
  13.0 0.9 copy-done.7
  14.0 3.8 %grad_act_w_go.1 = (bf16[256,1536]{1,0:T(8,128)(2,1)S(1)}, bf16[1536,1536]{1,0:T(8,128)(2,1)S(1)}, bf16[256,1536]{1,0:T(8,128)(2,1)S(1)}) custom-call(s32[1]{0:T(128)} %bitcast.me_ref.refs_4_.refs_2_, bf16[64,1536]{1,0:T(8,128)(2,1)S(1)} %copy-done.7, bf16[64,1536]{1,0:T(8,128)(2,1)S(1)} %collective-permute-done.1.refs_1_, ...), custom_call_target="tpu_custom_call" | custom-call | tf_op jit(solution)/shard_map/grad_act_w_go/pallas_call | solution.py:94
  17.8 1.9 %collective-permute-start.4 = (f32[2,64]{1,0:T(2,128)S(1)}, f32[2,64]{1,0:T(2,128)S(1)}, u32[]{:S(2)}, u32[]{:S(2)}) collective-permute-start(f32[2,64]{1,0:T(2,128)S(1)} %fusion.32), channel_id=1, source_target_pairs={{0,16},{8,24},{16,0},{24,8},{1,17},{9,25},{17,1},{25,9},{2,18},{10... | collective-permute-start | bytes 1544 | tf_op jit(solution)/shard_map/ppermute | solution.py:329
  19.8 1.6 collective-permute-start.8
  21.5 4.9 %collective-permute-done.6 = bf16[64,1536]{1,0:T(8,128)(2,1)S(1)} collective-permute-done((bf16[64,1536]{1,0:T(8,128)(2,1)S(1)}, bf16[64,1536]{1,0:T(8,128)(2,1)S(1)}, u32[]{:S(2)}, u32[]{:S(2)}) %collective-permute-start.6) | collective-permute-done | bytes 196640 | tf_op jit(solution)/shard_map/ppermute | solution.py:326
  26.5 1.7 collective-permute-done.7.refs_1_
  28.2 1.4 grad_act_x_go.1
  29.6 1.6 collective-permute-start.9
  31.3 1.6 collective-permute-start.15
  32.9 1.7 %collective-permute-start.10 = (bf16[64,1536]{1,0:T(8,128)(2,1)S(1)}, bf16[64,1536]{1,0:T(8,128)(2,1)S(1)}, u32[]{:S(2)}, u32[]{:S(2)}) collective-permute-start(bf16[64,1536]{1,0:T(8,128)(2,1)S(1)} %fusion.17.refs_0_), channel_id=1, source_target_pairs={{0,2},{1,3},{2,0},{3,1},{4,6},{5,7},{6,4},{7,5},{8,10},{9,11},{10,... | collective-permute-start | bytes 589832 | tf_op jit(solution)/shard_map/ppermute | solution.py:326
  34.7 4.6 %grad_act_keep.1 = (f32[256,1536]{1,0:T(8,128)S(1)}, f32[256,1536]{1,0:T(8,128)S(1)}) custom-call(s32[1]{0:T(128)} %bitcast.me_ref.refs_4_.refs_2_, bf16[256,1536]{1,0:T(8,128)(2,1)S(1)} %get-tuple-element.61.refs_0_.c0, bf16[256,1536]{1,0:T(8,128)(2,1)S(1)} %get-tuple-element.65.refs_1_.c1, bf16[3072,1536]{1,0:T(8,128)(2,1)} %w_ref.7), custom_call_target="tpu_custom_call" | custom-call | tf_op jit(solution)/shard_map/grad_act_keep/pallas_call | solution.py:94
  39.3 2.9 %collective-permute-done.15 = bf16[64,1536]{1,0:T(8,128)(2,1)S(1)} collective-permute-done((bf16[64,1536]{1,0:T(8,128)(2,1)S(1)}, bf16[64,1536]{1,0:T(8,128)(2,1)S(1)}, u32[]{:S(2)}, u32[]{:S(2)}) %collective-permute-start.15) | collective-permute-done | bytes 196640 | tf_op jit(solution)/shard_map/ppermute | solution.py:326
  42.6 1.5 collective-permute-start.17
  44.3 2.7 %hidden_w.1 = (bf16[256,1536]{1,0:T(8,128)(2,1)S(1)}, f32[256,1536]{1,0:T(8,128)S(1)}, bf16[256,1536]{1,0:T(8,128)(2,1)S(1)}) custom-call(bf16[64,1536]{1,0:T(8,128)(2,1)S(1)} %fusion.17.refs_0_, bf16[64,1536]{1,0:T(8,128)(2,1)S(1)} %collective-permute-done.10.refs_1_, bf16[64,1536]{1,0:T(8,128)(2,1)S(1)} %collective-permute-done.11.refs_2_, ...), custom_call_target="tpu_custom_call" | custom-call | tf_op jit(solution)/shard_map/hidden_w/pallas_call | solution.py:127
  47.0 1.7 collective-permute-done.16
  48.8 1.8 %collective-permute-start.13 = (bf16[256,1536]{1,0:T(8,128)(2,1)S(1)}, bf16[256,1536]{1,0:T(8,128)(2,1)S(1)}, u32[]{:S(2)}, u32[]{:S(2)}) collective-permute-start(bf16[256,1536]{1,0:T(8,128)(2,1)S(1)} %get-tuple-element.72), channel_id=1, source_target_pairs={{0,8},{1,17},{2,10},{3,19},{4,12},{5,21},{6,14},{7,23},{8,0},{9,25... | collective-permute-start | bytes 2359304 | tf_op jit(solution)/shard_map/ppermute | solution.py:320
  50.6 1.6 collective-permute-start.14
  52.3 2.7 %hidden_x.1 = (bf16[256,1536]{1,0:T(8,128)(2,1)}, f32[256,1536]{1,0:T(8,128)S(1)}, bf16[256,1536]{1,0:T(8,128)(2,1)S(1)}) custom-call(bf16[128,1536]{1,0:T(8,128)(2,1)S(1)} %constant_dynamic-update-slice_fusion.2.refs_0_, bf16[128,1536]{1,0:T(8,128)(2,1)S(1)} %collective-permute-done.18.refs_1_, s32[1]{0:T(128)} %bitcast.me_ref.refs_4_.refs_2_, ...), custom_call_target="tpu_custom_call" | custom-call | tf_op jit(solution)/shard_map/hidden_x/pallas_call | solution.py:127
  55.0 1.1 copy-done.5
  56.5 6.1 %collective-permute-done.14 = bf16[256,768]{1,0:T(8,128)(2,1)S(1)} collective-permute-done((bf16[256,768]{1,0:T(8,128)(2,1)S(1)}, bf16[256,768]{1,0:T(8,128)(2,1)S(1)}, u32[]{:S(2)}, u32[]{:S(2)}) %collective-permute-start.14) | collective-permute-done | bytes 393248 | tf_op jit(solution)/shard_map/ppermute | solution.py:323
  62.7 2.4 %collective-permute-done.13 = bf16[256,1536]{1,0:T(8,128)(2,1)S(1)} collective-permute-done((bf16[256,1536]{1,0:T(8,128)(2,1)S(1)}, bf16[256,1536]{1,0:T(8,128)(2,1)S(1)}, u32[]{:S(2)}, u32[]{:S(2)}) %collective-permute-start.13) | collective-permute-done | bytes 786464 | tf_op jit(solution)/shard_map/ppermute | solution.py:320
  65.1 1.0 add_convert_fusion.1
  66.1 1.3 collective-permute-start.19
  67.4 0.9 dynamic_slice.3
  68.3 9.5 %collective-permute-done.20 = bf16[256,1536]{1,0:T(8,128)(2,1)} collective-permute-done((bf16[256,1536]{1,0:T(8,128)(2,1)}, bf16[256,1536]{1,0:T(8,128)(2,1)}, u32[]{:S(2)}, u32[]{:S(2)}) %collective-permute-start.20) | collective-permute-done | bytes 786464 | tf_op jit(solution)/shard_map/ppermute | solution.py:320
  77.8 1.3 add_convert_fusion
  79.2 1.3 collective-permute-start.22
  80.5 2.2 %fusion.5 = (bf16[256,768]{1,0:T(8,128)(2,1)S(1)}, bf16[256,768]{1,0:T(8,128)(2,1)S(1)}) fusion(bf16[256,768]{1,0:T(8,128)(2,1)} %copy-done.13, f32[256,1536]{1,0:T(8,128)S(1)} %copy-done.3, bf16[256,1536]{1,0:T(8,128)(2,1)} %copy-done.9, f32[768]{0:T(1024)S(1)} %dynamic_slice.3, bf16[256,768]{1,0:T(8,128)(2,1)} %collective-permute-done.19, ...), kind=kLoop, calls=%fused_computation.9 | loop fusion | flops 4128768 | bytes 3935232 | tf_op jit(solution)/shard_map/convert_element_type | solution.py:414
  82.7 1.8 %collective-permute-start.25 = (bf16[256,768]{1,0:T(8,128)(2,1)S(1)}, bf16[256,768]{1,0:T(8,128)(2,1)S(1)}, u32[]{:S(2)}, u32[]{:S(2)}) collective-permute-start(bf16[256,768]{1,0:T(8,128)(2,1)S(1)} %get-tuple-element.121), channel_id=1, source_target_pairs={{0,8},{1,17},{2,10},{3,19},{4,12},{5,21},{6,14},{7,23},{8,0},{9,25... | collective-permute-start | bytes 1179656 | tf_op jit(solution)/shard_map/ppermute | solution.py:320
  84.8 4.9 %collective-permute-done.22 = bf16[256,768]{1,0:T(8,128)(2,1)S(1)} collective-permute-done((bf16[256,768]{1,0:T(8,128)(2,1)S(1)}, bf16[256,768]{1,0:T(8,128)(2,1)S(1)}, u32[]{:S(2)}, u32[]{:S(2)}) %collective-permute-start.22) | collective-permute-done | bytes 393248 | tf_op jit(solution)/shard_map/ppermute | solution.py:323
  89.7 1.7 fusion.11
  91.5 2.9 %collective-permute-start.24 = (bf16[256,768]{1,0:T(8,128)(2,1)S(1)}, bf16[256,768]{1,0:T(8,128)(2,1)S(1)}, u32[]{:S(2)}, u32[]{:S(2)}) collective-permute-start(bf16[256,768]{1,0:T(8,128)(2,1)S(1)} %get-tuple-element.119), channel_id=1, source_target_pairs={{0,8},{1,17},{2,10},{3,19},{4,12},{5,21},{6,14},{7,23},{8,0},{9,25... | collective-permute-start | bytes 1179656 | tf_op jit(solution)/shard_map/ppermute | solution.py:320
  94.8 5.3 %collective-permute-done.24 = bf16[256,768]{1,0:T(8,128)(2,1)S(1)} collective-permute-done((bf16[256,768]{1,0:T(8,128)(2,1)S(1)}, bf16[256,768]{1,0:T(8,128)(2,1)S(1)}, u32[]{:S(2)}, u32[]{:S(2)}) %collective-permute-start.24) | collective-permute-done | bytes 393248 | tf_op jit(solution)/shard_map/ppermute | solution.py:320
  100.9 5.3 %collective-permute-done.23 = bf16[256,768]{1,0:T(8,128)(2,1)S(1)} collective-permute-done((bf16[256,768]{1,0:T(8,128)(2,1)S(1)}, bf16[256,768]{1,0:T(8,128)(2,1)S(1)}, u32[]{:S(2)}, u32[]{:S(2)}) %collective-permute-start.23) | collective-permute-done | bytes 393248 | tf_op jit(solution)/shard_map/ppermute | solution.py:320
  106.3 2.1 %collective-permute-start.27 = (bf16[256,1536]{1,0:T(8,128)(2,1)S(1)}, bf16[256,1536]{1,0:T(8,128)(2,1)S(1)}, u32[]{:S(2)}, u32[]{:S(2)}) collective-permute-start(bf16[256,1536]{1,0:T(8,128)(2,1)S(1)} %pad_maximum_fusion.3.p1.near_ref), channel_id=1, source_target_pairs={{0,16},{1,9},{2,18},{3,11},{4,20},{5,13},{6,22},{7,15},{8,24},{9,1... | collective-permute-start | bytes 2359304 | tf_op jit(solution)/shard_map/ppermute | solution.py:323
  108.3 5.2 %wgrad_near.1.refs_0_ = f32[3072,1536]{1,0:T(8,128)} custom-call(s32[1]{0:T(128)} %bitcast.me_ref.refs_4_.refs_2_, bf16[256,1536]{1,0:T(8,128)(2,1)S(1)} %pad_maximum_fusion.p0.near_ref, bf16[256,1536]{1,0:T(8,128)(2,1)S(1)} %pad_maximum_fusion.3.p1.near_ref, bf16[256,1536]{1,0:T(8,128)(2,1)S(1)} %get-tuple-element.61.refs_0_.c0, ...), custom_call_target="tpu_custom_call" | custom-call | tf_op jit(solution)/shard_map/wgrad_near/pallas_call | solution.py:241
  113.6 2.7 %normed_grad_x.1 = (f32[128,1536]{1,0:T(8,128)S(1)}, bf16[128,1536]{1,0:T(8,128)(2,1)S(1)}, f32[1,1536]{1,0:T(1,128)S(1)}) custom-call(s32[1]{0:T(128)} %bitcast.me_ref.refs_4_.refs_2_, bf16[256,1536]{1,0:T(8,128)(2,1)S(1)} %pad_maximum_fusion.2.near_ref.near1, bf16[256,1536]{1,0:T(8,128)(2,1)S(1)} %collective-permute-done.29.far_ref.far1, ...), custom_call_target="tpu_custom_call" | custom-call | tf_op jit(solution)/shard_map/normed_grad_x/pallas_call | solution.py:194
  117.2 1.6 collective-permute-start.26
  118.8 1.9 %collective-permute-done.28.far_ref.far0 = bf16[256,1536]{1,0:T(8,128)(2,1)S(1)} collective-permute-done((bf16[256,1536]{1,0:T(8,128)(2,1)S(1)}, bf16[256,1536]{1,0:T(8,128)(2,1)S(1)}, u32[]{:S(2)}, u32[]{:S(2)}) %collective-permute-start.28) | collective-permute-done | bytes 786464 | tf_op jit(solution)/shard_map/ppermute | solution.py:323
  120.7 2.7 %normed_grad_w.1 = (f32[128,1536]{1,0:T(8,128)S(1)}, bf16[144,1536]{1,0:T(8,128)(2,1)S(1)}, f32[1,1536]{1,0:T(1,128)S(1)}) custom-call(s32[1]{0:T(128)} %bitcast.me_ref.refs_4_.refs_2_, bf16[256,1536]{1,0:T(8,128)(2,1)S(1)} %pad_maximum_fusion.1.near_ref.near0, bf16[256,1536]{1,0:T(8,128)(2,1)S(1)} %collective-permute-done.28.far_ref.far0, ...), custom_call_target="tpu_custom_call" | custom-call | tf_op jit(solution)/shard_map/normed_grad_w/pallas_call | solution.py:194
  124.1 6.1 %wgrad_up_1.1 = (f32[1536,3072]{1,0:T(8,128)}, f32[1,3072]{1,0:T(1,128)}) custom-call(s32[1]{0:T(128)} %bitcast.me_ref.refs_4_.refs_2_, bf16[256,1536]{1,0:T(8,128)(2,1)S(1)} %get-tuple-element.99.n_ref.n0, bf16[256,1536]{1,0:T(8,128)(2,1)S(1)} %get-tuple-element.87.n_ref.n1, bf16[256,1536]{1,0:T(8,128)(2,1)S(1)} %pad_maximum_fusion.1.near_ref.near0, ...), custom_call_target="tpu_custom_call" | custom-call | tf_op jit(solution)/shard_map/wgrad_up_1/pallas_call | solution.py:290
  130.2 2.6 %mlp_x.1 = (f32[128,1536]{1,0:T(8,128)S(1)}, bf16[128,1536]{1,0:T(8,128)(2,1)S(1)}) custom-call(s32[1]{0:T(128)} %bitcast.me_ref.refs_4_.refs_2_, bf16[256,1536]{1,0:T(8,128)(2,1)S(1)} %pad_maximum_fusion.3.p1.near_ref, bf16[256,1536]{1,0:T(8,128)(2,1)S(1)} %collective-permute-done.27.far_ref.p1, bf16[3072,1536]{1,0:T(8,128)(2,1)S(1)} %bitcast.25), custom_call_target="tpu_custom_call" | custom-call | tf_op jit(solution)/shard_map/mlp_x/pallas_call | solution.py:160
  133.4 1.2 collective-permute-done.31
  135.9 1.6 collective-permute-start.38
  137.4 3.4 %collective-permute-done.33 = bf16[64,1536]{1,0:T(8,128)(2,1)S(1)} collective-permute-done((bf16[64,1536]{1,0:T(8,128)(2,1)S(1)}, bf16[64,1536]{1,0:T(8,128)(2,1)S(1)}, u32[]{:S(2)}, u32[]{:S(2)}) %collective-permute-start.33) | collective-permute-done | bytes 196640 | tf_op jit(solution)/shard_map/ppermute | solution.py:326
  140.9 1.5 collective-permute-start.39
  142.3 5.3 %wgrad_up_2.1 = f32[1536,3072]{1,0:T(8,128)} custom-call(s32[1]{0:T(128)} %bitcast.me_ref.refs_4_.refs_2_, bf16[256,1536]{1,0:T(8,128)(2,1)S(1)} %get-tuple-element.99.n_ref.n0, bf16[256,1536]{1,0:T(8,128)(2,1)S(1)} %get-tuple-element.87.n_ref.n1, bf16[256,1536]{1,0:T(8,128)(2,1)S(1)} %pad_maximum_fusion.1.near_ref.near0, ...), custom_call_target="tpu_custom_call", output_to_operand_aliasing={{}: (7, {})} | custom-call | tf_op jit(solution)/shard_map/wgrad_up_2/pallas_call | solution.py:290
  147.7 2.6 %mlp_w.1 = (f32[128,1536]{1,0:T(8,128)S(1)}, bf16[128,1536]{1,0:T(8,128)(2,1)S(1)}) custom-call(s32[1]{0:T(128)} %bitcast.me_ref.refs_4_.refs_2_, bf16[256,1536]{1,0:T(8,128)(2,1)S(1)} %pad_maximum_fusion.p0.near_ref, bf16[256,1536]{1,0:T(8,128)(2,1)S(1)} %collective-permute-done.26.far_ref.p0, bf16[3072,1536]{1,0:T(8,128)(2,1)S(1)} %bitcast.25), custom_call_target="tpu_custom_call" | custom-call | tf_op jit(solution)/shard_map/mlp_w/pallas_call | solution.py:160
  150.5 1.6 collective-permute-start.37
  152.1 2.1 %collective-permute-done.38 = bf16[80,1536]{1,0:T(8,128)(2,1)S(1)} collective-permute-done((bf16[80,1536]{1,0:T(8,128)(2,1)S(1)}, bf16[80,1536]{1,0:T(8,128)(2,1)S(1)}, u32[]{:S(2)}, u32[]{:S(2)}) %collective-permute-start.38) | collective-permute-done | bytes 245792 | tf_op jit(solution)/shard_map/ppermute | solution.py:326
  154.2 1.6 collective-permute-start.42
  156.1 2.1 %collective-permute-start.40 = (f32[2,64]{1,0:T(2,128)S(1)}, f32[2,64]{1,0:T(2,128)S(1)}, u32[]{:S(2)}, u32[]{:S(2)}) collective-permute-start(f32[2,64]{1,0:T(2,128)S(1)} %pad_maximum_fusion.6), channel_id=1, source_target_pairs={{0,8},{8,0},{16,24},{24,16},{1,9},{9,1},{17,25},{25,17},{2,10},{10... | collective-permute-start | bytes 1544 | tf_op jit(solution)/shard_map/ppermute | solution.py:329
  158.3 5.2 %wgrad_far.1 = f32[3072,1536]{1,0:T(8,128)} custom-call(s32[1]{0:T(128)} %bitcast.me_ref.refs_4_.refs_2_, bf16[256,1536]{1,0:T(8,128)(2,1)S(1)} %collective-permute-done.26.far_ref.p0, bf16[256,1536]{1,0:T(8,128)(2,1)S(1)} %collective-permute-done.27.far_ref.p1, bf16[256,1536]{1,0:T(8,128)(2,1)S(1)} %get-tuple-element.61.refs_0_.c0, ...), custom_call_target="tpu_custom_call", output_to_operand_aliasing={{}: (5, {})} | custom-call | tf_op jit(solution)/shard_map/wgrad_far/pallas_call | solution.py:241
  163.6 1.0 collective-permute-start.41
  165.2 2.5 %collective-permute-start.35 = (bf16[64,1536]{1,0:T(8,128)(2,1)S(1)}, bf16[64,1536]{1,0:T(8,128)(2,1)S(1)}, u32[]{:S(2)}, u32[]{:S(2)}) collective-permute-start(bf16[64,1536]{1,0:T(8,128)(2,1)S(1)} %slice.227), channel_id=1, source_target_pairs={{0,2},{1,3},{2,0},{3,1},{4,6},{5,7},{6,4},{7,5},{8,10},{9,11},{10,... | collective-permute-start | bytes 589832 | tf_op jit(solution)/shard_map/ppermute | solution.py:326
  167.8 0.9 fusion.21
  168.6 3.0 %collective-permute-done.35 = bf16[64,1536]{1,0:T(8,128)(2,1)S(1)} collective-permute-done((bf16[64,1536]{1,0:T(8,128)(2,1)S(1)}, bf16[64,1536]{1,0:T(8,128)(2,1)S(1)}, u32[]{:S(2)}, u32[]{:S(2)}) %collective-permute-start.35) | collective-permute-done | bytes 196640 | tf_op jit(solution)/shard_map/ppermute | solution.py:326
  171.7 0.8 fusion.26
  (143 shorter events, 7.9 us)
Async XLA Ops:
  0.6 11.0 %collective-permute-start.1 = (bf16[64,1536]{1,0:T(8,128)(2,1)}, bf16[64,1536]{1,0:T(8,128)(2,1)S(1)}, u32[]{:S(2)}, u32[]{:S(2)}) collective-permute-start(bf16[64,1536]{1,0:T(8,128)(2,1)} %refs_0_.1), channel_id=1, source_target_pairs={{0,2},{1,3},{2,0},{3,1},{4,6},{5,7},{6,4},{7,5},{8,10},{9,11},{10,... | collective-permute-start | bytes 589832 | tf_op jit(solution)/shard_map/ppermute | solution.py:326
  3.7 7.9 %collective-permute-start.2 = (bf16[64,1536]{1,0:T(8,128)(2,1)}, bf16[64,1536]{1,0:T(8,128)(2,1)S(1)}, u32[]{:S(2)}, u32[]{:S(2)}) collective-permute-start(bf16[64,1536]{1,0:T(8,128)(2,1)} %refs_0_.1), channel_id=1, source_target_pairs={{0,1},{1,0},{2,3},{3,2},{4,5},{5,4},{6,7},{7,6},{8,9},{9,8},{10,11... | collective-permute-start | bytes 589832 | tf_op jit(solution)/shard_map/ppermute | solution.py:326
  3.7 16.0 %collective-permute-start.5 = (bf16[64,1536]{1,0:T(8,128)(2,1)}, bf16[64,1536]{1,0:T(8,128)(2,1)S(1)}, u32[]{:S(2)}, u32[]{:S(2)}) collective-permute-start(bf16[64,1536]{1,0:T(8,128)(2,1)} %refs_0_.1), channel_id=1, source_target_pairs={{0,4},{1,5},{2,6},{3,7},{4,0},{5,1},{6,2},{7,3},{8,12},{9,13},{10,... | collective-permute-start | bytes 589832 | tf_op jit(solution)/shard_map/ppermute | solution.py:326
  7.4 4.2 %collective-permute-start = (f32[2,64]{1,0:T(2,128)S(1)}, f32[2,64]{1,0:T(2,128)S(1)}, u32[]{:S(2)}, u32[]{:S(2)}) collective-permute-start(f32[2,64]{1,0:T(2,128)S(1)} %pad_maximum_fusion.5), channel_id=1, source_target_pairs={{0,8},{8,0},{16,24},{24,16},{1,9},{9,1},{17,25},{25,17},{2,10},{10... | collective-permute-start | bytes 1544 | tf_op jit(solution)/shard_map/ppermute | solution.py:329
  11.6 1.4 collective-permute-start.3
  14.0 30.3 %slice-start = ((s8[9437184]{0:T(1024)(128)(4,1)}), s8[4194304]{0:T(1024)(128)(4,1)S(1)}, s32[]{:S(2)}) async-start(s8[9437184]{0:T(1024)(128)(4,1)} %bitcast.20), calls=%async_computation | async-start | bytes 8388608
  17.8 26.4 %slice-start.1 = ((s8[9437184]{0:T(1024)(128)(4,1)}), s8[4194304]{0:T(1024)(128)(4,1)S(1)}, s32[]{:S(2)}) async-start(s8[9437184]{0:T(1024)(128)(4,1)} %bitcast.20), calls=%async_computation.1 | async-start | bytes 8388608
  17.8 3.6 %collective-permute-start.4 = (f32[2,64]{1,0:T(2,128)S(1)}, f32[2,64]{1,0:T(2,128)S(1)}, u32[]{:S(2)}, u32[]{:S(2)}) collective-permute-start(f32[2,64]{1,0:T(2,128)S(1)} %fusion.32), channel_id=1, source_target_pairs={{0,16},{8,24},{16,0},{24,8},{1,17},{9,25},{17,1},{25,9},{2,18},{10... | collective-permute-start | bytes 1544 | tf_op jit(solution)/shard_map/ppermute | solution.py:329
  19.7 6.7 %collective-permute-start.6 = (bf16[64,1536]{1,0:T(8,128)(2,1)S(1)}, bf16[64,1536]{1,0:T(8,128)(2,1)S(1)}, u32[]{:S(2)}, u32[]{:S(2)}) collective-permute-start(bf16[64,1536]{1,0:T(8,128)(2,1)S(1)} %collective-permute-done.5), channel_id=1, source_target_pairs={{0,2},{1,3},{2,0},{3,1},{4,6},{5,7},{6,4},{7,5},{8,10},{9,11},{10,... | collective-permute-start | bytes 589832 | tf_op jit(solution)/shard_map/ppermute | solution.py:326
  19.8 22.7 %collective-permute-start.8 = (bf16[256,1536]{1,0:T(8,128)(2,1)S(1)}, bf16[256,1536]{1,0:T(8,128)(2,1)S(1)}, u32[]{:S(2)}, u32[]{:S(2)}) collective-permute-start(bf16[256,1536]{1,0:T(8,128)(2,1)S(1)} %get-tuple-element.59), channel_id=1, source_target_pairs={{0,8},{1,17},{2,10},{3,19},{4,12},{5,21},{6,14},{7,23},{8,0},{9,25... | collective-permute-start | bytes 2359304 | tf_op jit(solution)/shard_map/ppermute | solution.py:320
  26.4 1.8 %collective-permute-start.7 = (bf16[128,1536]{1,0:T(8,128)(2,1)S(1)}, bf16[128,1536]{1,0:T(8,128)(2,1)S(1)}, u32[]{:S(2)}, u32[]{:S(2)}) collective-permute-start(bf16[128,1536]{1,0:T(8,128)(2,1)S(1)} %constant_dynamic-update-slice_fusion.refs_0_), channel_id=1, source_target_pairs={{0,1},{1,0},{2,3},{3,2},{4,5},{5,4},{6,7},{7,6},{8,9},{9,8},{10,11... | collective-permute-start | bytes 1179656 | tf_op jit(solution)/shard_map/ppermute | solution.py:326
  28.2 3.0 %copy-start.8 = (bf16[64,1536]{1,0:T(8,128)(2,1)S(1)}, bf16[64,1536]{1,0:T(8,128)(2,1)}, u32[]{:S(2)}) copy-start(bf16[64,1536]{1,0:T(8,128)(2,1)} %param.7) | copy-start | bytes 589828
  28.2 3.0 %copy-start.15 = (f32[1536]{0:T(1024)S(1)}, f32[1536]{0:T(1024)}, u32[]{:S(2)}) copy-start(f32[1536]{0:T(1024)} %param.8) | copy-start | bytes 18436
  29.6 14.5 %collective-permute-start.9 = (bf16[256,1536]{1,0:T(8,128)(2,1)S(1)}, bf16[256,1536]{1,0:T(8,128)(2,1)S(1)}, u32[]{:S(2)}, u32[]{:S(2)}) collective-permute-start(bf16[256,1536]{1,0:T(8,128)(2,1)S(1)} %get-tuple-element.68), channel_id=1, source_target_pairs={{0,8},{1,17},{2,10},{3,19},{4,12},{5,21},{6,14},{7,23},{8,0},{9,25... | collective-permute-start | bytes 2359304 | tf_op jit(solution)/shard_map/ppermute | solution.py:320
  31.3 10.8 %collective-permute-start.15 = (bf16[64,1536]{1,0:T(8,128)(2,1)S(1)}, bf16[64,1536]{1,0:T(8,128)(2,1)S(1)}, u32[]{:S(2)}, u32[]{:S(2)}) collective-permute-start(bf16[64,1536]{1,0:T(8,128)(2,1)S(1)} %fusion.17.refs_0_), channel_id=1, source_target_pairs={{0,4},{1,5},{2,6},{3,7},{4,0},{5,1},{6,2},{7,3},{8,12},{9,13},{10,... | collective-permute-start | bytes 589832 | tf_op jit(solution)/shard_map/ppermute | solution.py:326
  32.9 9.5 %collective-permute-start.10 = (bf16[64,1536]{1,0:T(8,128)(2,1)S(1)}, bf16[64,1536]{1,0:T(8,128)(2,1)S(1)}, u32[]{:S(2)}, u32[]{:S(2)}) collective-permute-start(bf16[64,1536]{1,0:T(8,128)(2,1)S(1)} %fusion.17.refs_0_), channel_id=1, source_target_pairs={{0,2},{1,3},{2,0},{3,1},{4,6},{5,7},{6,4},{7,5},{8,10},{9,11},{10,... | collective-permute-start | bytes 589832 | tf_op jit(solution)/shard_map/ppermute | solution.py:326
  34.7 9.6 %collective-permute-start.11 = (bf16[64,1536]{1,0:T(8,128)(2,1)S(1)}, bf16[64,1536]{1,0:T(8,128)(2,1)S(1)}, u32[]{:S(2)}, u32[]{:S(2)}) collective-permute-start(bf16[64,1536]{1,0:T(8,128)(2,1)S(1)} %fusion.17.refs_0_), channel_id=1, source_target_pairs={{0,1},{1,0},{2,3},{3,2},{4,5},{5,4},{6,7},{7,6},{8,9},{9,8},{10,11... | collective-permute-start | bytes 589832 | tf_op jit(solution)/shard_map/ppermute | solution.py:326
  34.7 9.6 %slice-start.2 = ((s8[9437184]{0:T(1024)(128)(4,1)}), s8[1048576]{0:T(1024)(128)(4,1)S(1)}, s32[]{:S(2)}) async-start(s8[9437184]{0:T(1024)(128)(4,1)} %bitcast.20), calls=%async_computation.2 | async-start | bytes 2097152
  39.3 4.9 %copy-start = (f32[256,1536]{1,0:T(8,128)}, f32[256,1536]{1,0:T(8,128)S(1)}, u32[]{:S(2)}) copy-start(f32[256,1536]{1,0:T(8,128)S(1)} %get-tuple-element.67) | copy-start | bytes 4718596
  39.3 4.9 %copy-start.2 = (f32[256,1536]{1,0:T(8,128)}, f32[256,1536]{1,0:T(8,128)S(1)}, u32[]{:S(2)}) copy-start(f32[256,1536]{1,0:T(8,128)S(1)} %get-tuple-element.66) | copy-start | bytes 4718596
  42.2 6.6 %collective-permute-start.16 = (bf16[64,1536]{1,0:T(8,128)(2,1)S(1)}, bf16[64,1536]{1,0:T(8,128)(2,1)S(1)}, u32[]{:S(2)}, u32[]{:S(2)}) collective-permute-start(bf16[64,1536]{1,0:T(8,128)(2,1)S(1)} %collective-permute-done.15), channel_id=1, source_target_pairs={{0,2},{1,3},{2,0},{3,1},{4,6},{5,7},{6,4},{7,5},{8,10},{9,11},{10,... | collective-permute-start | bytes 589832 | tf_op jit(solution)/shard_map/ppermute | solution.py:326
  42.4 1.8 %collective-permute-start.12 = (bf16[64,1536]{1,0:T(8,128)(2,1)S(1)}, bf16[64,1536]{1,0:T(8,128)(2,1)S(1)}, u32[]{:S(2)}, u32[]{:S(2)}) collective-permute-start(bf16[64,1536]{1,0:T(8,128)(2,1)S(1)} %collective-permute-done.10.refs_1_), channel_id=1, source_target_pairs={{0,1},{1,0},{2,3},{3,2},{4,5},{5,4},{6,7},{7,6},{8,9},{9,8},{10,11... | collective-permute-start | bytes 589832 | tf_op jit(solution)/shard_map/ppermute | solution.py:326
  42.5 4.5 %copy-start.9 = (bf16[256,1536]{1,0:T(8,128)(2,1)}, bf16[256,1536]{1,0:T(8,128)(2,1)S(1)}, u32[]{:S(2)}) copy-start(bf16[256,1536]{1,0:T(8,128)(2,1)S(1)} %collective-permute-done.8) | copy-start | bytes 2359300
  42.6 9.7 %collective-permute-start.17 = (bf16[256,768]{1,0:T(8,128)(2,1)S(1)}, bf16[256,768]{1,0:T(8,128)(2,1)S(1)}, u32[]{:S(2)}, u32[]{:S(2)}) collective-permute-start(bf16[256,768]{1,0:T(8,128)(2,1)S(1)} %add_convert_fusion.3), channel_id=1, source_target_pairs={{0,16},{1,9},{2,18},{3,11},{4,20},{5,13},{6,22},{7,15},{8,24},{9,1... | collective-permute-start | bytes 1179656 | tf_op jit(solution)/shard_map/ppermute | solution.py:323
  47.0 18.1 %copy-start.4 = (f32[256,1536]{1,0:T(8,128)}, f32[256,1536]{1,0:T(8,128)S(1)}, u32[]{:S(2)}) copy-start(f32[256,1536]{1,0:T(8,128)S(1)} %get-tuple-element.71) | copy-start | bytes 4718596
  48.7 3.5 %collective-permute-start.18 = (bf16[128,1536]{1,0:T(8,128)(2,1)S(1)}, bf16[128,1536]{1,0:T(8,128)(2,1)S(1)}, u32[]{:S(2)}, u32[]{:S(2)}) collective-permute-start(bf16[128,1536]{1,0:T(8,128)(2,1)S(1)} %constant_dynamic-update-slice_fusion.2.refs_0_), channel_id=1, source_target_pairs={{0,1},{1,0},{2,3},{3,2},{4,5},{5,4},{6,7},{7,6},{8,9},{9,8},{10,11... | collective-permute-start | bytes 1179656 | tf_op jit(solution)/shard_map/ppermute | solution.py:326
  48.8 16.3 %collective-permute-start.13 = (bf16[256,1536]{1,0:T(8,128)(2,1)S(1)}, bf16[256,1536]{1,0:T(8,128)(2,1)S(1)}, u32[]{:S(2)}, u32[]{:S(2)}) collective-permute-start(bf16[256,1536]{1,0:T(8,128)(2,1)S(1)} %get-tuple-element.72), channel_id=1, source_target_pairs={{0,8},{1,17},{2,10},{3,19},{4,12},{5,21},{6,14},{7,23},{8,0},{9,25... | collective-permute-start | bytes 2359304 | tf_op jit(solution)/shard_map/ppermute | solution.py:320
  50.6 12.1 %collective-permute-start.14 = (bf16[256,768]{1,0:T(8,128)(2,1)S(1)}, bf16[256,768]{1,0:T(8,128)(2,1)S(1)}, u32[]{:S(2)}, u32[]{:S(2)}) collective-permute-start(bf16[256,768]{1,0:T(8,128)(2,1)S(1)} %add_convert_fusion.2), channel_id=1, source_target_pairs={{0,16},{1,9},{2,18},{3,11},{4,20},{5,13},{6,22},{7,15},{8,24},{9,1... | collective-permute-start | bytes 1179656 | tf_op jit(solution)/shard_map/ppermute | solution.py:323
  56.1 21.7 %collective-permute-start.20 = (bf16[256,1536]{1,0:T(8,128)(2,1)}, bf16[256,1536]{1,0:T(8,128)(2,1)}, u32[]{:S(2)}, u32[]{:S(2)}) collective-permute-start(bf16[256,1536]{1,0:T(8,128)(2,1)} %get-tuple-element.76), channel_id=1, source_target_pairs={{0,8},{1,17},{2,10},{3,19},{4,12},{5,21},{6,14},{7,23},{8,0},{9,25... | collective-permute-start | bytes 2359304 | tf_op jit(solution)/shard_map/ppermute | solution.py:320
  62.7 3.3 %copy-start.14 = (bf16[256,768]{1,0:T(8,128)(2,1)}, bf16[256,768]{1,0:T(8,128)(2,1)S(1)}, u32[]{:S(2)}) copy-start(bf16[256,768]{1,0:T(8,128)(2,1)S(1)} %collective-permute-done.14) | copy-start | bytes 1179652
  66.1 14.4 %collective-permute-start.19 = (bf16[256,768]{1,0:T(8,128)(2,1)}, bf16[256,768]{1,0:T(8,128)(2,1)}, u32[]{:S(2)}, u32[]{:S(2)}) collective-permute-start(bf16[256,768]{1,0:T(8,128)(2,1)} %add_convert_fusion.1), channel_id=1, source_target_pairs={{0,16},{1,9},{2,18},{3,11},{4,20},{5,13},{6,22},{7,15},{8,24},{9,1... | collective-permute-start | bytes 1179656 | tf_op jit(solution)/shard_map/ppermute | solution.py:323
  67.4 13.1 %copy-start.3 = (f32[256,1536]{1,0:T(8,128)S(1)}, f32[256,1536]{1,0:T(8,128)}, u32[]{:S(2)}) copy-start(f32[256,1536]{1,0:T(8,128)} %copy-done.2) | copy-start | bytes 4718596
  79.1 10.6 %copy-start.1 = (f32[256,1536]{1,0:T(8,128)S(1)}, f32[256,1536]{1,0:T(8,128)}, u32[]{:S(2)}) copy-start(f32[256,1536]{1,0:T(8,128)} %copy-done) | copy-start | bytes 4718596
  79.1 10.6 %copy-start.6 = (f32[256,1536]{1,0:T(8,128)S(1)}, f32[256,1536]{1,0:T(8,128)}, u32[]{:S(2)}) copy-start(f32[256,1536]{1,0:T(8,128)} %copy-done.5) | copy-start | bytes 4718596
  79.1 10.6 %copy-start.11 = (bf16[256,1536]{1,0:T(8,128)(2,1)S(1)}, bf16[256,1536]{1,0:T(8,128)(2,1)}, u32[]{:S(2)}) copy-start(bf16[256,1536]{1,0:T(8,128)(2,1)} %copy-done.10) | copy-start | bytes 2359300
  79.2 10.6 %collective-permute-start.22 = (bf16[256,768]{1,0:T(8,128)(2,1)S(1)}, bf16[256,768]{1,0:T(8,128)(2,1)S(1)}, u32[]{:S(2)}, u32[]{:S(2)}) collective-permute-start(bf16[256,768]{1,0:T(8,128)(2,1)S(1)} %add_convert_fusion), channel_id=1, source_target_pairs={{0,16},{1,9},{2,18},{3,11},{4,20},{5,13},{6,22},{7,15},{8,24},{9,1... | collective-permute-start | bytes 1179656 | tf_op jit(solution)/shard_map/ppermute | solution.py:323
  82.7 12.0 %collective-permute-start.25 = (bf16[256,768]{1,0:T(8,128)(2,1)S(1)}, bf16[256,768]{1,0:T(8,128)(2,1)S(1)}, u32[]{:S(2)}, u32[]{:S(2)}) collective-permute-start(bf16[256,768]{1,0:T(8,128)(2,1)S(1)} %get-tuple-element.121), channel_id=1, source_target_pairs={{0,8},{1,17},{2,10},{3,19},{4,12},{5,21},{6,14},{7,23},{8,0},{9,25... | collective-permute-start | bytes 1179656 | tf_op jit(solution)/shard_map/ppermute | solution.py:320
  84.5 10.3 %collective-permute-start.21 = (bf16[256,768]{1,0:T(8,128)(2,1)S(1)}, bf16[256,768]{1,0:T(8,128)(2,1)S(1)}, u32[]{:S(2)}, u32[]{:S(2)}) collective-permute-start(bf16[256,768]{1,0:T(8,128)(2,1)S(1)} %get-tuple-element.122), channel_id=1, source_target_pairs={{0,8},{1,17},{2,10},{3,19},{4,12},{5,21},{6,14},{7,23},{8,0},{9,25... | collective-permute-start | bytes 1179656 | tf_op jit(solution)/shard_map/ppermute | solution.py:320
  91.5 8.7 %collective-permute-start.24 = (bf16[256,768]{1,0:T(8,128)(2,1)S(1)}, bf16[256,768]{1,0:T(8,128)(2,1)S(1)}, u32[]{:S(2)}, u32[]{:S(2)}) collective-permute-start(bf16[256,768]{1,0:T(8,128)(2,1)S(1)} %get-tuple-element.119), channel_id=1, source_target_pairs={{0,8},{1,17},{2,10},{3,19},{4,12},{5,21},{6,14},{7,23},{8,0},{9,25... | collective-permute-start | bytes 1179656 | tf_op jit(solution)/shard_map/ppermute | solution.py:320
  94.4 11.8 %collective-permute-start.23 = (bf16[256,768]{1,0:T(8,128)(2,1)S(1)}, bf16[256,768]{1,0:T(8,128)(2,1)S(1)}, u32[]{:S(2)}, u32[]{:S(2)}) collective-permute-start(bf16[256,768]{1,0:T(8,128)(2,1)S(1)} %get-tuple-element.120), channel_id=1, source_target_pairs={{0,8},{1,17},{2,10},{3,19},{4,12},{5,21},{6,14},{7,23},{8,0},{9,25... | collective-permute-start | bytes 1179656 | tf_op jit(solution)/shard_map/ppermute | solution.py:320
  100.2 13.4 %collective-permute-start.29 = (bf16[256,1536]{1,0:T(8,128)(2,1)S(1)}, bf16[256,1536]{1,0:T(8,128)(2,1)S(1)}, u32[]{:S(2)}, u32[]{:S(2)}) collective-permute-start(bf16[256,1536]{1,0:T(8,128)(2,1)S(1)} %pad_maximum_fusion.2.near_ref.near1), channel_id=1, source_target_pairs={{0,16},{1,9},{2,18},{3,11},{4,20},{5,13},{6,22},{7,15},{8,24},{9,1... | collective-permute-start | bytes 2359304 | tf_op jit(solution)/shard_map/ppermute | solution.py:323
  106.2 14.5 %collective-permute-start.28 = (bf16[256,1536]{1,0:T(8,128)(2,1)S(1)}, bf16[256,1536]{1,0:T(8,128)(2,1)S(1)}, u32[]{:S(2)}, u32[]{:S(2)}) collective-permute-start(bf16[256,1536]{1,0:T(8,128)(2,1)S(1)} %pad_maximum_fusion.1.near_ref.near0), channel_id=1, source_target_pairs={{0,16},{1,9},{2,18},{3,11},{4,20},{5,13},{6,22},{7,15},{8,24},{9,1... | collective-permute-start | bytes 2359304 | tf_op jit(solution)/shard_map/ppermute | solution.py:323
  106.2 7.4 %slice-start.3 = ((s8[9437184]{0:T(1024)(128)(4,1)}), s8[4194304]{0:T(1024)(128)(4,1)S(1)}, s32[]{:S(2)}) async-start(s8[9437184]{0:T(1024)(128)(4,1)} %bitcast.22), calls=%async_computation.3 | async-start | bytes 8388608
  106.2 7.4 %slice-start.4 = ((s8[9437184]{0:T(1024)(128)(4,1)}), s8[4194304]{0:T(1024)(128)(4,1)S(1)}, s32[]{:S(2)}) async-start(s8[9437184]{0:T(1024)(128)(4,1)} %bitcast.22), calls=%async_computation.4 | async-start | bytes 8388608
  106.2 7.4 %slice-start.5 = ((s8[9437184]{0:T(1024)(128)(4,1)}), s8[1048576]{0:T(1024)(128)(4,1)S(1)}, s32[]{:S(2)}) async-start(s8[9437184]{0:T(1024)(128)(4,1)} %bitcast.22), calls=%async_computation.5 | async-start | bytes 2097152
  106.3 23.9 %collective-permute-start.27 = (bf16[256,1536]{1,0:T(8,128)(2,1)S(1)}, bf16[256,1536]{1,0:T(8,128)(2,1)S(1)}, u32[]{:S(2)}, u32[]{:S(2)}) collective-permute-start(bf16[256,1536]{1,0:T(8,128)(2,1)S(1)} %pad_maximum_fusion.3.p1.near_ref), channel_id=1, source_target_pairs={{0,16},{1,9},{2,18},{3,11},{4,20},{5,13},{6,22},{7,15},{8,24},{9,1... | collective-permute-start | bytes 2359304 | tf_op jit(solution)/shard_map/ppermute | solution.py:323
  116.3 16.6 %collective-permute-start.32 = (bf16[128,1536]{1,0:T(8,128)(2,1)S(1)}, bf16[128,1536]{1,0:T(8,128)(2,1)S(1)}, u32[]{:S(2)}, u32[]{:S(2)}) collective-permute-start(bf16[128,1536]{1,0:T(8,128)(2,1)S(1)} %get-tuple-element.88), channel_id=1, source_target_pairs={{0,1},{1,0},{2,3},{3,2},{4,5},{5,4},{6,7},{7,6},{8,9},{9,8},{10,11... | collective-permute-start | bytes 1179656 | tf_op jit(solution)/shard_map/ppermute | solution.py:326
  116.4 13.8 %slice-start.6 = ((s8[9437184]{0:T(1024)(128)(4,1)}), s8[4194304]{0:T(1024)(128)(4,1)S(1)}, s32[]{:S(2)}) async-start(s8[9437184]{0:T(1024)(128)(4,1)} %bitcast.24), calls=%async_computation.6 | async-start | bytes 8388608
  117.2 30.5 %collective-permute-start.26 = (bf16[256,1536]{1,0:T(8,128)(2,1)S(1)}, bf16[256,1536]{1,0:T(8,128)(2,1)S(1)}, u32[]{:S(2)}, u32[]{:S(2)}) collective-permute-start(bf16[256,1536]{1,0:T(8,128)(2,1)S(1)} %pad_maximum_fusion.p0.near_ref), channel_id=1, source_target_pairs={{0,16},{1,9},{2,18},{3,11},{4,20},{5,13},{6,22},{7,15},{8,24},{9,1... | collective-permute-start | bytes 2359304 | tf_op jit(solution)/shard_map/ppermute | solution.py:323
  120.7 9.5 %slice-start.7 = ((s8[9437184]{0:T(1024)(128)(4,1)}), s8[4194304]{0:T(1024)(128)(4,1)S(1)}, s32[]{:S(2)}) async-start(s8[9437184]{0:T(1024)(128)(4,1)} %bitcast.24), calls=%async_computation.7 | async-start | bytes 8388608
  120.7 9.5 %slice-start.8 = ((s8[9437184]{0:T(1024)(128)(4,1)}), s8[1048576]{0:T(1024)(128)(4,1)S(1)}, s32[]{:S(2)}) async-start(s8[9437184]{0:T(1024)(128)(4,1)} %bitcast.24), calls=%async_computation.8 | async-start | bytes 2097152
  123.4 12.2 %collective-permute-start.30 = (bf16[144,1536]{1,0:T(8,128)(2,1)S(1)}, bf16[144,1536]{1,0:T(8,128)(2,1)S(1)}, u32[]{:S(2)}, u32[]{:S(2)}) collective-permute-start(bf16[144,1536]{1,0:T(8,128)(2,1)S(1)} %get-tuple-element.91), channel_id=1, source_target_pairs={{0,1},{1,0},{2,3},{3,2},{4,5},{5,4},{6,7},{7,6},{8,9},{9,8},{10,11... | collective-permute-start | bytes 1327112 | tf_op jit(solution)/shard_map/ppermute | solution.py:326
  132.8 1.8 %collective-permute-start.31 = (bf16[128,1536]{1,0:T(8,128)(2,1)S(1)}, bf16[128,1536]{1,0:T(8,128)(2,1)S(1)}, u32[]{:S(2)}, u32[]{:S(2)}) collective-permute-start(bf16[128,1536]{1,0:T(8,128)(2,1)S(1)} %get-tuple-element.95), channel_id=1, source_target_pairs={{0,1},{1,0},{2,3},{3,2},{4,5},{5,4},{6,7},{7,6},{8,9},{9,8},{10,11... | collective-permute-start | bytes 1179656 | tf_op jit(solution)/shard_map/ppermute | solution.py:326
  133.1 7.8 %collective-permute-start.33 = (bf16[64,1536]{1,0:T(8,128)(2,1)S(1)}, bf16[64,1536]{1,0:T(8,128)(2,1)S(1)}, u32[]{:S(2)}, u32[]{:S(2)}) collective-permute-start(bf16[64,1536]{1,0:T(8,128)(2,1)S(1)} %slice.228), channel_id=1, source_target_pairs={{0,2},{1,3},{2,0},{3,1},{4,6},{5,7},{6,4},{7,5},{8,10},{9,11},{10,... | collective-permute-start | bytes 589832 | tf_op jit(solution)/shard_map/ppermute | solution.py:326
  135.0 15.4 %collective-permute-start.36 = (bf16[64,1536]{1,0:T(8,128)(2,1)S(1)}, bf16[64,1536]{1,0:T(8,128)(2,1)S(1)}, u32[]{:S(2)}, u32[]{:S(2)}) collective-permute-start(bf16[64,1536]{1,0:T(8,128)(2,1)S(1)} %slice.226), channel_id=1, source_target_pairs={{0,2},{1,3},{2,0},{3,1},{4,6},{5,7},{6,4},{7,5},{8,10},{9,11},{10,... | collective-permute-start | bytes 589832 | tf_op jit(solution)/shard_map/ppermute | solution.py:326
  135.9 18.2 %collective-permute-start.38 = (bf16[80,1536]{1,0:T(8,128)(2,1)S(1)}, bf16[80,1536]{1,0:T(8,128)(2,1)S(1)}, u32[]{:S(2)}, u32[]{:S(2)}) collective-permute-start(bf16[80,1536]{1,0:T(8,128)(2,1)S(1)} %pad_maximum_fusion.4), channel_id=1, source_target_pairs={{0,2},{1,3},{2,0},{3,1},{4,6},{5,7},{6,4},{7,5},{8,10},{9,11},{10,... | collective-permute-start | bytes 737288 | tf_op jit(solution)/shard_map/ppermute | solution.py:326
  140.9 15.0 %collective-permute-start.39 = (bf16[64,1536]{1,0:T(8,128)(2,1)S(1)}, bf16[64,1536]{1,0:T(8,128)(2,1)S(1)}, u32[]{:S(2)}, u32[]{:S(2)}) collective-permute-start(bf16[64,1536]{1,0:T(8,128)(2,1)S(1)} %slice_add_fusion.4), channel_id=1, source_target_pairs={{0,4},{1,5},{2,6},{3,7},{4,0},{5,1},{6,2},{7,3},{8,12},{9,13},{10,... | collective-permute-start | bytes 589832 | tf_op jit(solution)/shard_map/ppermute | solution.py:326
  150.3 7.9 %collective-permute-start.34 = (bf16[128,1536]{1,0:T(8,128)(2,1)S(1)}, bf16[128,1536]{1,0:T(8,128)(2,1)S(1)}, u32[]{:S(2)}, u32[]{:S(2)}) collective-permute-start(bf16[128,1536]{1,0:T(8,128)(2,1)S(1)} %get-tuple-element.103), channel_id=1, source_target_pairs={{0,1},{1,0},{2,3},{3,2},{4,5},{5,4},{6,7},{7,6},{8,9},{9,8},{10,11... | collective-permute-start | bytes 1179656 | tf_op jit(solution)/shard_map/ppermute | solution.py:326
  150.5 21.2 %collective-permute-start.37 = (bf16[64,1536]{1,0:T(8,128)(2,1)S(1)}, bf16[64,1536]{1,0:T(8,128)(2,1)S(1)}, u32[]{:S(2)}, u32[]{:S(2)}) collective-permute-start(bf16[64,1536]{1,0:T(8,128)(2,1)S(1)} %slice_add_fusion.2), channel_id=1, source_target_pairs={{0,4},{1,5},{2,6},{3,7},{4,0},{5,1},{6,2},{7,3},{8,12},{9,13},{10,... | collective-permute-start | bytes 589832 | tf_op jit(solution)/shard_map/ppermute | solution.py:326
  154.2 10.4 %collective-permute-start.42 = (f32[1,1536]{1,0:T(1,128)S(1)}, f32[1,1536]{1,0:T(1,128)S(1)}, u32[]{:S(2)}, u32[]{:S(2)}) collective-permute-start(f32[1,1536]{1,0:T(1,128)S(1)} %fusion.27), channel_id=1, source_target_pairs={{0,4},{1,5},{2,6},{3,7},{4,0},{5,1},{6,2},{7,3},{8,12},{9,13},{10,... | collective-permute-start | bytes 18440 | tf_op jit(solution)/shard_map/ppermute | solution.py:326
  156.1 7.5 %collective-permute-start.40 = (f32[2,64]{1,0:T(2,128)S(1)}, f32[2,64]{1,0:T(2,128)S(1)}, u32[]{:S(2)}, u32[]{:S(2)}) collective-permute-start(f32[2,64]{1,0:T(2,128)S(1)} %pad_maximum_fusion.6), channel_id=1, source_target_pairs={{0,8},{8,0},{16,24},{24,16},{1,9},{9,1},{17,25},{25,17},{2,10},{10... | collective-permute-start | bytes 1544 | tf_op jit(solution)/shard_map/ppermute | solution.py:329
  158.3 13.4 %copy-start.16 = (f32[1536]{0:T(1024)S(1)}, f32[1536]{0:T(1024)}, u32[]{:S(2)}) copy-start(f32[1536]{0:T(1024)} %param.12) | copy-start | bytes 18436
  163.6 4.2 %collective-permute-start.41 = (f32[2,64]{1,0:T(2,128)S(1)}, f32[2,64]{1,0:T(2,128)S(1)}, u32[]{:S(2)}, u32[]{:S(2)}) collective-permute-start(f32[2,64]{1,0:T(2,128)S(1)} %fusion.31), channel_id=1, source_target_pairs={{0,16},{8,24},{16,0},{24,8},{1,17},{9,25},{17,1},{25,9},{2,18},{10... | collective-permute-start | bytes 1544 | tf_op jit(solution)/shard_map/ppermute | solution.py:329
  165.2 6.5 %collective-permute-start.35 = (bf16[64,1536]{1,0:T(8,128)(2,1)S(1)}, bf16[64,1536]{1,0:T(8,128)(2,1)S(1)}, u32[]{:S(2)}, u32[]{:S(2)}) collective-permute-start(bf16[64,1536]{1,0:T(8,128)(2,1)S(1)} %slice.227), channel_id=1, source_target_pairs={{0,2},{1,3},{2,0},{3,1},{4,6},{5,7},{6,4},{7,5},{8,10},{9,11},{10,... | collective-permute-start | bytes 589832 | tf_op jit(solution)/shard_map/ppermute | solution.py:326
  (5 other events, 8.7 us)

commit v5 on v4

--- a/solution.py
+++ b/solution.py
@@ -499,12 +499,12 @@
         grad_normed = grad_sums_w[:rows] + after(came, go) + grad_far
         scaled = grad_normed * norm_gain
         sums = jnp.stack([jnp.sum(scaled, axis=1), jnp.sum(scaled * standard, axis=1)])
-        sums = sums + after(along_gx(sums, 1), grad_w_down)
+        sums = sums + along_gx(sums, 1)
         mlp_home = sums_w[:rows] + after(along_gy(sums_w[rows:].astype(bf16), 2), grad_w_down).astype(f32)
         held = [after(h, grad_w_up) for h in held]
         mlp_out = (mlp_home + from_far(held)[0] + bias_down).astype(bf16)
         for step in bits(chips)[1:]:
-            gain = gain + along_gy(gain, 2 * step)
+            gain = gain + after(along_gy(gain, 2 * step), grad_w_down)
         grad_gain = gain[0] / norm_gain
 
         grad_bias_down = jnp.sum(cot_w.astype(f32), axis=0) + jnp.sum(cot_x.astype(f32), axis=0)

time: 173 us -> 171 us (0.988)
    ppermute x23, waiting for transfers between devices: 25.2 us -> 22.9 us  [along_gy(): return lax.ppermute(x, 'gy', [(i, i ^ m) for i in range(n_gy)])]
  transfers between devices with their start and end apart: 43 -> 43, of which waited for: 19 -> 20; matrix products, arithmetic and copies ran while one was open for 7% -> 7% of each run, Pallas kernels for 28% -> 28%
where the time goes in v5:
time: 171 us
  waiting for transfers between devices  61.1 us (36%)
  Pallas kernels  47.6 us (28%)
  starting transfers between devices  45.7 us (27%)
  other arithmetic  12 us (7%)
  local copies, waits for them, and re-layouts  3.34 us (2%)
    ppermute x23, waiting for transfers between devices, along_gy(): return lax.ppermute(x, 'gy', [(i, i ^ m) for i in range(n_gy)])  22.9 us
    ppermute x8, waiting for transfers between devices, to_first(): return lax.ppermute(x, both, first_pairs)  22.6 us
    ppermute x23, starting transfers between devices, along_gy(): return lax.ppermute(x, 'gy', [(i, i ^ m) for i in range(n_gy)])  18.7 us
    ppermute x8, waiting for transfers between devices, to_second(): return lax.ppermute(x, both, second_pairs)  13.8 us
    pallas_call x2, Pallas kernels, weight_grad_up(): call(kernel, name, out_shape, [IN_SMEM] + [IN_VMEM] * 6 + ([] if sums els...  11.5 us
    ppermute x8, starting transfers between devices, to_first(): return lax.ppermute(x, both, first_pairs)  10.7 us
    pallas_call x2, Pallas kernels, weight_grad_down(): call(kernel, name, jax.ShapeDtypeStruct((units, out), f32), [IN_SMEM] + [...  10.4 us
    ppermute x8, starting transfers between devices, to_second(): return lax.ppermute(x, both, second_pairs)  10.1 us
  transfers between devices with their start and end apart: 43, of which 20 were waited for; matrix products, arithmetic and copies ran while one was open for 7% of the time, Pallas kernels for 28%

profile of v5, /device:TPU:0, one launch (start us, length us, event | category | flops | bytes accessed | tf_op | source)
XLA Modules:
  0.0 171.2 jit_solution(8286334982857644495)
XLA Ops:
  0.6 3.1 %collective-permute-start.1 = (bf16[64,1536]{1,0:T(8,128)(2,1)}, bf16[64,1536]{1,0:T(8,128)(2,1)S(1)}, u32[]{:S(2)}, u32[]{:S(2)}) collective-permute-start(bf16[64,1536]{1,0:T(8,128)(2,1)} %refs_0_.1), channel_id=1, source_target_pairs={{0,2},{1,3},{2,0},{3,1},{4,6},{5,7},{6,4},{7,5},{8,10},{9,11},{10,... | collective-permute-start | bytes 589832 | tf_op jit(solution)/shard_map/ppermute | solution.py:326
  3.7 2.6 %collective-permute-start.5 = (bf16[64,1536]{1,0:T(8,128)(2,1)}, bf16[64,1536]{1,0:T(8,128)(2,1)S(1)}, u32[]{:S(2)}, u32[]{:S(2)}) collective-permute-start(bf16[64,1536]{1,0:T(8,128)(2,1)} %refs_0_.1), channel_id=1, source_target_pairs={{0,4},{1,5},{2,6},{3,7},{4,0},{5,1},{6,2},{7,3},{8,12},{9,13},{10,... | collective-permute-start | bytes 589832 | tf_op jit(solution)/shard_map/ppermute | solution.py:326
  6.3 1.1 convert_reduce_fusion.2
  7.4 1.6 collective-permute-start
  9.0 2.6 %collective-permute-done.1.refs_1_ = bf16[64,1536]{1,0:T(8,128)(2,1)S(1)} collective-permute-done((bf16[64,1536]{1,0:T(8,128)(2,1)}, bf16[64,1536]{1,0:T(8,128)(2,1)S(1)}, u32[]{:S(2)}, u32[]{:S(2)}) %collective-permute-start.1) | collective-permute-done | bytes 196640 | tf_op jit(solution)/shard_map/ppermute | solution.py:326
  11.6 1.4 collective-permute-done.3.refs_3_
  13.0 0.9 copy-done.7
  14.0 3.8 %grad_act_w_go.1 = (bf16[256,1536]{1,0:T(8,128)(2,1)S(1)}, bf16[1536,1536]{1,0:T(8,128)(2,1)S(1)}, bf16[256,1536]{1,0:T(8,128)(2,1)S(1)}) custom-call(s32[1]{0:T(128)} %bitcast.me_ref.refs_4_.refs_2_, bf16[64,1536]{1,0:T(8,128)(2,1)S(1)} %copy-done.7, bf16[64,1536]{1,0:T(8,128)(2,1)S(1)} %collective-permute-done.1.refs_1_, ...), custom_call_target="tpu_custom_call" | custom-call | tf_op jit(solution)/shard_map/grad_act_w_go/pallas_call | solution.py:94
  17.8 1.9 %collective-permute-start.4 = (f32[2,64]{1,0:T(2,128)S(1)}, f32[2,64]{1,0:T(2,128)S(1)}, u32[]{:S(2)}, u32[]{:S(2)}) collective-permute-start(f32[2,64]{1,0:T(2,128)S(1)} %fusion.32), channel_id=1, source_target_pairs={{0,16},{8,24},{16,0},{24,8},{1,17},{9,25},{17,1},{25,9},{2,18},{10... | collective-permute-start | bytes 1544 | tf_op jit(solution)/shard_map/ppermute | solution.py:329
  19.8 1.6 collective-permute-start.8
  21.5 4.9 %collective-permute-done.6 = bf16[64,1536]{1,0:T(8,128)(2,1)S(1)} collective-permute-done((bf16[64,1536]{1,0:T(8,128)(2,1)S(1)}, bf16[64,1536]{1,0:T(8,128)(2,1)S(1)}, u32[]{:S(2)}, u32[]{:S(2)}) %collective-permute-start.6) | collective-permute-done | bytes 196640 | tf_op jit(solution)/shard_map/ppermute | solution.py:326
  26.5 1.7 collective-permute-done.7.refs_1_
  28.2 1.4 grad_act_x_go.1
  29.6 1.6 collective-permute-start.9
  31.3 1.6 collective-permute-start.15
  32.9 1.7 %collective-permute-start.10 = (bf16[64,1536]{1,0:T(8,128)(2,1)S(1)}, bf16[64,1536]{1,0:T(8,128)(2,1)S(1)}, u32[]{:S(2)}, u32[]{:S(2)}) collective-permute-start(bf16[64,1536]{1,0:T(8,128)(2,1)S(1)} %fusion.17.refs_0_), channel_id=1, source_target_pairs={{0,2},{1,3},{2,0},{3,1},{4,6},{5,7},{6,4},{7,5},{8,10},{9,11},{10,... | collective-permute-start | bytes 589832 | tf_op jit(solution)/shard_map/ppermute | solution.py:326
  34.7 4.6 %grad_act_keep.1 = (f32[256,1536]{1,0:T(8,128)S(1)}, f32[256,1536]{1,0:T(8,128)S(1)}) custom-call(s32[1]{0:T(128)} %bitcast.me_ref.refs_4_.refs_2_, bf16[256,1536]{1,0:T(8,128)(2,1)S(1)} %get-tuple-element.61.refs_0_.c0, bf16[256,1536]{1,0:T(8,128)(2,1)S(1)} %get-tuple-element.65.refs_1_.c1, bf16[3072,1536]{1,0:T(8,128)(2,1)} %w_ref.7), custom_call_target="tpu_custom_call" | custom-call | tf_op jit(solution)/shard_map/grad_act_keep/pallas_call | solution.py:94
  39.3 2.9 %collective-permute-done.15 = bf16[64,1536]{1,0:T(8,128)(2,1)S(1)} collective-permute-done((bf16[64,1536]{1,0:T(8,128)(2,1)S(1)}, bf16[64,1536]{1,0:T(8,128)(2,1)S(1)}, u32[]{:S(2)}, u32[]{:S(2)}) %collective-permute-start.15) | collective-permute-done | bytes 196640 | tf_op jit(solution)/shard_map/ppermute | solution.py:326
  42.6 1.5 collective-permute-start.17
  44.3 2.7 %hidden_w.1 = (bf16[256,1536]{1,0:T(8,128)(2,1)S(1)}, f32[256,1536]{1,0:T(8,128)S(1)}, bf16[256,1536]{1,0:T(8,128)(2,1)S(1)}) custom-call(bf16[64,1536]{1,0:T(8,128)(2,1)S(1)} %fusion.17.refs_0_, bf16[64,1536]{1,0:T(8,128)(2,1)S(1)} %collective-permute-done.10.refs_1_, bf16[64,1536]{1,0:T(8,128)(2,1)S(1)} %collective-permute-done.11.refs_2_, ...), custom_call_target="tpu_custom_call" | custom-call | tf_op jit(solution)/shard_map/hidden_w/pallas_call | solution.py:127
  47.0 1.7 collective-permute-done.16
  48.8 1.8 %collective-permute-start.13 = (bf16[256,1536]{1,0:T(8,128)(2,1)S(1)}, bf16[256,1536]{1,0:T(8,128)(2,1)S(1)}, u32[]{:S(2)}, u32[]{:S(2)}) collective-permute-start(bf16[256,1536]{1,0:T(8,128)(2,1)S(1)} %get-tuple-element.72), channel_id=1, source_target_pairs={{0,8},{1,17},{2,10},{3,19},{4,12},{5,21},{6,14},{7,23},{8,0},{9,25... | collective-permute-start | bytes 2359304 | tf_op jit(solution)/shard_map/ppermute | solution.py:320
  50.6 1.6 collective-permute-start.14
  52.3 2.7 %hidden_x.1 = (bf16[256,1536]{1,0:T(8,128)(2,1)}, f32[256,1536]{1,0:T(8,128)S(1)}, bf16[256,1536]{1,0:T(8,128)(2,1)S(1)}) custom-call(bf16[128,1536]{1,0:T(8,128)(2,1)S(1)} %constant_dynamic-update-slice_fusion.2.refs_0_, bf16[128,1536]{1,0:T(8,128)(2,1)S(1)} %collective-permute-done.18.refs_1_, s32[1]{0:T(128)} %bitcast.me_ref.refs_4_.refs_2_, ...), custom_call_target="tpu_custom_call" | custom-call | tf_op jit(solution)/shard_map/hidden_x/pallas_call | solution.py:127
  55.0 1.1 copy-done.5
  56.5 6.1 %collective-permute-done.14 = bf16[256,768]{1,0:T(8,128)(2,1)S(1)} collective-permute-done((bf16[256,768]{1,0:T(8,128)(2,1)S(1)}, bf16[256,768]{1,0:T(8,128)(2,1)S(1)}, u32[]{:S(2)}, u32[]{:S(2)}) %collective-permute-start.14) | collective-permute-done | bytes 393248 | tf_op jit(solution)/shard_map/ppermute | solution.py:323
  62.7 2.4 %collective-permute-done.13 = bf16[256,1536]{1,0:T(8,128)(2,1)S(1)} collective-permute-done((bf16[256,1536]{1,0:T(8,128)(2,1)S(1)}, bf16[256,1536]{1,0:T(8,128)(2,1)S(1)}, u32[]{:S(2)}, u32[]{:S(2)}) %collective-permute-start.13) | collective-permute-done | bytes 786464 | tf_op jit(solution)/shard_map/ppermute | solution.py:320
  65.1 1.0 add_convert_fusion.1
  66.1 1.3 collective-permute-start.19
  67.4 0.9 dynamic_slice.3
  68.3 9.5 %collective-permute-done.20 = bf16[256,1536]{1,0:T(8,128)(2,1)} collective-permute-done((bf16[256,1536]{1,0:T(8,128)(2,1)}, bf16[256,1536]{1,0:T(8,128)(2,1)}, u32[]{:S(2)}, u32[]{:S(2)}) %collective-permute-start.20) | collective-permute-done | bytes 786464 | tf_op jit(solution)/shard_map/ppermute | solution.py:320
  77.8 1.3 add_convert_fusion
  79.2 1.3 collective-permute-start.22
  80.5 2.2 %fusion.5 = (bf16[256,768]{1,0:T(8,128)(2,1)S(1)}, bf16[256,768]{1,0:T(8,128)(2,1)S(1)}) fusion(bf16[256,768]{1,0:T(8,128)(2,1)} %copy-done.13, f32[256,1536]{1,0:T(8,128)S(1)} %copy-done.3, bf16[256,1536]{1,0:T(8,128)(2,1)} %copy-done.9, f32[768]{0:T(1024)S(1)} %dynamic_slice.3, bf16[256,768]{1,0:T(8,128)(2,1)} %collective-permute-done.19, ...), kind=kLoop, calls=%fused_computation.9 | loop fusion | flops 4128768 | bytes 3935232 | tf_op jit(solution)/shard_map/convert_element_type | solution.py:414
  82.7 1.8 %collective-permute-start.25 = (bf16[256,768]{1,0:T(8,128)(2,1)S(1)}, bf16[256,768]{1,0:T(8,128)(2,1)S(1)}, u32[]{:S(2)}, u32[]{:S(2)}) collective-permute-start(bf16[256,768]{1,0:T(8,128)(2,1)S(1)} %get-tuple-element.121), channel_id=1, source_target_pairs={{0,8},{1,17},{2,10},{3,19},{4,12},{5,21},{6,14},{7,23},{8,0},{9,25... | collective-permute-start | bytes 1179656 | tf_op jit(solution)/shard_map/ppermute | solution.py:320
  84.8 4.9 %collective-permute-done.22 = bf16[256,768]{1,0:T(8,128)(2,1)S(1)} collective-permute-done((bf16[256,768]{1,0:T(8,128)(2,1)S(1)}, bf16[256,768]{1,0:T(8,128)(2,1)S(1)}, u32[]{:S(2)}, u32[]{:S(2)}) %collective-permute-start.22) | collective-permute-done | bytes 393248 | tf_op jit(solution)/shard_map/ppermute | solution.py:323
  89.8 1.7 fusion.11
  91.5 2.9 %collective-permute-start.24 = (bf16[256,768]{1,0:T(8,128)(2,1)S(1)}, bf16[256,768]{1,0:T(8,128)(2,1)S(1)}, u32[]{:S(2)}, u32[]{:S(2)}) collective-permute-start(bf16[256,768]{1,0:T(8,128)(2,1)S(1)} %get-tuple-element.119), channel_id=1, source_target_pairs={{0,8},{1,17},{2,10},{3,19},{4,12},{5,21},{6,14},{7,23},{8,0},{9,25... | collective-permute-start | bytes 1179656 | tf_op jit(solution)/shard_map/ppermute | solution.py:320
  94.8 5.3 %collective-permute-done.24 = bf16[256,768]{1,0:T(8,128)(2,1)S(1)} collective-permute-done((bf16[256,768]{1,0:T(8,128)(2,1)S(1)}, bf16[256,768]{1,0:T(8,128)(2,1)S(1)}, u32[]{:S(2)}, u32[]{:S(2)}) %collective-permute-start.24) | collective-permute-done | bytes 393248 | tf_op jit(solution)/shard_map/ppermute | solution.py:320
  100.9 5.3 %collective-permute-done.23 = bf16[256,768]{1,0:T(8,128)(2,1)S(1)} collective-permute-done((bf16[256,768]{1,0:T(8,128)(2,1)S(1)}, bf16[256,768]{1,0:T(8,128)(2,1)S(1)}, u32[]{:S(2)}, u32[]{:S(2)}) %collective-permute-start.23) | collective-permute-done | bytes 393248 | tf_op jit(solution)/shard_map/ppermute | solution.py:320
  106.3 2.1 %collective-permute-start.27 = (bf16[256,1536]{1,0:T(8,128)(2,1)S(1)}, bf16[256,1536]{1,0:T(8,128)(2,1)S(1)}, u32[]{:S(2)}, u32[]{:S(2)}) collective-permute-start(bf16[256,1536]{1,0:T(8,128)(2,1)S(1)} %pad_maximum_fusion.3.p1.near_ref), channel_id=1, source_target_pairs={{0,16},{1,9},{2,18},{3,11},{4,20},{5,13},{6,22},{7,15},{8,24},{9,1... | collective-permute-start | bytes 2359304 | tf_op jit(solution)/shard_map/ppermute | solution.py:323
  108.4 5.2 %wgrad_near.1.refs_0_ = f32[3072,1536]{1,0:T(8,128)} custom-call(s32[1]{0:T(128)} %bitcast.me_ref.refs_4_.refs_2_, bf16[256,1536]{1,0:T(8,128)(2,1)S(1)} %pad_maximum_fusion.p0.near_ref, bf16[256,1536]{1,0:T(8,128)(2,1)S(1)} %pad_maximum_fusion.3.p1.near_ref, bf16[256,1536]{1,0:T(8,128)(2,1)S(1)} %get-tuple-element.61.refs_0_.c0, ...), custom_call_target="tpu_custom_call" | custom-call | tf_op jit(solution)/shard_map/wgrad_near/pallas_call | solution.py:241
  113.7 2.7 %normed_grad_x.1 = (f32[128,1536]{1,0:T(8,128)S(1)}, bf16[128,1536]{1,0:T(8,128)(2,1)S(1)}, f32[1,1536]{1,0:T(1,128)S(1)}) custom-call(s32[1]{0:T(128)} %bitcast.me_ref.refs_4_.refs_2_, bf16[256,1536]{1,0:T(8,128)(2,1)S(1)} %pad_maximum_fusion.2.near_ref.near1, bf16[256,1536]{1,0:T(8,128)(2,1)S(1)} %collective-permute-done.29.far_ref.far1, ...), custom_call_target="tpu_custom_call" | custom-call | tf_op jit(solution)/shard_map/normed_grad_x/pallas_call | solution.py:194
  116.4 1.6 collective-permute-start.26
  118.0 2.7 %collective-permute-done.28.far_ref.far0 = bf16[256,1536]{1,0:T(8,128)(2,1)S(1)} collective-permute-done((bf16[256,1536]{1,0:T(8,128)(2,1)S(1)}, bf16[256,1536]{1,0:T(8,128)(2,1)S(1)}, u32[]{:S(2)}, u32[]{:S(2)}) %collective-permute-start.28) | collective-permute-done | bytes 786464 | tf_op jit(solution)/shard_map/ppermute | solution.py:323
  120.7 2.7 %normed_grad_w.1 = (f32[128,1536]{1,0:T(8,128)S(1)}, bf16[144,1536]{1,0:T(8,128)(2,1)S(1)}, f32[1,1536]{1,0:T(1,128)S(1)}) custom-call(s32[1]{0:T(128)} %bitcast.me_ref.refs_4_.refs_2_, bf16[256,1536]{1,0:T(8,128)(2,1)S(1)} %pad_maximum_fusion.1.near_ref.near0, bf16[256,1536]{1,0:T(8,128)(2,1)S(1)} %collective-permute-done.28.far_ref.far0, ...), custom_call_target="tpu_custom_call" | custom-call | tf_op jit(solution)/shard_map/normed_grad_w/pallas_call | solution.py:194
  124.1 6.1 %wgrad_up_1.1 = (f32[1536,3072]{1,0:T(8,128)}, f32[1,3072]{1,0:T(1,128)}) custom-call(s32[1]{0:T(128)} %bitcast.me_ref.refs_4_.refs_2_, bf16[256,1536]{1,0:T(8,128)(2,1)S(1)} %get-tuple-element.99.n_ref.n0, bf16[256,1536]{1,0:T(8,128)(2,1)S(1)} %get-tuple-element.87.n_ref.n1, bf16[256,1536]{1,0:T(8,128)(2,1)S(1)} %pad_maximum_fusion.1.near_ref.near0, ...), custom_call_target="tpu_custom_call" | custom-call | tf_op jit(solution)/shard_map/wgrad_up_1/pallas_call | solution.py:290
  130.2 2.6 %mlp_x.1 = (f32[128,1536]{1,0:T(8,128)S(1)}, bf16[128,1536]{1,0:T(8,128)(2,1)S(1)}) custom-call(s32[1]{0:T(128)} %bitcast.me_ref.refs_4_.refs_2_, bf16[256,1536]{1,0:T(8,128)(2,1)S(1)} %pad_maximum_fusion.3.p1.near_ref, bf16[256,1536]{1,0:T(8,128)(2,1)S(1)} %collective-permute-done.27.far_ref.p1, bf16[3072,1536]{1,0:T(8,128)(2,1)S(1)} %bitcast.25), custom_call_target="tpu_custom_call" | custom-call | tf_op jit(solution)/shard_map/mlp_x/pallas_call | solution.py:160
  133.4 1.2 collective-permute-done.31
  135.9 1.6 collective-permute-start.38
  137.5 3.4 %collective-permute-done.33 = bf16[64,1536]{1,0:T(8,128)(2,1)S(1)} collective-permute-done((bf16[64,1536]{1,0:T(8,128)(2,1)S(1)}, bf16[64,1536]{1,0:T(8,128)(2,1)S(1)}, u32[]{:S(2)}, u32[]{:S(2)}) %collective-permute-start.33) | collective-permute-done | bytes 196640 | tf_op jit(solution)/shard_map/ppermute | solution.py:326
  140.9 1.5 collective-permute-start.39
  143.2 5.3 %wgrad_up_2.1 = f32[1536,3072]{1,0:T(8,128)} custom-call(s32[1]{0:T(128)} %bitcast.me_ref.refs_4_.refs_2_, bf16[256,1536]{1,0:T(8,128)(2,1)S(1)} %get-tuple-element.99.n_ref.n0, bf16[256,1536]{1,0:T(8,128)(2,1)S(1)} %get-tuple-element.87.n_ref.n1, bf16[256,1536]{1,0:T(8,128)(2,1)S(1)} %pad_maximum_fusion.1.near_ref.near0, ...), custom_call_target="tpu_custom_call", output_to_operand_aliasing={{}: (7, {})} | custom-call | tf_op jit(solution)/shard_map/wgrad_up_2/pallas_call | solution.py:290
  148.6 2.6 %mlp_w.1 = (f32[128,1536]{1,0:T(8,128)S(1)}, bf16[128,1536]{1,0:T(8,128)(2,1)S(1)}) custom-call(s32[1]{0:T(128)} %bitcast.me_ref.refs_4_.refs_2_, bf16[256,1536]{1,0:T(8,128)(2,1)S(1)} %pad_maximum_fusion.p0.near_ref, bf16[256,1536]{1,0:T(8,128)(2,1)S(1)} %collective-permute-done.26.far_ref.p0, bf16[3072,1536]{1,0:T(8,128)(2,1)S(1)} %bitcast.25), custom_call_target="tpu_custom_call" | custom-call | tf_op jit(solution)/shard_map/mlp_w/pallas_call | solution.py:160
  151.3 2.8 %collective-permute-done.38 = bf16[80,1536]{1,0:T(8,128)(2,1)S(1)} collective-permute-done((bf16[80,1536]{1,0:T(8,128)(2,1)S(1)}, bf16[80,1536]{1,0:T(8,128)(2,1)S(1)}, u32[]{:S(2)}, u32[]{:S(2)}) %collective-permute-start.38) | collective-permute-done | bytes 245792 | tf_op jit(solution)/shard_map/ppermute | solution.py:326
  154.4 2.1 %collective-permute-start.40 = (f32[2,64]{1,0:T(2,128)S(1)}, f32[2,64]{1,0:T(2,128)S(1)}, u32[]{:S(2)}, u32[]{:S(2)}) collective-permute-start(f32[2,64]{1,0:T(2,128)S(1)} %pad_maximum_fusion.6), channel_id=1, source_target_pairs={{0,8},{8,0},{16,24},{24,16},{1,9},{9,1},{17,25},{25,17},{2,10},{10... | collective-permute-start | bytes 1544 | tf_op jit(solution)/shard_map/ppermute | solution.py:329
  156.6 1.2 collective-permute-start.37
  158.1 0.7 collective-permute-start.41
  158.8 1.6 collective-permute-start.42
  160.4 1.3 collective-permute-done.41
  161.9 1.8 %collective-permute-start.35 = (bf16[64,1536]{1,0:T(8,128)(2,1)S(1)}, bf16[64,1536]{1,0:T(8,128)(2,1)S(1)}, u32[]{:S(2)}, u32[]{:S(2)}) collective-permute-start(bf16[64,1536]{1,0:T(8,128)(2,1)S(1)} %slice.227), channel_id=1, source_target_pairs={{0,2},{1,3},{2,0},{3,1},{4,6},{5,7},{6,4},{7,5},{8,10},{9,11},{10,... | collective-permute-start | bytes 589832 | tf_op jit(solution)/shard_map/ppermute | solution.py:326
  163.7 0.9 fusion.21
  164.6 5.2 %wgrad_far.1 = f32[3072,1536]{1,0:T(8,128)} custom-call(s32[1]{0:T(128)} %bitcast.me_ref.refs_4_.refs_2_, bf16[256,1536]{1,0:T(8,128)(2,1)S(1)} %collective-permute-done.26.far_ref.p0, bf16[256,1536]{1,0:T(8,128)(2,1)S(1)} %collective-permute-done.27.far_ref.p1, bf16[256,1536]{1,0:T(8,128)(2,1)S(1)} %get-tuple-element.61.refs_0_.c0, ...), custom_call_target="tpu_custom_call", output_to_operand_aliasing={{}: (5, {})} | custom-call | tf_op jit(solution)/shard_map/wgrad_far/pallas_call | solution.py:241
  170.4 0.8 fusion.26
  (143 shorter events, 8.0 us)
Async XLA Ops:
  0.6 11.0 %collective-permute-start.1 = (bf16[64,1536]{1,0:T(8,128)(2,1)}, bf16[64,1536]{1,0:T(8,128)(2,1)S(1)}, u32[]{:S(2)}, u32[]{:S(2)}) collective-permute-start(bf16[64,1536]{1,0:T(8,128)(2,1)} %refs_0_.1), channel_id=1, source_target_pairs={{0,2},{1,3},{2,0},{3,1},{4,6},{5,7},{6,4},{7,5},{8,10},{9,11},{10,... | collective-permute-start | bytes 589832 | tf_op jit(solution)/shard_map/ppermute | solution.py:326
  3.7 7.9 %collective-permute-start.2 = (bf16[64,1536]{1,0:T(8,128)(2,1)}, bf16[64,1536]{1,0:T(8,128)(2,1)S(1)}, u32[]{:S(2)}, u32[]{:S(2)}) collective-permute-start(bf16[64,1536]{1,0:T(8,128)(2,1)} %refs_0_.1), channel_id=1, source_target_pairs={{0,1},{1,0},{2,3},{3,2},{4,5},{5,4},{6,7},{7,6},{8,9},{9,8},{10,11... | collective-permute-start | bytes 589832 | tf_op jit(solution)/shard_map/ppermute | solution.py:326
  3.7 16.0 %collective-permute-start.5 = (bf16[64,1536]{1,0:T(8,128)(2,1)}, bf16[64,1536]{1,0:T(8,128)(2,1)S(1)}, u32[]{:S(2)}, u32[]{:S(2)}) collective-permute-start(bf16[64,1536]{1,0:T(8,128)(2,1)} %refs_0_.1), channel_id=1, source_target_pairs={{0,4},{1,5},{2,6},{3,7},{4,0},{5,1},{6,2},{7,3},{8,12},{9,13},{10,... | collective-permute-start | bytes 589832 | tf_op jit(solution)/shard_map/ppermute | solution.py:326
  7.4 4.2 %collective-permute-start = (f32[2,64]{1,0:T(2,128)S(1)}, f32[2,64]{1,0:T(2,128)S(1)}, u32[]{:S(2)}, u32[]{:S(2)}) collective-permute-start(f32[2,64]{1,0:T(2,128)S(1)} %pad_maximum_fusion.5), channel_id=1, source_target_pairs={{0,8},{8,0},{16,24},{24,16},{1,9},{9,1},{17,25},{25,17},{2,10},{10... | collective-permute-start | bytes 1544 | tf_op jit(solution)/shard_map/ppermute | solution.py:329
  11.6 1.4 collective-permute-start.3
  14.0 30.3 %slice-start = ((s8[9437184]{0:T(1024)(128)(4,1)}), s8[4194304]{0:T(1024)(128)(4,1)S(1)}, s32[]{:S(2)}) async-start(s8[9437184]{0:T(1024)(128)(4,1)} %bitcast.20), calls=%async_computation | async-start | bytes 8388608
  17.8 26.4 %slice-start.1 = ((s8[9437184]{0:T(1024)(128)(4,1)}), s8[4194304]{0:T(1024)(128)(4,1)S(1)}, s32[]{:S(2)}) async-start(s8[9437184]{0:T(1024)(128)(4,1)} %bitcast.20), calls=%async_computation.1 | async-start | bytes 8388608
  17.8 3.6 %collective-permute-start.4 = (f32[2,64]{1,0:T(2,128)S(1)}, f32[2,64]{1,0:T(2,128)S(1)}, u32[]{:S(2)}, u32[]{:S(2)}) collective-permute-start(f32[2,64]{1,0:T(2,128)S(1)} %fusion.32), channel_id=1, source_target_pairs={{0,16},{8,24},{16,0},{24,8},{1,17},{9,25},{17,1},{25,9},{2,18},{10... | collective-permute-start | bytes 1544 | tf_op jit(solution)/shard_map/ppermute | solution.py:329
  19.7 6.7 %collective-permute-start.6 = (bf16[64,1536]{1,0:T(8,128)(2,1)S(1)}, bf16[64,1536]{1,0:T(8,128)(2,1)S(1)}, u32[]{:S(2)}, u32[]{:S(2)}) collective-permute-start(bf16[64,1536]{1,0:T(8,128)(2,1)S(1)} %collective-permute-done.5), channel_id=1, source_target_pairs={{0,2},{1,3},{2,0},{3,1},{4,6},{5,7},{6,4},{7,5},{8,10},{9,11},{10,... | collective-permute-start | bytes 589832 | tf_op jit(solution)/shard_map/ppermute | solution.py:326
  19.8 22.7 %collective-permute-start.8 = (bf16[256,1536]{1,0:T(8,128)(2,1)S(1)}, bf16[256,1536]{1,0:T(8,128)(2,1)S(1)}, u32[]{:S(2)}, u32[]{:S(2)}) collective-permute-start(bf16[256,1536]{1,0:T(8,128)(2,1)S(1)} %get-tuple-element.59), channel_id=1, source_target_pairs={{0,8},{1,17},{2,10},{3,19},{4,12},{5,21},{6,14},{7,23},{8,0},{9,25... | collective-permute-start | bytes 2359304 | tf_op jit(solution)/shard_map/ppermute | solution.py:320
  26.4 1.8 %collective-permute-start.7 = (bf16[128,1536]{1,0:T(8,128)(2,1)S(1)}, bf16[128,1536]{1,0:T(8,128)(2,1)S(1)}, u32[]{:S(2)}, u32[]{:S(2)}) collective-permute-start(bf16[128,1536]{1,0:T(8,128)(2,1)S(1)} %constant_dynamic-update-slice_fusion.refs_0_), channel_id=1, source_target_pairs={{0,1},{1,0},{2,3},{3,2},{4,5},{5,4},{6,7},{7,6},{8,9},{9,8},{10,11... | collective-permute-start | bytes 1179656 | tf_op jit(solution)/shard_map/ppermute | solution.py:326
  28.2 3.0 %copy-start.8 = (bf16[64,1536]{1,0:T(8,128)(2,1)S(1)}, bf16[64,1536]{1,0:T(8,128)(2,1)}, u32[]{:S(2)}) copy-start(bf16[64,1536]{1,0:T(8,128)(2,1)} %param.7) | copy-start | bytes 589828
  28.2 3.0 %copy-start.15 = (f32[1536]{0:T(1024)S(1)}, f32[1536]{0:T(1024)}, u32[]{:S(2)}) copy-start(f32[1536]{0:T(1024)} %param.8) | copy-start | bytes 18436
  29.6 14.5 %collective-permute-start.9 = (bf16[256,1536]{1,0:T(8,128)(2,1)S(1)}, bf16[256,1536]{1,0:T(8,128)(2,1)S(1)}, u32[]{:S(2)}, u32[]{:S(2)}) collective-permute-start(bf16[256,1536]{1,0:T(8,128)(2,1)S(1)} %get-tuple-element.68), channel_id=1, source_target_pairs={{0,8},{1,17},{2,10},{3,19},{4,12},{5,21},{6,14},{7,23},{8,0},{9,25... | collective-permute-start | bytes 2359304 | tf_op jit(solution)/shard_map/ppermute | solution.py:320
  31.3 10.8 %collective-permute-start.15 = (bf16[64,1536]{1,0:T(8,128)(2,1)S(1)}, bf16[64,1536]{1,0:T(8,128)(2,1)S(1)}, u32[]{:S(2)}, u32[]{:S(2)}) collective-permute-start(bf16[64,1536]{1,0:T(8,128)(2,1)S(1)} %fusion.17.refs_0_), channel_id=1, source_target_pairs={{0,4},{1,5},{2,6},{3,7},{4,0},{5,1},{6,2},{7,3},{8,12},{9,13},{10,... | collective-permute-start | bytes 589832 | tf_op jit(solution)/shard_map/ppermute | solution.py:326
  32.9 9.5 %collective-permute-start.10 = (bf16[64,1536]{1,0:T(8,128)(2,1)S(1)}, bf16[64,1536]{1,0:T(8,128)(2,1)S(1)}, u32[]{:S(2)}, u32[]{:S(2)}) collective-permute-start(bf16[64,1536]{1,0:T(8,128)(2,1)S(1)} %fusion.17.refs_0_), channel_id=1, source_target_pairs={{0,2},{1,3},{2,0},{3,1},{4,6},{5,7},{6,4},{7,5},{8,10},{9,11},{10,... | collective-permute-start | bytes 589832 | tf_op jit(solution)/shard_map/ppermute | solution.py:326
  34.7 9.6 %collective-permute-start.11 = (bf16[64,1536]{1,0:T(8,128)(2,1)S(1)}, bf16[64,1536]{1,0:T(8,128)(2,1)S(1)}, u32[]{:S(2)}, u32[]{:S(2)}) collective-permute-start(bf16[64,1536]{1,0:T(8,128)(2,1)S(1)} %fusion.17.refs_0_), channel_id=1, source_target_pairs={{0,1},{1,0},{2,3},{3,2},{4,5},{5,4},{6,7},{7,6},{8,9},{9,8},{10,11... | collective-permute-start | bytes 589832 | tf_op jit(solution)/shard_map/ppermute | solution.py:326
  34.7 9.6 %slice-start.2 = ((s8[9437184]{0:T(1024)(128)(4,1)}), s8[1048576]{0:T(1024)(128)(4,1)S(1)}, s32[]{:S(2)}) async-start(s8[9437184]{0:T(1024)(128)(4,1)} %bitcast.20), calls=%async_computation.2 | async-start | bytes 2097152
  39.3 4.9 %copy-start = (f32[256,1536]{1,0:T(8,128)}, f32[256,1536]{1,0:T(8,128)S(1)}, u32[]{:S(2)}) copy-start(f32[256,1536]{1,0:T(8,128)S(1)} %get-tuple-element.67) | copy-start | bytes 4718596
  39.3 4.9 %copy-start.2 = (f32[256,1536]{1,0:T(8,128)}, f32[256,1536]{1,0:T(8,128)S(1)}, u32[]{:S(2)}) copy-start(f32[256,1536]{1,0:T(8,128)S(1)} %get-tuple-element.66) | copy-start | bytes 4718596
  42.2 6.6 %collective-permute-start.16 = (bf16[64,1536]{1,0:T(8,128)(2,1)S(1)}, bf16[64,1536]{1,0:T(8,128)(2,1)S(1)}, u32[]{:S(2)}, u32[]{:S(2)}) collective-permute-start(bf16[64,1536]{1,0:T(8,128)(2,1)S(1)} %collective-permute-done.15), channel_id=1, source_target_pairs={{0,2},{1,3},{2,0},{3,1},{4,6},{5,7},{6,4},{7,5},{8,10},{9,11},{10,... | collective-permute-start | bytes 589832 | tf_op jit(solution)/shard_map/ppermute | solution.py:326
  42.4 1.8 %collective-permute-start.12 = (bf16[64,1536]{1,0:T(8,128)(2,1)S(1)}, bf16[64,1536]{1,0:T(8,128)(2,1)S(1)}, u32[]{:S(2)}, u32[]{:S(2)}) collective-permute-start(bf16[64,1536]{1,0:T(8,128)(2,1)S(1)} %collective-permute-done.10.refs_1_), channel_id=1, source_target_pairs={{0,1},{1,0},{2,3},{3,2},{4,5},{5,4},{6,7},{7,6},{8,9},{9,8},{10,11... | collective-permute-start | bytes 589832 | tf_op jit(solution)/shard_map/ppermute | solution.py:326
  42.5 4.5 %copy-start.9 = (bf16[256,1536]{1,0:T(8,128)(2,1)}, bf16[256,1536]{1,0:T(8,128)(2,1)S(1)}, u32[]{:S(2)}) copy-start(bf16[256,1536]{1,0:T(8,128)(2,1)S(1)} %collective-permute-done.8) | copy-start | bytes 2359300
  42.6 9.7 %collective-permute-start.17 = (bf16[256,768]{1,0:T(8,128)(2,1)S(1)}, bf16[256,768]{1,0:T(8,128)(2,1)S(1)}, u32[]{:S(2)}, u32[]{:S(2)}) collective-permute-start(bf16[256,768]{1,0:T(8,128)(2,1)S(1)} %add_convert_fusion.3), channel_id=1, source_target_pairs={{0,16},{1,9},{2,18},{3,11},{4,20},{5,13},{6,22},{7,15},{8,24},{9,1... | collective-permute-start | bytes 1179656 | tf_op jit(solution)/shard_map/ppermute | solution.py:323
  47.0 18.1 %copy-start.4 = (f32[256,1536]{1,0:T(8,128)}, f32[256,1536]{1,0:T(8,128)S(1)}, u32[]{:S(2)}) copy-start(f32[256,1536]{1,0:T(8,128)S(1)} %get-tuple-element.71) | copy-start | bytes 4718596
  48.7 3.5 %collective-permute-start.18 = (bf16[128,1536]{1,0:T(8,128)(2,1)S(1)}, bf16[128,1536]{1,0:T(8,128)(2,1)S(1)}, u32[]{:S(2)}, u32[]{:S(2)}) collective-permute-start(bf16[128,1536]{1,0:T(8,128)(2,1)S(1)} %constant_dynamic-update-slice_fusion.2.refs_0_), channel_id=1, source_target_pairs={{0,1},{1,0},{2,3},{3,2},{4,5},{5,4},{6,7},{7,6},{8,9},{9,8},{10,11... | collective-permute-start | bytes 1179656 | tf_op jit(solution)/shard_map/ppermute | solution.py:326
  48.8 16.3 %collective-permute-start.13 = (bf16[256,1536]{1,0:T(8,128)(2,1)S(1)}, bf16[256,1536]{1,0:T(8,128)(2,1)S(1)}, u32[]{:S(2)}, u32[]{:S(2)}) collective-permute-start(bf16[256,1536]{1,0:T(8,128)(2,1)S(1)} %get-tuple-element.72), channel_id=1, source_target_pairs={{0,8},{1,17},{2,10},{3,19},{4,12},{5,21},{6,14},{7,23},{8,0},{9,25... | collective-permute-start | bytes 2359304 | tf_op jit(solution)/shard_map/ppermute | solution.py:320
  50.6 12.1 %collective-permute-start.14 = (bf16[256,768]{1,0:T(8,128)(2,1)S(1)}, bf16[256,768]{1,0:T(8,128)(2,1)S(1)}, u32[]{:S(2)}, u32[]{:S(2)}) collective-permute-start(bf16[256,768]{1,0:T(8,128)(2,1)S(1)} %add_convert_fusion.2), channel_id=1, source_target_pairs={{0,16},{1,9},{2,18},{3,11},{4,20},{5,13},{6,22},{7,15},{8,24},{9,1... | collective-permute-start | bytes 1179656 | tf_op jit(solution)/shard_map/ppermute | solution.py:323
  56.1 21.7 %collective-permute-start.20 = (bf16[256,1536]{1,0:T(8,128)(2,1)}, bf16[256,1536]{1,0:T(8,128)(2,1)}, u32[]{:S(2)}, u32[]{:S(2)}) collective-permute-start(bf16[256,1536]{1,0:T(8,128)(2,1)} %get-tuple-element.76), channel_id=1, source_target_pairs={{0,8},{1,17},{2,10},{3,19},{4,12},{5,21},{6,14},{7,23},{8,0},{9,25... | collective-permute-start | bytes 2359304 | tf_op jit(solution)/shard_map/ppermute | solution.py:320
  62.7 3.3 %copy-start.14 = (bf16[256,768]{1,0:T(8,128)(2,1)}, bf16[256,768]{1,0:T(8,128)(2,1)S(1)}, u32[]{:S(2)}) copy-start(bf16[256,768]{1,0:T(8,128)(2,1)S(1)} %collective-permute-done.14) | copy-start | bytes 1179652
  66.1 14.4 %collective-permute-start.19 = (bf16[256,768]{1,0:T(8,128)(2,1)}, bf16[256,768]{1,0:T(8,128)(2,1)}, u32[]{:S(2)}, u32[]{:S(2)}) collective-permute-start(bf16[256,768]{1,0:T(8,128)(2,1)} %add_convert_fusion.1), channel_id=1, source_target_pairs={{0,16},{1,9},{2,18},{3,11},{4,20},{5,13},{6,22},{7,15},{8,24},{9,1... | collective-permute-start | bytes 1179656 | tf_op jit(solution)/shard_map/ppermute | solution.py:323
  67.4 13.1 %copy-start.3 = (f32[256,1536]{1,0:T(8,128)S(1)}, f32[256,1536]{1,0:T(8,128)}, u32[]{:S(2)}) copy-start(f32[256,1536]{1,0:T(8,128)} %copy-done.2) | copy-start | bytes 4718596
  79.1 10.6 %copy-start.1 = (f32[256,1536]{1,0:T(8,128)S(1)}, f32[256,1536]{1,0:T(8,128)}, u32[]{:S(2)}) copy-start(f32[256,1536]{1,0:T(8,128)} %copy-done) | copy-start | bytes 4718596
  79.1 10.6 %copy-start.6 = (f32[256,1536]{1,0:T(8,128)S(1)}, f32[256,1536]{1,0:T(8,128)}, u32[]{:S(2)}) copy-start(f32[256,1536]{1,0:T(8,128)} %copy-done.5) | copy-start | bytes 4718596
  79.1 10.6 %copy-start.11 = (bf16[256,1536]{1,0:T(8,128)(2,1)S(1)}, bf16[256,1536]{1,0:T(8,128)(2,1)}, u32[]{:S(2)}) copy-start(bf16[256,1536]{1,0:T(8,128)(2,1)} %copy-done.10) | copy-start | bytes 2359300
  79.2 10.6 %collective-permute-start.22 = (bf16[256,768]{1,0:T(8,128)(2,1)S(1)}, bf16[256,768]{1,0:T(8,128)(2,1)S(1)}, u32[]{:S(2)}, u32[]{:S(2)}) collective-permute-start(bf16[256,768]{1,0:T(8,128)(2,1)S(1)} %add_convert_fusion), channel_id=1, source_target_pairs={{0,16},{1,9},{2,18},{3,11},{4,20},{5,13},{6,22},{7,15},{8,24},{9,1... | collective-permute-start | bytes 1179656 | tf_op jit(solution)/shard_map/ppermute | solution.py:323
  82.7 12.0 %collective-permute-start.25 = (bf16[256,768]{1,0:T(8,128)(2,1)S(1)}, bf16[256,768]{1,0:T(8,128)(2,1)S(1)}, u32[]{:S(2)}, u32[]{:S(2)}) collective-permute-start(bf16[256,768]{1,0:T(8,128)(2,1)S(1)} %get-tuple-element.121), channel_id=1, source_target_pairs={{0,8},{1,17},{2,10},{3,19},{4,12},{5,21},{6,14},{7,23},{8,0},{9,25... | collective-permute-start | bytes 1179656 | tf_op jit(solution)/shard_map/ppermute | solution.py:320
  84.5 10.3 %collective-permute-start.21 = (bf16[256,768]{1,0:T(8,128)(2,1)S(1)}, bf16[256,768]{1,0:T(8,128)(2,1)S(1)}, u32[]{:S(2)}, u32[]{:S(2)}) collective-permute-start(bf16[256,768]{1,0:T(8,128)(2,1)S(1)} %get-tuple-element.122), channel_id=1, source_target_pairs={{0,8},{1,17},{2,10},{3,19},{4,12},{5,21},{6,14},{7,23},{8,0},{9,25... | collective-permute-start | bytes 1179656 | tf_op jit(solution)/shard_map/ppermute | solution.py:320
  91.5 8.7 %collective-permute-start.24 = (bf16[256,768]{1,0:T(8,128)(2,1)S(1)}, bf16[256,768]{1,0:T(8,128)(2,1)S(1)}, u32[]{:S(2)}, u32[]{:S(2)}) collective-permute-start(bf16[256,768]{1,0:T(8,128)(2,1)S(1)} %get-tuple-element.119), channel_id=1, source_target_pairs={{0,8},{1,17},{2,10},{3,19},{4,12},{5,21},{6,14},{7,23},{8,0},{9,25... | collective-permute-start | bytes 1179656 | tf_op jit(solution)/shard_map/ppermute | solution.py:320
  94.4 11.8 %collective-permute-start.23 = (bf16[256,768]{1,0:T(8,128)(2,1)S(1)}, bf16[256,768]{1,0:T(8,128)(2,1)S(1)}, u32[]{:S(2)}, u32[]{:S(2)}) collective-permute-start(bf16[256,768]{1,0:T(8,128)(2,1)S(1)} %get-tuple-element.120), channel_id=1, source_target_pairs={{0,8},{1,17},{2,10},{3,19},{4,12},{5,21},{6,14},{7,23},{8,0},{9,25... | collective-permute-start | bytes 1179656 | tf_op jit(solution)/shard_map/ppermute | solution.py:320
  100.2 13.4 %collective-permute-start.29 = (bf16[256,1536]{1,0:T(8,128)(2,1)S(1)}, bf16[256,1536]{1,0:T(8,128)(2,1)S(1)}, u32[]{:S(2)}, u32[]{:S(2)}) collective-permute-start(bf16[256,1536]{1,0:T(8,128)(2,1)S(1)} %pad_maximum_fusion.2.near_ref.near1), channel_id=1, source_target_pairs={{0,16},{1,9},{2,18},{3,11},{4,20},{5,13},{6,22},{7,15},{8,24},{9,1... | collective-permute-start | bytes 2359304 | tf_op jit(solution)/shard_map/ppermute | solution.py:323
  106.2 14.5 %collective-permute-start.28 = (bf16[256,1536]{1,0:T(8,128)(2,1)S(1)}, bf16[256,1536]{1,0:T(8,128)(2,1)S(1)}, u32[]{:S(2)}, u32[]{:S(2)}) collective-permute-start(bf16[256,1536]{1,0:T(8,128)(2,1)S(1)} %pad_maximum_fusion.1.near_ref.near0), channel_id=1, source_target_pairs={{0,16},{1,9},{2,18},{3,11},{4,20},{5,13},{6,22},{7,15},{8,24},{9,1... | collective-permute-start | bytes 2359304 | tf_op jit(solution)/shard_map/ppermute | solution.py:323
  106.2 7.4 %slice-start.3 = ((s8[9437184]{0:T(1024)(128)(4,1)}), s8[4194304]{0:T(1024)(128)(4,1)S(1)}, s32[]{:S(2)}) async-start(s8[9437184]{0:T(1024)(128)(4,1)} %bitcast.22), calls=%async_computation.3 | async-start | bytes 8388608
  106.2 7.4 %slice-start.4 = ((s8[9437184]{0:T(1024)(128)(4,1)}), s8[4194304]{0:T(1024)(128)(4,1)S(1)}, s32[]{:S(2)}) async-start(s8[9437184]{0:T(1024)(128)(4,1)} %bitcast.22), calls=%async_computation.4 | async-start | bytes 8388608
  106.3 7.4 %slice-start.5 = ((s8[9437184]{0:T(1024)(128)(4,1)}), s8[1048576]{0:T(1024)(128)(4,1)S(1)}, s32[]{:S(2)}) async-start(s8[9437184]{0:T(1024)(128)(4,1)} %bitcast.22), calls=%async_computation.5 | async-start | bytes 2097152
  106.3 23.9 %collective-permute-start.27 = (bf16[256,1536]{1,0:T(8,128)(2,1)S(1)}, bf16[256,1536]{1,0:T(8,128)(2,1)S(1)}, u32[]{:S(2)}, u32[]{:S(2)}) collective-permute-start(bf16[256,1536]{1,0:T(8,128)(2,1)S(1)} %pad_maximum_fusion.3.p1.near_ref), channel_id=1, source_target_pairs={{0,16},{1,9},{2,18},{3,11},{4,20},{5,13},{6,22},{7,15},{8,24},{9,1... | collective-permute-start | bytes 2359304 | tf_op jit(solution)/shard_map/ppermute | solution.py:323
  113.6 16.6 %slice-start.6 = ((s8[9437184]{0:T(1024)(128)(4,1)}), s8[4194304]{0:T(1024)(128)(4,1)S(1)}, s32[]{:S(2)}) async-start(s8[9437184]{0:T(1024)(128)(4,1)} %bitcast.24), calls=%async_computation.6 | async-start | bytes 8388608
  113.6 16.6 %slice-start.7 = ((s8[9437184]{0:T(1024)(128)(4,1)}), s8[4194304]{0:T(1024)(128)(4,1)S(1)}, s32[]{:S(2)}) async-start(s8[9437184]{0:T(1024)(128)(4,1)} %bitcast.24), calls=%async_computation.7 | async-start | bytes 8388608
  116.3 16.6 %collective-permute-start.32 = (bf16[128,1536]{1,0:T(8,128)(2,1)S(1)}, bf16[128,1536]{1,0:T(8,128)(2,1)S(1)}, u32[]{:S(2)}, u32[]{:S(2)}) collective-permute-start(bf16[128,1536]{1,0:T(8,128)(2,1)S(1)} %get-tuple-element.88), channel_id=1, source_target_pairs={{0,1},{1,0},{2,3},{3,2},{4,5},{5,4},{6,7},{7,6},{8,9},{9,8},{10,11... | collective-permute-start | bytes 1179656 | tf_op jit(solution)/shard_map/ppermute | solution.py:326
  116.4 32.1 %collective-permute-start.26 = (bf16[256,1536]{1,0:T(8,128)(2,1)S(1)}, bf16[256,1536]{1,0:T(8,128)(2,1)S(1)}, u32[]{:S(2)}, u32[]{:S(2)}) collective-permute-start(bf16[256,1536]{1,0:T(8,128)(2,1)S(1)} %pad_maximum_fusion.p0.near_ref), channel_id=1, source_target_pairs={{0,16},{1,9},{2,18},{3,11},{4,20},{5,13},{6,22},{7,15},{8,24},{9,1... | collective-permute-start | bytes 2359304 | tf_op jit(solution)/shard_map/ppermute | solution.py:323
  120.7 9.5 %slice-start.8 = ((s8[9437184]{0:T(1024)(128)(4,1)}), s8[1048576]{0:T(1024)(128)(4,1)S(1)}, s32[]{:S(2)}) async-start(s8[9437184]{0:T(1024)(128)(4,1)} %bitcast.24), calls=%async_computation.8 | async-start | bytes 2097152
  123.4 12.0 %collective-permute-start.30 = (bf16[144,1536]{1,0:T(8,128)(2,1)S(1)}, bf16[144,1536]{1,0:T(8,128)(2,1)S(1)}, u32[]{:S(2)}, u32[]{:S(2)}) collective-permute-start(bf16[144,1536]{1,0:T(8,128)(2,1)S(1)} %get-tuple-element.91), channel_id=1, source_target_pairs={{0,1},{1,0},{2,3},{3,2},{4,5},{5,4},{6,7},{7,6},{8,9},{9,8},{10,11... | collective-permute-start | bytes 1327112 | tf_op jit(solution)/shard_map/ppermute | solution.py:326
  132.9 1.8 %collective-permute-start.31 = (bf16[128,1536]{1,0:T(8,128)(2,1)S(1)}, bf16[128,1536]{1,0:T(8,128)(2,1)S(1)}, u32[]{:S(2)}, u32[]{:S(2)}) collective-permute-start(bf16[128,1536]{1,0:T(8,128)(2,1)S(1)} %get-tuple-element.95), channel_id=1, source_target_pairs={{0,1},{1,0},{2,3},{3,2},{4,5},{5,4},{6,7},{7,6},{8,9},{9,8},{10,11... | collective-permute-start | bytes 1179656 | tf_op jit(solution)/shard_map/ppermute | solution.py:326
  133.1 7.8 %collective-permute-start.33 = (bf16[64,1536]{1,0:T(8,128)(2,1)S(1)}, bf16[64,1536]{1,0:T(8,128)(2,1)S(1)}, u32[]{:S(2)}, u32[]{:S(2)}) collective-permute-start(bf16[64,1536]{1,0:T(8,128)(2,1)S(1)} %slice.228), channel_id=1, source_target_pairs={{0,2},{1,3},{2,0},{3,1},{4,6},{5,7},{6,4},{7,5},{8,10},{9,11},{10,... | collective-permute-start | bytes 589832 | tf_op jit(solution)/shard_map/ppermute | solution.py:326
  134.8 16.5 %collective-permute-start.36 = (bf16[64,1536]{1,0:T(8,128)(2,1)S(1)}, bf16[64,1536]{1,0:T(8,128)(2,1)S(1)}, u32[]{:S(2)}, u32[]{:S(2)}) collective-permute-start(bf16[64,1536]{1,0:T(8,128)(2,1)S(1)} %slice.226), channel_id=1, source_target_pairs={{0,2},{1,3},{2,0},{3,1},{4,6},{5,7},{6,4},{7,5},{8,10},{9,11},{10,... | collective-permute-start | bytes 589832 | tf_op jit(solution)/shard_map/ppermute | solution.py:326
  135.9 18.2 %collective-permute-start.38 = (bf16[80,1536]{1,0:T(8,128)(2,1)S(1)}, bf16[80,1536]{1,0:T(8,128)(2,1)S(1)}, u32[]{:S(2)}, u32[]{:S(2)}) collective-permute-start(bf16[80,1536]{1,0:T(8,128)(2,1)S(1)} %pad_maximum_fusion.4), channel_id=1, source_target_pairs={{0,2},{1,3},{2,0},{3,1},{4,6},{5,7},{6,4},{7,5},{8,10},{9,11},{10,... | collective-permute-start | bytes 737288 | tf_op jit(solution)/shard_map/ppermute | solution.py:326
  140.9 13.3 %collective-permute-start.39 = (bf16[64,1536]{1,0:T(8,128)(2,1)S(1)}, bf16[64,1536]{1,0:T(8,128)(2,1)S(1)}, u32[]{:S(2)}, u32[]{:S(2)}) collective-permute-start(bf16[64,1536]{1,0:T(8,128)(2,1)S(1)} %slice_add_fusion.4), channel_id=1, source_target_pairs={{0,4},{1,5},{2,6},{3,7},{4,0},{5,1},{6,2},{7,3},{8,12},{9,13},{10,... | collective-permute-start | bytes 589832 | tf_op jit(solution)/shard_map/ppermute | solution.py:326
  151.2 10.6 %collective-permute-start.34 = (bf16[128,1536]{1,0:T(8,128)(2,1)S(1)}, bf16[128,1536]{1,0:T(8,128)(2,1)S(1)}, u32[]{:S(2)}, u32[]{:S(2)}) collective-permute-start(bf16[128,1536]{1,0:T(8,128)(2,1)S(1)} %get-tuple-element.103), channel_id=1, source_target_pairs={{0,1},{1,0},{2,3},{3,2},{4,5},{5,4},{6,7},{7,6},{8,9},{9,8},{10,11... | collective-permute-start | bytes 1179656 | tf_op jit(solution)/shard_map/ppermute | solution.py:326
  154.4 3.7 %collective-permute-start.40 = (f32[2,64]{1,0:T(2,128)S(1)}, f32[2,64]{1,0:T(2,128)S(1)}, u32[]{:S(2)}, u32[]{:S(2)}) collective-permute-start(f32[2,64]{1,0:T(2,128)S(1)} %pad_maximum_fusion.6), channel_id=1, source_target_pairs={{0,8},{8,0},{16,24},{24,16},{1,9},{9,1},{17,25},{25,17},{2,10},{10... | collective-permute-start | bytes 1544 | tf_op jit(solution)/shard_map/ppermute | solution.py:329
  156.6 13.9 %collective-permute-start.37 = (bf16[64,1536]{1,0:T(8,128)(2,1)S(1)}, bf16[64,1536]{1,0:T(8,128)(2,1)S(1)}, u32[]{:S(2)}, u32[]{:S(2)}) collective-permute-start(bf16[64,1536]{1,0:T(8,128)(2,1)S(1)} %slice_add_fusion.2), channel_id=1, source_target_pairs={{0,4},{1,5},{2,6},{3,7},{4,0},{5,1},{6,2},{7,3},{8,12},{9,13},{10,... | collective-permute-start | bytes 589832 | tf_op jit(solution)/shard_map/ppermute | solution.py:326
  158.1 3.6 %collective-permute-start.41 = (f32[2,64]{1,0:T(2,128)S(1)}, f32[2,64]{1,0:T(2,128)S(1)}, u32[]{:S(2)}, u32[]{:S(2)}) collective-permute-start(f32[2,64]{1,0:T(2,128)S(1)} %fusion.31), channel_id=1, source_target_pairs={{0,16},{8,24},{16,0},{24,8},{1,17},{9,25},{17,1},{25,9},{2,18},{10... | collective-permute-start | bytes 1544 | tf_op jit(solution)/shard_map/ppermute | solution.py:329
  158.8 11.0 %collective-permute-start.42 = (f32[1,1536]{1,0:T(1,128)S(1)}, f32[1,1536]{1,0:T(1,128)S(1)}, u32[]{:S(2)}, u32[]{:S(2)}) collective-permute-start(f32[1,1536]{1,0:T(1,128)S(1)} %fusion.27), channel_id=1, source_target_pairs={{0,4},{1,5},{2,6},{3,7},{4,0},{5,1},{6,2},{7,3},{8,12},{9,13},{10,... | collective-permute-start | bytes 18440 | tf_op jit(solution)/shard_map/ppermute | solution.py:326
  161.9 8.6 %collective-permute-start.35 = (bf16[64,1536]{1,0:T(8,128)(2,1)S(1)}, bf16[64,1536]{1,0:T(8,128)(2,1)S(1)}, u32[]{:S(2)}, u32[]{:S(2)}) collective-permute-start(bf16[64,1536]{1,0:T(8,128)(2,1)S(1)} %slice.227), channel_id=1, source_target_pairs={{0,2},{1,3},{2,0},{3,1},{4,6},{5,7},{6,4},{7,5},{8,10},{9,11},{10,... | collective-permute-start | bytes 589832 | tf_op jit(solution)/shard_map/ppermute | solution.py:326
  164.6 5.9 %copy-start.16 = (f32[1536]{0:T(1024)S(1)}, f32[1536]{0:T(1024)}, u32[]{:S(2)}) copy-start(f32[1536]{0:T(1024)} %param.12) | copy-start | bytes 18436
  (5 other events, 8.7 us)
